TPU v7x, 512 devices: a whole 4x8x8 slice. The times are simulated.
512 devices in a mesh: rows: 128 (over y, z, core), rep: 4 (over x).
Axes of the slice: x: 4, y: 8, z: 8, core: 2. Of those that a mesh axis runs over, the one named last changes fastest.
Arguments:
- tables: bfloat16 [262144, 128], P('rows'), may hold values from -0.5 to 0.5
- indices: int32 [8192, 8, 8], P(('rows', 'rep')), may hold values from 0 to 32767
- bag_lengths: int32 [8192, 8], P(('rows', 'rep')), may hold values from 1 to 8
- dense: bfloat16 [8192, 13], P(('rows', 'rep')), may hold values from -6 to 6
- bottom_first: bfloat16 [13, 512], replicated, may hold values from -1.75 to 1.75
- bottom_second: bfloat16 [512, 256], replicated, may hold values from -0.375 to 0.375
- bottom_third: bfloat16 [256, 128], replicated, may hold values from -0.5 to 0.5
- top_first: bfloat16 [164, 1024], P(None, 'rep'), may hold values from -0.5 to 0.5
- top_second: bfloat16 [1024, 1024], P(None, 'rep'), may hold values from -0.25 to 0.25
- top_third: bfloat16 [1024, 512], P(None, 'rep'), may hold values from -0.25 to 0.25
- top_fourth: bfloat16 [512, 256], P(None, 'rep'), may hold values from -0.375 to 0.375
- top_last: bfloat16 [256], replicated, may hold values from -0.5 to 0.5
Outputs:
- logit: float32 [8192], P(('rows', 'rep'))
Inputs may be any that keep to these rules, and one draw needn't show every extreme that they name: `indices`: each entry is a row number within its own table; entries at positions of a bag at or past its length are ignored.
All inputs are finite; a program needn't handle non-finite values.
Results may differ from a plain program's by a relative error of at most 0.0076.
Values may be sent and summed in bfloat16 or wider, within the bound.
No kernel may reach another device: no remote copies, remote signals or barrier semaphores. Data moves between devices by JAX's collectives and lax.ppermute only.
A program may use at most 64 MiB of HBM per device.

v0:
```python
import jax
import jax.numpy as jnp
import numpy as np
from jax import lax
from jax.sharding import Mesh
from jax.sharding import PartitionSpec as P

TAB = 8
HOT = 8
ROWS = ("rows_0", "rows_1", "rows_2")
ROWS_REP = ("rows_0", "rows_1", "rows_2", "rep")


def split_up(shard, dim, peers):
    before, after = (shard.shape[:dim], shard.shape[dim + 1 :])
    return jnp.moveaxis(shard.reshape(*before, peers, -1, *after), dim, 0)


def laid_out(blocks, dim):
    dims = list(blocks.shape[1:])
    dims[dim] *= blocks.shape[0]
    return jnp.moveaxis(blocks, 0, dim).reshape(dims)


def turned_blocks(blocks, axes, turns):
    inside = blocks.shape[1:]
    result = blocks.reshape(*(lax.axis_size(a) for a in axes), *inside)
    for k in turns:
        result = lax.all_to_all(result, axes[k], k, k, tiled=True)
    return result.reshape(-1, *inside)


def two_step_exchange(shard, groups, turns, split_dim, concat_dim):
    peers = lax.axis_size(groups[0]) * lax.axis_size(groups[1])
    blocks = split_up(shard, split_dim, peers)
    return laid_out(turned_blocks(blocks, groups, turns), concat_dim)


def sent_together(arrays, axis, dim, along):
    both = jnp.concatenate(arrays, axis=along)
    result, at, finished = (lax.all_gather(both, axis, axis=dim, tiled=True), 0, [])
    for a in arrays:
        finished.append(lax.slice_in_dim(result, at, at + a.shape[along], axis=along))
        at += a.shape[along]
    return tuple(finished)


def interact(bottom_out, pooled):
    features = jnp.concatenate([bottom_out[None], pooled], axis=0)
    gram_matrix = jnp.einsum("ibe,jbe->bij", features, features, precision=lax.Precision.HIGHEST)
    left_ids, right_ids = np.triu_indices(TAB + 1, 1)
    pair_dots = gram_matrix[:, left_ids, right_ids]
    return jnp.concatenate([bottom_out, pair_dots], axis=1).astype(jnp.bfloat16)


def bottom_net(dense, bottom_first, bottom_second, bottom_third):
    lower_act = jax.nn.relu(
        jnp.dot(dense, bottom_first, preferred_element_type=jnp.float32)
    ).astype(jnp.bfloat16)
    middle = jax.nn.relu(
        jnp.dot(lower_act, bottom_second, preferred_element_type=jnp.float32)
    ).astype(jnp.bfloat16)
    return jax.nn.relu(jnp.dot(middle, bottom_third, preferred_element_type=jnp.float32))


def body(
    tables,
    indices,
    bag_lengths,
    dense,
    bottom_first,
    bottom_second,
    bottom_third,
    top_first,
    top_second,
    top_third,
    top_fourth,
    top_last,
):
    batch_rows = indices.shape[0]
    row_count = tables.shape[0]
    emb_width = tables.shape[1]
    device_count = lax.axis_size(ROWS)
    per_table = device_count // TAB
    position = lax.axis_index(ROWS)
    row_offset = position % per_table * row_count
    slot_ids = jnp.arange(HOT, dtype=jnp.int32)
    masked = jnp.where(slot_ids[None, None, :] < bag_lengths[:, :, None], indices, -1)
    outgoing = jnp.repeat(jnp.transpose(masked, (1, 0, 2)), per_table, axis=0)
    incoming = lax.all_to_all(outgoing, ROWS, split_axis=0, concat_axis=0, tiled=True)
    wanted = incoming.reshape(device_count * batch_rows, HOT)
    local_ids = wanted - row_offset
    block_rows = min(512, row_count)
    block_count = row_count // block_rows

    def add_block(block_num, partial_value):
        first_row = block_num * block_rows
        cell_ids = first_row + jnp.arange(block_rows, dtype=jnp.int32)
        counts = jnp.zeros((local_ids.shape[0], block_rows), jnp.float32)
        for slot_num in range(HOT):
            counts = counts + (local_ids[:, slot_num : slot_num + 1] == cell_ids[None, :]).astype(
                jnp.float32
            )
        block_table = lax.dynamic_slice_in_dim(tables, first_row, block_rows, 0)
        return partial_value + jnp.dot(
            counts.astype(jnp.bfloat16), block_table, preferred_element_type=jnp.float32
        )

    partial_value = lax.fori_loop(
        0, block_count, add_block, jnp.zeros((local_ids.shape[0], emb_width), jnp.float32)
    )
    bag_parts = two_step_exchange(
        partial_value.reshape(device_count, batch_rows, emb_width),
        (("rows_0", "rows_1"), "rows_2"),
        (1, 0),
        0,
        0,
    )
    pooled = jnp.sum(bag_parts.reshape(TAB, per_table, batch_rows, emb_width), axis=1)
    bottom_out = bottom_net(dense, bottom_first, bottom_second, bottom_third)
    activation = interact(bottom_out, pooled)
    whole = (
        *sent_together((top_first, top_second), "rep", 1, 0),
        lax.all_gather(top_third, "rep", axis=1, tiled=True),
        lax.all_gather(top_fourth, "rep", axis=1, tiled=True),
    )
    for weight_mat in whole:
        activation = jax.nn.relu(
            jnp.dot(activation, weight_mat, preferred_element_type=jnp.float32)
        ).astype(jnp.bfloat16)
    return jnp.dot(activation, top_last, preferred_element_type=jnp.float32)


def solution(mesh):
    torus = Mesh(
        mesh.devices.reshape(8, 8, 2, mesh.shape["rep"]), ("rows_0", "rows_1", "rows_2", "rep")
    )
    in_specs = (
        P(ROWS, None),
        P(ROWS_REP, None, None),
        P(ROWS_REP, None),
        P(ROWS_REP, None),
        P(),
        P(),
        P(),
        P(None, "rep"),
        P(None, "rep"),
        P(None, "rep"),
        P(None, "rep"),
        P(),
    )
    out_specs = P(ROWS_REP)
    return jax.shard_map(body, mesh=torus, in_specs=in_specs, out_specs=out_specs, check_vma=False)
```

profile of v0, /device:TPU:1, one launch (start us, length us, event | category | flops | bytes accessed | tf_op | source)
XLA Modules:
  0.0 116.0 jit_solution(14366075911128937941)
XLA Ops:
  6.5 0.8 select_bitcast_fusion
  7.4 0.9 reshape.21
  8.2 18.4 %all-to-all-start = ((s32[128,1,128]{2,1,0:T(1,128)}), s32[128,1,128]{2,1,0:T(1,128)S(1)}, u32[]{:S(2)}, u32[]{:S(2)}) async-start(s32[128,1,128]{2,1,0:T(1,128)} %reshape.21), calls=%async_computation | async-start | bytes 131072 | tf_op jit(solution)/shard_map/all_to_all | solution.py:90
  26.7 2.0 %pad_maximum_fusion = bf16[1188,256]{1,0:T(8,128)(2,1)} fusion(bf16[1024,256]{1,0:T(8,128)(2,1)} %param.26, bf16[164,256]{1,0:T(8,128)(2,1)} %param.25), kind=kLoop, calls=%fused_computation.31 | loop fusion | flops 1216512 | bytes 1216512 | tf_op jit(solution)/shard_map/concatenate | solution.py:40
  28.8 9.4 %all-to-all-done = s32[128,1,128]{2,1,0:T(1,128)S(1)} async-done(((s32[128,1,128]{2,1,0:T(1,128)}), s32[128,1,128]{2,1,0:T(1,128)S(1)}, u32[]{:S(2)}, u32[]{:S(2)}) %all-to-all-start) | async-done | bytes 65568 | tf_op jit(solution)/shard_map/all_to_all | solution.py:90
  38.2 0.6 broadcast.35
  38.8 0.8 reduce.2
  40.5 17.9 %while.14 = (s32[]{:T(128)}, f32[2048,128]{1,0:T(8,128)S(1)}, s32[2048,8]{0,1:T(8,128)S(1)}, bf16[2048,128]{1,0:T(8,128)(2,1)}, s32[]{:T(128)}, /*index=5*/s32[]{:T(128)}, s32[]{:T(128)}, s32[]{:T(128)}) while((s32[]{:T(128)}, f32[2048,128]{1,0:T(8,128)S(1)}, s32[2048,8]{0,1:T(8,128)S(1)}, bf16[2048,128]{1,0:T(8,128)(2,1)}, ...), condition=%wide.region_1.2_spmd.clone, body=%wide.region_0.1_spmd.clone.sunk | while | flops 294126080 | bytes 2429077 | solution.py:109
  40.5 4.4 %convolution_add_fusion.2 = f32[2048,128]{1,0:T(8,128)S(1)} fusion(s32[512]{0:T(512)S(1)} %iota_add_fusion.2, s32[2048]{0:T(1024)S(1)} %bitcast.56, s32[2048]{0:T(1024)S(1)} %bitcast.57, s32[2048]{0:T(1024)S(1)} %bitcast.58, s32[2048]{0:T(1024)S(1)} %bitcast.59, s32[2048]{0:T(1024)S(1)} %bitcast.60, s32[2048]{0:T(1024)S(1)} %bitcast.61, ...), kind=kOutput, calls=%fused_computation.2.clone.1 | convolution fusion | flops 294125568 | bytes 2295813 | tf_op jit(solution)/shard_map/while/body/eval_jaxpr/dot_general | solution.py:105
  45.0 4.4 %convolution_add_fusion.2 = f32[2048,128]{1,0:T(8,128)S(1)} fusion(s32[512]{0:T(512)S(1)} %iota_add_fusion.2, s32[2048]{0:T(1024)S(1)} %bitcast.56, s32[2048]{0:T(1024)S(1)} %bitcast.57, s32[2048]{0:T(1024)S(1)} %bitcast.58, s32[2048]{0:T(1024)S(1)} %bitcast.59, s32[2048]{0:T(1024)S(1)} %bitcast.60, s32[2048]{0:T(1024)S(1)} %bitcast.61, ...), kind=kOutput, calls=%fused_computation.2.clone.1 | convolution fusion | flops 294125568 | bytes 2295813 | tf_op jit(solution)/shard_map/while/body/eval_jaxpr/dot_general | solution.py:105
  49.5 4.4 %convolution_add_fusion.2 = f32[2048,128]{1,0:T(8,128)S(1)} fusion(s32[512]{0:T(512)S(1)} %iota_add_fusion.2, s32[2048]{0:T(1024)S(1)} %bitcast.56, s32[2048]{0:T(1024)S(1)} %bitcast.57, s32[2048]{0:T(1024)S(1)} %bitcast.58, s32[2048]{0:T(1024)S(1)} %bitcast.59, s32[2048]{0:T(1024)S(1)} %bitcast.60, s32[2048]{0:T(1024)S(1)} %bitcast.61, ...), kind=kOutput, calls=%fused_computation.2.clone.1 | convolution fusion | flops 294125568 | bytes 2295813 | tf_op jit(solution)/shard_map/while/body/eval_jaxpr/dot_general | solution.py:105
  54.0 4.4 %convolution_add_fusion.2 = f32[2048,128]{1,0:T(8,128)S(1)} fusion(s32[512]{0:T(512)S(1)} %iota_add_fusion.2, s32[2048]{0:T(1024)S(1)} %bitcast.56, s32[2048]{0:T(1024)S(1)} %bitcast.57, s32[2048]{0:T(1024)S(1)} %bitcast.58, s32[2048]{0:T(1024)S(1)} %bitcast.59, s32[2048]{0:T(1024)S(1)} %bitcast.60, s32[2048]{0:T(1024)S(1)} %bitcast.61, ...), kind=kOutput, calls=%fused_computation.2.clone.1 | convolution fusion | flops 294125568 | bytes 2295813 | tf_op jit(solution)/shard_map/while/body/eval_jaxpr/dot_general | solution.py:105
  58.5 4.7 %all_to_all.15 = f32[64,2,1,16,128]{4,3,0,2,1:T(8,128)S(1)} all-to-all(f32[64,2,1,16,128]{4,3,0,2,1:T(8,128)S(1)} %copy.41), channel_id=1, replica_groups=mesh['rows_0'=8,'rows_1'=8,'rows_2'=2,'rep'=4] {'rows_2'}, dimensions={1} | all-to-all | bytes 2097152 | tf_op jit(solution)/shard_map/all_to_all | solution.py:29
  63.2 1.1 copy.42
  64.3 4.8 %all-to-all-start.2 = ((f32[64,2,1,16,128]{4,3,1,2,0:T(8,128)}), f32[64,2,1,16,128]{4,3,1,2,0:T(8,128)S(1)}, u32[]{:S(2)}, u32[]{:S(2)}) async-start(f32[64,2,1,16,128]{4,3,1,2,0:T(8,128)} %copy.42), calls=%async_computation.2 | async-start | bytes 2097152 | tf_op jit(solution)/shard_map/all_to_all | solution.py:29
  69.2 0.7 all-gather.5.cloned.1.call-update
  69.9 10.6 %all_gather.11 = bf16[512,256]{0,1:T(8,128)(2,1)S(1)} all-gather(bf16[512,64]{0,1:T(8,128)(2,1)S(1)} %copy-done.2), channel_id=1, replica_groups=mesh['rows_0'=8,'rows_1'=8,'rows_2'=2,'rep'=4] {'rep'}, dimensions={1}, use_global_device_ids=true | all-gather | bytes 327680 | tf_op jit(solution)/shard_map/all_gather | solution.py:125
  80.9 15.7 %all-to-all-done.2 = f32[64,2,1,16,128]{4,3,1,2,0:T(8,128)S(1)} async-done(((f32[64,2,1,16,128]{4,3,1,2,0:T(8,128)}), f32[64,2,1,16,128]{4,3,1,2,0:T(8,128)S(1)}, u32[]{:S(2)}, u32[]{:S(2)}) %all-to-all-start.2) | async-done | bytes 1048608 | tf_op jit(solution)/shard_map/all_to_all | solution.py:29
  96.8 0.3 fusion.27
  97.2 1.0 gather_fusion
  98.4 2.4 %fusion.15 = bf16[16,1024]{1,0:T(8,128)(2,1)S(1)} fusion(bf16[1188,1024]{1,0:T(8,128)(2,1)} %all-gather.3.cloned.1.call-done, bf16[16,36]{1,0:T(8,128)(2,1)S(1)} %bitcast.64, bf16[16,128]{1,0:T(8,128)(2,1)S(1)} %get-tuple-element.116), kind=kOutput, calls=%fused_computation.18 | convolution fusion | flops 39004416 | bytes 2471040 | tf_op jit(solution)/shard_map/dot_general | solution.py:129
  100.8 6.1 %all-gather.5.cloned.1.call-done = bf16[1024,512]{1,0:T(8,128)(2,1)} async-done(((bf16[1024,128]{1,0:T(8,128)(2,1)}), bf16[1024,512]{1,0:T(8,128)(2,1)}) %all-gather.5.cloned.1.call-update) | async-done | bytes 1048592 | tf_op jit(solution)/shard_map/all_gather | solution.py:124
  106.9 1.6 %fusion.23 = bf16[16,256]{1,0:T(8,128)(2,1)S(1)} fusion(bf16[512,256]{0,1:T(8,128)(2,1)S(1)} %all_gather.11, bf16[16,1024]{1,0:T(8,128)(2,1)S(1)} %fusion.15, bf16[1024,512]{1,0:T(8,128)(2,1)} %all-gather.5.cloned.1.call-done), kind=kOutput, calls=%fused_computation.27 | convolution fusion | flops 20996096 | bytes 1351680 | tf_op jit(solution)/shard_map/dot_general | solution.py:129
  108.5 0.7 convolution_bitcast_fusion
  (42 shorter events, 2.1 us)
Async XLA Ops:
  6.5 74.0 %copy-start = (bf16[512,256]{1,0:T(8,128)(2,1)S(1)}, bf16[512,256]{1,0:T(8,128)(2,1)}, u32[]{:S(2)}) copy-start(bf16[512,256]{1,0:T(8,128)(2,1)} %param.23) | copy-start | bytes 786436
  8.2 29.9 %all-to-all-start = ((s32[128,1,128]{2,1,0:T(1,128)}), s32[128,1,128]{2,1,0:T(1,128)S(1)}, u32[]{:S(2)}, u32[]{:S(2)}) async-start(s32[128,1,128]{2,1,0:T(1,128)} %reshape.21), calls=%async_computation | async-start | bytes 131072 | tf_op jit(solution)/shard_map/all_to_all | solution.py:90
  26.7 71.7 %all-gather.3.cloned.1.call-start = ((), (), s32[]{:S(2)}) async-start(), calls=%async_computation.3 | async-start | bytes 3051520 | tf_op jit(solution)/shard_map/all_gather | solution.py:41
  63.2 6.7 %copy-start.6 = (bf16[256]{0:T(256)(128)(2,1)S(1)}, bf16[256]{0:T(256)(128)(2,1)}, u32[]{:S(2)}) copy-start(bf16[256]{0:T(256)(128)(2,1)} %param.29) | copy-start | bytes 1540
  63.2 6.7 %copy-start.2 = (bf16[512,64]{0,1:T(8,128)(2,1)S(1)}, bf16[512,64]{0,1:T(8,128)(2,1)}, u32[]{:S(2)}) copy-start(bf16[512,64]{0,1:T(8,128)(2,1)} %param.28) | copy-start | bytes 196612
  63.2 17.3 %copy-start.4 = (bf16[13,512]{1,0:T(8,128)(2,1)S(1)}, bf16[13,512]{1,0:T(8,128)(2,1)}, u32[]{:S(2)}) copy-start(bf16[13,512]{1,0:T(8,128)(2,1)} %param.22) | copy-start | bytes 39940
  63.2 17.3 %copy-start.5 = (bf16[16,13]{1,0:T(8,128)(2,1)S(1)}, bf16[16,13]{1,0:T(8,128)(2,1)}, u32[]{:S(2)}) copy-start(bf16[16,13]{1,0:T(8,128)(2,1)} %param.21) | copy-start | bytes 1252
  63.2 17.5 %copy-start.3 = (bf16[256,128]{1,0:T(8,128)(2,1)S(1)}, bf16[256,128]{1,0:T(8,128)(2,1)}, u32[]{:S(2)}) copy-start(bf16[256,128]{1,0:T(8,128)(2,1)} %param.24) | copy-start | bytes 196612
  64.3 32.9 %copy-start.1 = (s32[36]{0:T(128)S(1)}, s32[36]{0:T(128)}, u32[]{:S(2)}) copy-start(s32[36]{0:T(128)} %constant.114) | copy-start | bytes 436
  64.3 32.2 %all-to-all-start.2 = ((f32[64,2,1,16,128]{4,3,1,2,0:T(8,128)}), f32[64,2,1,16,128]{4,3,1,2,0:T(8,128)S(1)}, u32[]{:S(2)}, u32[]{:S(2)}) async-start(f32[64,2,1,16,128]{4,3,1,2,0:T(8,128)} %copy.42), calls=%async_computation.2 | async-start | bytes 2097152 | tf_op jit(solution)/shard_map/all_to_all | solution.py:29
  69.1 37.8 %all-gather.5.cloned.1.call-start = ((), (), s32[]{:S(2)}) async-start(), calls=%async_computation.4 | async-start | bytes 1310720 | tf_op jit(solution)/shard_map/all_gather | solution.py:124
Sparse Core Ops, SparseCore 0:
  29.6 42.5 all-gather.2
  74.3 32.5 all-gather.4
where the time goes:
time: 116 us
  waiting for transfers between devices  31.9 us (28%)
  starting transfers between devices  23.3 us (20%)
  matrix products  22.9 us (20%)
  blocking collectives  15.3 us (13%)
  between operations  13.6 us (12%)
  local copies, waits for them, and re-layouts  5.03 us (4%)
  other arithmetic  3.79 us (3%)
    all_to_all x1, starting transfers between devices, body(): lax.all_to_all(outgoing, ROWS, split_axis=0, concat_axis=0, tiled=True)  18.4 us
    dot_general x4, matrix products, add_block(): jnp.dot(counts.astype(jnp.bfloat16), block_table, preferred_element_type=...  17.6 us
    all_to_all x1, waiting for transfers between devices, turned_blocks(): result = lax.all_to_all(result, axes[k], k, k, tiled=True)  15.7 us
    all_gather x1, blocking collectives, body(): lax.all_gather(top_fourth, 'rep', axis=1, tiled=True)  10.6 us
    all_to_all x1, waiting for transfers between devices, body(): lax.all_to_all(outgoing, ROWS, split_axis=0, concat_axis=0, tiled=True)  9.4 us
    all_gather x1, waiting for transfers between devices, body(): lax.all_gather(top_third, 'rep', axis=1, tiled=True)  6.13 us
    all_to_all x1, starting transfers between devices, turned_blocks(): result = lax.all_to_all(result, axes[k], k, k, tiled=True)  4.78 us
    all_to_all x1, blocking collectives, turned_blocks(): result = lax.all_to_all(result, axes[k], k, k, tiled=True)  4.74 us
  transfers between devices with their start and end apart: 4, of which 3 were waited for; matrix products, arithmetic and copies ran while one was open for 24% of the time, Pallas kernels for 0%

commit v1 on v0

v1 whole, which is shorter than its diff:
```python
import functools

import jax
import jax.numpy as jnp
from jax import lax
from jax.experimental import pallas as pl
from jax.experimental.pallas import tpu as pltpu
from jax.sharding import Mesh
from jax.sharding import PartitionSpec as P

TAB = 8
HOT = 8
Y, Z, C, X = "y", "z", "c", "x"
ALL = (Y, Z, C, X)
LO = 256
GROUP = 2
HEAD_ROWS = 128
BF = jnp.bfloat16
F32 = jnp.float32
VM = pl.BlockSpec(memory_space=pltpu.VMEM)
SM = pl.BlockSpec(memory_space=pltpu.SMEM)
LANES = (((1,), (1,)), ((), ()))


def mm(a, b):
    return jnp.dot(a, b, preferred_element_type=F32)


def mm_t(a, b):
    return lax.dot_general(a, b, LANES, preferred_element_type=F32)


def relu(a):
    return jnp.maximum(a, 0.0)


def cost(micros):
    return pl.CostEstimate(flops=int(micros * 1.0e9), bytes_accessed=1 << 20, transcendentals=0)


def params(mib):
    return pltpu.CompilerParams(vmem_limit_bytes=mib << 20)


def prepare_kernel(peers, idx_ref, len_ref, out_ref):
    lens = len_ref[...]
    parts = [jnp.where(lens > h, idx_ref[:, h, :], -1) for h in range(HOT)]
    rows = jnp.concatenate(parts, axis=1)
    for t in range(TAB):
        out_ref[t * peers : (t + 1) * peers, :] = jnp.broadcast_to(
            rows[t : t + 1, :], (peers, rows.shape[1])
        )


def pack_kernel(
    meta_ref, w1_ref, w2_ref, w3_ref, w4_ref, dense_ref, b1_ref, b2_ref, b3_ref, pack_ref, bottom_ref
):
    core = meta_ref[2]
    w1 = w1_ref[...]
    lead, tail = w1[:HEAD_ROWS], w1[HEAD_ROWS:]
    padded = jnp.concatenate(
        [tail, jnp.zeros((HEAD_ROWS - tail.shape[0], tail.shape[1]), BF)], axis=0
    )
    pack_ref[0:HEAD_ROWS, :] = jnp.where(core == 0, lead, padded)
    at = HEAD_ROWS
    half = w2_ref.shape[0] // 2
    pack_ref[at : at + half, :] = w2_ref[pl.ds(pl.multiple_of(core * half, half), half), :]
    at += half
    half = w3_ref.shape[0] // 2
    quarter = half // 2
    for q in range(2):
        pack_ref[at : at + quarter, q * 128 : (q + 1) * 128] = w3_ref[
            pl.ds(pl.multiple_of(core * half + q * quarter, quarter), quarter), :
        ]
    at += quarter
    half = w4_ref.shape[1] // 2
    pack_ref[at : at + w4_ref.shape[0], :] = w4_ref[:, pl.ds(pl.multiple_of(core * half, half), half)]
    lower = relu(mm(dense_ref[...], b1_ref[...])).astype(BF)
    middle = relu(mm(lower, b2_ref[...])).astype(BF)
    bottom_ref[...] = relu(mm(middle, b3_ref[...]))


def lookup_kernel(meta_ref, idx_ref, own_ref, other_ref, out_ref, code_ref, lo_ref, count_ref):
    peers, width = idx_ref.shape
    samples = width // HOT
    span = own_ref.shape[0]
    held = 2 * span
    his = held // LO
    bags = GROUP * samples
    per_chunk = 256 // bags
    z, core = meta_ref[1], meta_ref[2]
    rel = idx_ref[...] - z * held
    valid = (rel >= 0) & (rel < held)
    rel = rel ^ (core * span)
    row = lax.broadcasted_iota(jnp.int32, (peers, width), 0)
    lane = lax.broadcasted_iota(jnp.int32, (peers, width), 1)
    bag = (row % GROUP) * samples + lane % samples
    code_ref[...] = jnp.where(valid, (rel // LO) * bags + bag, -1)
    lo_ref[...] = rel % LO
    entries = GROUP * width
    code_rows = lax.broadcasted_iota(jnp.int32, (his * bags, entries), 0)
    lo_rows = lax.broadcasted_iota(jnp.int32, (LO, entries), 0)

    def spread(ref, first):
        return jnp.concatenate([ref[pl.ds(first + k, 1), :] for k in range(GROUP)], axis=1)

    @pl.loop(0, peers // (GROUP * per_chunk))
    def _(chunk):
        for g in range(per_chunk):
            first = (chunk * per_chunk + g) * GROUP
            left = jnp.where(code_rows == spread(code_ref, first), 1.0, 0.0).astype(BF)
            right = jnp.where(lo_rows == spread(lo_ref, first), 1.0, 0.0).astype(BF)
            counts = mm_t(left, right).astype(BF)
            for hi in range(his):
                count_ref[g * bags : (g + 1) * bags, hi * LO : (hi + 1) * LO] = counts[
                    hi * bags : (hi + 1) * bags
                ]
        total = mm(count_ref[:, :span], own_ref[...]) + mm(count_ref[:, span:], other_ref[...])
        rows = per_chunk * bags
        out_ref[pl.ds(pl.multiple_of(chunk * rows, rows), rows), :] = total


def top_kernel(meta_ref, bags_ref, bottom_ref, w1_ref, w2_ref, w3_ref, w4_ref, last_ref, *rest):
    near, far = rest[0:3], rest[3:6]
    out_ref, in_ref, a1_ref, a2_ref, a3_ref = rest[6:]
    core, x = meta_ref[2], meta_ref[3]
    reps = 1 + len(near)
    peers = bags_ref.shape[0] // TAB
    bottom = bottom_ref[...]
    vectors = [bottom]
    for t in range(TAB):
        total = bags_ref[t * peers]
        for k in range(1, peers):
            total = total + bags_ref[t * peers + k]
        vectors.append(total)
    lane = lax.broadcasted_iota(jnp.int32, bottom.shape, 1)
    pairs = jnp.zeros(bottom.shape, F32)
    at = 0
    for i in range(TAB + 1):
        for j in range(i + 1, TAB + 1):
            dots = jnp.sum(vectors[i] * vectors[j], axis=1, keepdims=True)
            pairs = jnp.where(lane == at, dots, pairs)
            at += 1
    in_ref[0] = bottom.astype(BF)
    in_ref[1] = pairs.astype(BF)
    owners = [lax.rem(x - k + reps, reps) for k in range(reps)]
    halves = (core, 1 - core)

    def sides(k):
        return zip(halves, (near[k - 1], far[k - 1]))

    tail = w1_ref.shape[0] - HEAD_ROWS
    for k in range(reps):
        if k == 0:
            y = mm(in_ref[0], w1_ref[0:HEAD_ROWS, :]) + mm(in_ref[1][:, :tail], w1_ref[HEAD_ROWS:, :])
        else:
            y = sum(mm(in_ref[h], w[0:HEAD_ROWS, :]) for h, w in sides(k))
        a1_ref[owners[k]] = relu(y).astype(BF)
    base = HEAD_ROWS
    for k in range(reps):
        if k == 0:
            y = sum(mm(a1_ref[q], w2_ref[q * 256 : (q + 1) * 256, :]) for q in range(4))
        else:
            y = sum(
                mm(a1_ref[2 * h + q], w[base + q * 256 : base + (q + 1) * 256, :])
                for h, w in sides(k)
                for q in range(2)
            )
        a2_ref[owners[k]] = relu(y).astype(BF)
    base += 512
    for k in range(reps):
        if k == 0:
            y = sum(mm(a2_ref[q], w3_ref[q * 256 : (q + 1) * 256, :]) for q in range(4))
        else:
            y = sum(
                mm(a2_ref[2 * h + q], w[base : base + 256, q * 128 : (q + 1) * 128])
                for h, w in sides(k)
                for q in range(2)
            )
        a3_ref[owners[k]] = relu(y).astype(BF)
    base += 256
    logit = jnp.zeros(out_ref.shape, F32)
    for k in range(reps):
        if k == 0:
            y = sum(mm_t(a3_ref[q], w4_ref[:, q * 128 : (q + 1) * 128]) for q in range(4))
        else:
            y = sum(
                mm_t(a3_ref[2 * h + q], w[base : base + 64, q * 128 : (q + 1) * 128])
                for h, w in sides(k)
                for q in range(2)
            )
        logit = logit + mm_t(last_ref[owners[k]], relu(y).astype(BF))
    out_ref[...] = logit


def shifted(a, axis, k):
    n = lax.axis_size(axis)
    return lax.ppermute(a, axis, [(i, (i + k) % n) for i in range(n)])


def body(tables, indices, bag_lengths, dense, b1, b2, b3, w1, w2, w3, w4, last):
    samples, width = indices.shape[0], tables.shape[1]
    reps = lax.axis_size(X)
    along_z = lax.axis_size(Z)
    peers = lax.axis_size((Y, Z))
    meta = jnp.stack([lax.axis_index(a) for a in ALL]).astype(jnp.int32)
    rows = pl.pallas_call(
        functools.partial(prepare_kernel, along_z),
        out_shape=jax.ShapeDtypeStruct((peers, HOT * samples), jnp.int32),
        in_specs=[VM] * 2,
        out_specs=VM,
        compiler_params=params(8),
        cost_estimate=cost(1),
        name="prepare",
    )(jnp.transpose(indices, (1, 2, 0)), jnp.transpose(bag_lengths))
    rows, tables, meta = lax.optimization_barrier((rows, tables, meta))
    wanted = lax.all_to_all(rows, (Y, Z), 0, 0, tiled=True)
    other = shifted(tables, C, 1)
    w4t = jnp.transpose(w4)
    pack_rows = HEAD_ROWS + w2.shape[0] // 2 + w3.shape[0] // 4 + w4t.shape[0]
    pack, bottom = pl.pallas_call(
        pack_kernel,
        out_shape=(
            jax.ShapeDtypeStruct((pack_rows, w2.shape[1]), BF),
            jax.ShapeDtypeStruct((samples, width), F32),
        ),
        in_specs=[SM] + [VM] * 8,
        out_specs=(VM, VM),
        compiler_params=params(12),
        cost_estimate=cost(3),
        name="pack",
    )(meta, w1, w2, w3, w4t, dense, b1, b2, b3)
    near = [shifted(pack, X, k) for k in range(1, reps)]
    partial_bags = pl.pallas_call(
        lookup_kernel,
        out_shape=jax.ShapeDtypeStruct((peers * samples, width), F32),
        in_specs=[SM] + [VM] * 3,
        out_specs=VM,
        scratch_shapes=[
            pltpu.VMEM(wanted.shape, jnp.int32),
            pltpu.VMEM(wanted.shape, jnp.int32),
            pltpu.VMEM((256, 2 * tables.shape[0]), BF),
        ],
        compiler_params=params(24),
        cost_estimate=cost(40),
        name="lookup",
    )(meta, wanted, tables, other)
    partial_bags, *near = lax.optimization_barrier((partial_bags, *near))
    far = [shifted(p, C, 1) for p in near]
    bags = lax.all_to_all(
        partial_bags.reshape(peers, samples, width), (Y, Z), 0, 0, tiled=True
    )
    logit = pl.pallas_call(
        top_kernel,
        out_shape=jax.ShapeDtypeStruct((1, samples), F32),
        in_specs=[SM] + [VM] * 13,
        out_specs=VM,
        scratch_shapes=[
            pltpu.VMEM((2, samples, width), BF),
            pltpu.VMEM((reps, samples, w1.shape[1]), BF),
            pltpu.VMEM((reps, samples, w2.shape[1]), BF),
            pltpu.VMEM((reps, samples, w3.shape[1]), BF),
        ],
        compiler_params=params(16),
        cost_estimate=cost(5),
        name="top",
    )(meta, bags, bottom, w1, w2, w3, w4t, last.reshape(reps, 1, -1), *near, *far)
    return logit.reshape(samples)


def solution(mesh):
    torus = Mesh(mesh.devices.reshape(8, 8, 2, mesh.shape["rep"]), ALL)
    in_specs = (
        P((Y, Z, C), None),
        P(ALL, None, None),
        P(ALL, None),
        P(ALL, None),
        P(),
        P(),
        P(),
        P(None, X),
        P(None, X),
        P(None, X),
        P(None, X),
        P(),
    )
    return jax.shard_map(body, mesh=torus, in_specs=in_specs, out_specs=P(ALL), check_vma=False)
```

time: 116 us -> 90.3 us (0.78)
  the two profiles are of different devices: /device:TPU:1 before, /device:TPU:16 now
where the time goes in v1:
time: 90.3 us; the launch traced here: 89.7 us
  starting transfers between devices  47.6 us (53%)
  waiting for transfers between devices  27.7 us (31%)
  Pallas kernels  12.3 us (14%)
  local copies, waits for them, and re-layouts  1.81 us (2%)
    ppermute x7, starting transfers between devices, shifted(): return lax.ppermute(a, axis, [(i, (i + k) % n) for i in range(n)])  18.3 us
    all_to_all x1, starting transfers between devices, body(): wanted = lax.all_to_all(rows, (Y, Z), 0, 0, tiled=True)  16.5 us
    ppermute x7, waiting for transfers between devices, shifted(): return lax.ppermute(a, axis, [(i, (i + k) % n) for i in range(n)])  16.4 us
    all_to_all x1, starting transfers between devices, body(): lax.all_to_all(partial_bags.reshape(peers, samples, width), (Y, Z), 0, 0,...  12.8 us
    all_to_all x1, waiting for transfers between devices, body(): lax.all_to_all(partial_bags.reshape(peers, samples, width), (Y, Z), 0, 0,...  11.4 us
    pallas_call x1, Pallas kernels, body(): pl.pallas_call(lookup_kernel, out_shape=jax.ShapeDtypeStruct((peers * sam...  6.88 us
    pallas_call x1, Pallas kernels, body(): pl.pallas_call(top_kernel, out_shape=jax.ShapeDtypeStruct((1, samples), F...  3.13 us
  transfers between devices with their start and end apart: 9, of which 4 were waited for; matrix products, arithmetic and copies ran while one was open for 0% of the time, Pallas kernels for 9%

profile of v1, /device:TPU:16, one launch (start us, length us, event | category | flops | bytes accessed | tf_op | source)
XLA Modules:
  0.0 89.7 jit_solution(1766058912992686887)
XLA Ops:
  0.0 0.7 copy-done.9
  0.7 0.8 copy-done.7
  1.5 0.7 prepare.1
  2.2 0.1 pad_add_fusion.meta_ref
  2.3 0.2 copy-done
  2.5 1.9 %collective-permute-start = (bf16[2048,128]{1,0:T(8,128)(2,1)S(1)}, bf16[2048,128]{1,0:T(8,128)(2,1)S(1)}, u32[]{:S(2)}, u32[]{:S(2)}) collective-permute-start(bf16[2048,128]{1,0:T(8,128)(2,1)S(1)} %copy-done), channel_id=1, source_target_pairs={{0,4},{4,0},{1,5},{5,1},{2,6},{6,2},{3,7},{7,3},{8,12},{12,8},{9,1... | collective-permute-start | bytes 1572872 | tf_op jit(solution)/shard_map/ppermute | solution.py:198
  4.4 0.0 copy-start.10
  4.4 16.5 %all-to-all-start = ((s32[64,1,128]{2,1,0:T(1,128)}), s32[64,1,128]{2,1,0:T(1,128)S(1)}, u32[]{:S(2)}, u32[]{:S(2)}) async-start(s32[64,1,128]{2,1,0:T(1,128)} %bitcast.7), calls=%async_computation | async-start | bytes 65536 | tf_op jit(solution)/shard_map/all_to_all | solution.py:217
  21.0 1.6 %pack.1 = (bf16[960,256]{1,0:T(8,128)(2,1)}, f32[16,128]{1,0:T(8,128)S(1)}) custom-call(s32[4]{0:T(128)S(1)} %pad_add_fusion.meta_ref, bf16[164,256]{1,0:T(8,128)(2,1)S(1)} %copy-done.4, bf16[1024,256]{1,0:T(8,128)(2,1)S(1)} %copy-done.1, bf16[1024,128]{1,0:T(8,128)(2,1)S(1)} %copy-done.3, bf16[64,512]{1,0:T(8,128)(2,1)S(1)} %bitcast.14, ...), custom_call_target="tpu_custom_call" | custom-call | flops 3000000000 | bytes 1048576 | tf_op jit(solution)/shard_map/pack/pallas_call | solution.py:221
  22.6 4.7 %collective-permute-start.3 = (bf16[960,256]{1,0:T(8,128)(2,1)}, bf16[960,256]{1,0:T(8,128)(2,1)S(1)}, u32[]{:S(2)}, u32[]{:S(2)}) collective-permute-start(bf16[960,256]{1,0:T(8,128)(2,1)} %get-tuple-element.17), channel_id=1, source_target_pairs={{0,3},{1,0},{2,1},{3,2},{4,7},{5,4},{6,5},{7,6},{8,11},{9,8},{10,9... | collective-permute-start | bytes 1474568 | tf_op jit(solution)/shard_map/ppermute | solution.py:198
  27.2 2.7 %collective-permute-start.2 = (bf16[960,256]{1,0:T(8,128)(2,1)}, bf16[960,256]{1,0:T(8,128)(2,1)S(1)}, u32[]{:S(2)}, u32[]{:S(2)}) collective-permute-start(bf16[960,256]{1,0:T(8,128)(2,1)} %get-tuple-element.17), channel_id=1, source_target_pairs={{0,2},{1,3},{2,0},{3,1},{4,6},{5,7},{6,4},{7,5},{8,10},{9,11},{10,... | collective-permute-start | bytes 1474568 | tf_op jit(solution)/shard_map/ppermute | solution.py:198
  30.0 2.8 %collective-permute-start.1 = (bf16[960,256]{1,0:T(8,128)(2,1)}, bf16[960,256]{1,0:T(8,128)(2,1)S(1)}, u32[]{:S(2)}, u32[]{:S(2)}) collective-permute-start(bf16[960,256]{1,0:T(8,128)(2,1)} %get-tuple-element.17), channel_id=1, source_target_pairs={{0,1},{1,2},{2,3},{3,0},{4,5},{5,6},{6,7},{7,4},{8,9},{9,10},{10,1... | collective-permute-start | bytes 1474568 | tf_op jit(solution)/shard_map/ppermute | solution.py:198
  32.8 0.0 all-to-all-done
  32.8 6.9 %lookup.1 = f32[1024,128]{1,0:T(8,128)} custom-call(s32[4]{0:T(128)S(1)} %pad_add_fusion.meta_ref, s32[64,128]{1,0:T(8,128)S(1)} %bitcast.13, bf16[2048,128]{1,0:T(8,128)(2,1)S(1)} %copy-done, bf16[2048,128]{1,0:T(8,128)(2,1)S(1)} %collective-permute-done.other_ref), custom_call_target="tpu_custom_call" | custom-call | flops 40000000000 | bytes 1048576 | tf_op jit(solution)/shard_map/lookup/pallas_call | solution.py:234
  39.7 9.0 %collective-permute-done.3.rest_2_ = bf16[960,256]{1,0:T(8,128)(2,1)S(1)} collective-permute-done((bf16[960,256]{1,0:T(8,128)(2,1)}, bf16[960,256]{1,0:T(8,128)(2,1)S(1)}, u32[]{:S(2)}, u32[]{:S(2)}) %collective-permute-start.3) | collective-permute-done | bytes 491552 | tf_op jit(solution)/shard_map/ppermute | solution.py:198
  48.7 5.5 %collective-permute-done.1.rest_0_ = bf16[960,256]{1,0:T(8,128)(2,1)S(1)} collective-permute-done((bf16[960,256]{1,0:T(8,128)(2,1)}, bf16[960,256]{1,0:T(8,128)(2,1)S(1)}, u32[]{:S(2)}, u32[]{:S(2)}) %collective-permute-start.1) | collective-permute-done | bytes 491552 | tf_op jit(solution)/shard_map/ppermute | solution.py:198
  54.2 12.8 %all-to-all-start.1 = ((f32[64,16,128]{2,1,0:T(8,128)}), f32[64,16,128]{2,1,0:T(8,128)S(1)}, u32[]{:S(2)}, u32[]{:S(2)}) async-start(f32[64,16,128]{2,1,0:T(8,128)} %bitcast.10), calls=%async_computation.1 | async-start | bytes 1048576 | tf_op jit(solution)/shard_map/all_to_all | solution.py:250
  67.0 1.9 %collective-permute-start.4 = (bf16[960,256]{1,0:T(8,128)(2,1)S(1)}, bf16[960,256]{1,0:T(8,128)(2,1)S(1)}, u32[]{:S(2)}, u32[]{:S(2)}) collective-permute-start(bf16[960,256]{1,0:T(8,128)(2,1)S(1)} %collective-permute-done.1.rest_0_), channel_id=1, source_target_pairs={{0,4},{4,0},{1,5},{5,1},{2,6},{6,2},{3,7},{7,3},{8,12},{12,8},{9,1... | collective-permute-start | bytes 1474568 | tf_op jit(solution)/shard_map/ppermute | solution.py:198
  68.9 2.4 %collective-permute-start.5 = (bf16[960,256]{1,0:T(8,128)(2,1)S(1)}, bf16[960,256]{1,0:T(8,128)(2,1)}, u32[]{:S(2)}, u32[]{:S(2)}) collective-permute-start(bf16[960,256]{1,0:T(8,128)(2,1)S(1)} %collective-permute-done.2.rest_1_), channel_id=1, source_target_pairs={{0,4},{4,0},{1,5},{5,1},{2,6},{6,2},{3,7},{7,3},{8,12},{12,8},{9,1... | collective-permute-start | bytes 1474568 | tf_op jit(solution)/shard_map/ppermute | solution.py:198
  71.4 1.9 %collective-permute-start.6 = (bf16[960,256]{1,0:T(8,128)(2,1)S(1)}, bf16[960,256]{1,0:T(8,128)(2,1)}, u32[]{:S(2)}, u32[]{:S(2)}) collective-permute-start(bf16[960,256]{1,0:T(8,128)(2,1)S(1)} %collective-permute-done.3.rest_2_), channel_id=1, source_target_pairs={{0,4},{4,0},{1,5},{5,1},{2,6},{6,2},{3,7},{7,3},{8,12},{12,8},{9,1... | collective-permute-start | bytes 1474568 | tf_op jit(solution)/shard_map/ppermute | solution.py:198
  73.3 0.1 reshape.14.last_ref
  73.4 1.9 %collective-permute-done.6.rest_5_ = bf16[960,256]{1,0:T(8,128)(2,1)} collective-permute-done((bf16[960,256]{1,0:T(8,128)(2,1)S(1)}, bf16[960,256]{1,0:T(8,128)(2,1)}, u32[]{:S(2)}, u32[]{:S(2)}) %collective-permute-start.6) | collective-permute-done | bytes 491552 | tf_op jit(solution)/shard_map/ppermute | solution.py:198
  75.2 11.4 %all-to-all-done.1.bags_ref = f32[64,16,128]{2,1,0:T(8,128)S(1)} async-done(((f32[64,16,128]{2,1,0:T(8,128)}), f32[64,16,128]{2,1,0:T(8,128)S(1)}, u32[]{:S(2)}, u32[]{:S(2)}) %all-to-all-start.1) | async-done | bytes 524320 | tf_op jit(solution)/shard_map/all_to_all | solution.py:250
  86.6 3.1 %top.1 = f32[1,16]{1,0:T(1,128)} custom-call(s32[4]{0:T(128)S(1)} %pad_add_fusion.meta_ref, f32[64,16,128]{2,1,0:T(8,128)S(1)} %all-to-all-done.1.bags_ref, f32[16,128]{1,0:T(8,128)S(1)} %get-tuple-element.19.bottom_ref, bf16[164,256]{1,0:T(8,128)(2,1)S(1)} %copy-done.4, bf16[1024,256]{1,0:T(8,128)(2,1)S(1)} %copy-done.1, bf16[1024,128]{1,0:T(8,128)(2,1)S(1)} %copy-done.3, ...), custom_call_target="tpu_custom_call" | custom-call | flops 5000000000 | bytes 1048576 | tf_op jit(solution)/shard_map/top/pallas_call | solution.py:253
  (24 shorter events, 0.0 us)
Async XLA Ops:
  0.0 0.7 copy-start.9
  0.7 0.8 copy-start.7
  1.4 1.1 %copy-start = (bf16[2048,128]{1,0:T(8,128)(2,1)S(1)}, bf16[2048,128]{1,0:T(8,128)(2,1)}, u32[]{:S(2)}) copy-start(bf16[2048,128]{1,0:T(8,128)(2,1)} %own_ref) | copy-start | bytes 1572868
  1.4 19.5 %copy-start.1 = (bf16[1024,256]{1,0:T(8,128)(2,1)S(1)}, bf16[1024,256]{1,0:T(8,128)(2,1)}, u32[]{:S(2)}) copy-start(bf16[1024,256]{1,0:T(8,128)(2,1)} %w2_ref.3) | copy-start | bytes 1572868
  1.5 19.5 %copy-start.2 = (bf16[512,256]{1,0:T(8,128)(2,1)S(1)}, bf16[512,256]{1,0:T(8,128)(2,1)}, u32[]{:S(2)}) copy-start(bf16[512,256]{1,0:T(8,128)(2,1)} %b2_ref.1) | copy-start | bytes 786436
  1.5 19.5 %copy-start.3 = (bf16[1024,128]{1,0:T(8,128)(2,1)S(1)}, bf16[1024,128]{1,0:T(8,128)(2,1)}, u32[]{:S(2)}) copy-start(bf16[1024,128]{1,0:T(8,128)(2,1)} %w3_ref.3) | copy-start | bytes 786436
  1.5 19.5 %copy-start.4 = (bf16[164,256]{1,0:T(8,128)(2,1)S(1)}, bf16[164,256]{1,0:T(8,128)(2,1)}, u32[]{:S(2)}) copy-start(bf16[164,256]{1,0:T(8,128)(2,1)} %w1_ref.3) | copy-start | bytes 251908
  1.5 19.5 %copy-start.6 = (bf16[512,64]{0,1:T(8,128)(2,1)S(1)}, bf16[512,64]{0,1:T(8,128)(2,1)}, u32[]{:S(2)}) copy-start(bf16[512,64]{0,1:T(8,128)(2,1)} %param.22) | copy-start | bytes 196612
  1.5 19.5 %copy-start.8 = (bf16[13,512]{1,0:T(8,128)(2,1)S(1)}, bf16[13,512]{1,0:T(8,128)(2,1)}, u32[]{:S(2)}) copy-start(bf16[13,512]{1,0:T(8,128)(2,1)} %b1_ref.1) | copy-start | bytes 39940
  2.2 18.8 %copy-start.5 = (bf16[256,128]{1,0:T(8,128)(2,1)S(1)}, bf16[256,128]{1,0:T(8,128)(2,1)}, u32[]{:S(2)}) copy-start(bf16[256,128]{1,0:T(8,128)(2,1)} %b3_ref.1) | copy-start | bytes 196612
  2.5 30.3 %collective-permute-start = (bf16[2048,128]{1,0:T(8,128)(2,1)S(1)}, bf16[2048,128]{1,0:T(8,128)(2,1)S(1)}, u32[]{:S(2)}, u32[]{:S(2)}) collective-permute-start(bf16[2048,128]{1,0:T(8,128)(2,1)S(1)} %copy-done), channel_id=1, source_target_pairs={{0,4},{4,0},{1,5},{5,1},{2,6},{6,2},{3,7},{7,3},{8,12},{12,8},{9,1... | collective-permute-start | bytes 1572872 | tf_op jit(solution)/shard_map/ppermute | solution.py:198
  4.4 16.6 %copy-start.10 = (bf16[16,13]{1,0:T(8,128)(2,1)S(1)}, bf16[16,13]{1,0:T(8,128)(2,1)}, u32[]{:S(2)}) copy-start(bf16[16,13]{1,0:T(8,128)(2,1)} %dense_ref.1) | copy-start | bytes 1252
  4.4 28.3 %all-to-all-start = ((s32[64,1,128]{2,1,0:T(1,128)}), s32[64,1,128]{2,1,0:T(1,128)S(1)}, u32[]{:S(2)}, u32[]{:S(2)}) async-start(s32[64,1,128]{2,1,0:T(1,128)} %bitcast.7), calls=%async_computation | async-start | bytes 65536 | tf_op jit(solution)/shard_map/all_to_all | solution.py:217
  22.6 26.1 %collective-permute-start.3 = (bf16[960,256]{1,0:T(8,128)(2,1)}, bf16[960,256]{1,0:T(8,128)(2,1)S(1)}, u32[]{:S(2)}, u32[]{:S(2)}) collective-permute-start(bf16[960,256]{1,0:T(8,128)(2,1)} %get-tuple-element.17), channel_id=1, source_target_pairs={{0,3},{1,0},{2,1},{3,2},{4,7},{5,4},{6,5},{7,6},{8,11},{9,8},{10,9... | collective-permute-start | bytes 1474568 | tf_op jit(solution)/shard_map/ppermute | solution.py:198
  27.2 21.4 %collective-permute-start.2 = (bf16[960,256]{1,0:T(8,128)(2,1)}, bf16[960,256]{1,0:T(8,128)(2,1)S(1)}, u32[]{:S(2)}, u32[]{:S(2)}) collective-permute-start(bf16[960,256]{1,0:T(8,128)(2,1)} %get-tuple-element.17), channel_id=1, source_target_pairs={{0,2},{1,3},{2,0},{3,1},{4,6},{5,7},{6,4},{7,5},{8,10},{9,11},{10,... | collective-permute-start | bytes 1474568 | tf_op jit(solution)/shard_map/ppermute | solution.py:198
  30.0 24.2 %collective-permute-start.1 = (bf16[960,256]{1,0:T(8,128)(2,1)}, bf16[960,256]{1,0:T(8,128)(2,1)S(1)}, u32[]{:S(2)}, u32[]{:S(2)}) collective-permute-start(bf16[960,256]{1,0:T(8,128)(2,1)} %get-tuple-element.17), channel_id=1, source_target_pairs={{0,1},{1,2},{2,3},{3,0},{4,5},{5,6},{6,7},{7,4},{8,9},{9,10},{10,1... | collective-permute-start | bytes 1474568 | tf_op jit(solution)/shard_map/ppermute | solution.py:198
  54.2 19.1 %copy-start.11 = (bf16[256]{0:T(256)(128)(2,1)S(1)}, bf16[256]{0:T(256)(128)(2,1)}, u32[]{:S(2)}) copy-start(bf16[256]{0:T(256)(128)(2,1)} %param.23) | copy-start | bytes 1540
  54.2 32.4 %all-to-all-start.1 = ((f32[64,16,128]{2,1,0:T(8,128)}), f32[64,16,128]{2,1,0:T(8,128)S(1)}, u32[]{:S(2)}, u32[]{:S(2)}) async-start(f32[64,16,128]{2,1,0:T(8,128)} %bitcast.10), calls=%async_computation.1 | async-start | bytes 1048576 | tf_op jit(solution)/shard_map/all_to_all | solution.py:250
  67.0 6.4 %collective-permute-start.4 = (bf16[960,256]{1,0:T(8,128)(2,1)S(1)}, bf16[960,256]{1,0:T(8,128)(2,1)S(1)}, u32[]{:S(2)}, u32[]{:S(2)}) collective-permute-start(bf16[960,256]{1,0:T(8,128)(2,1)S(1)} %collective-permute-done.1.rest_0_), channel_id=1, source_target_pairs={{0,4},{4,0},{1,5},{5,1},{2,6},{6,2},{3,7},{7,3},{8,12},{12,8},{9,1... | collective-permute-start | bytes 1474568 | tf_op jit(solution)/shard_map/ppermute | solution.py:198
  68.9 4.4 %collective-permute-start.5 = (bf16[960,256]{1,0:T(8,128)(2,1)S(1)}, bf16[960,256]{1,0:T(8,128)(2,1)}, u32[]{:S(2)}, u32[]{:S(2)}) collective-permute-start(bf16[960,256]{1,0:T(8,128)(2,1)S(1)} %collective-permute-done.2.rest_1_), channel_id=1, source_target_pairs={{0,4},{4,0},{1,5},{5,1},{2,6},{6,2},{3,7},{7,3},{8,12},{12,8},{9,1... | collective-permute-start | bytes 1474568 | tf_op jit(solution)/shard_map/ppermute | solution.py:198
  71.4 3.9 %collective-permute-start.6 = (bf16[960,256]{1,0:T(8,128)(2,1)S(1)}, bf16[960,256]{1,0:T(8,128)(2,1)}, u32[]{:S(2)}, u32[]{:S(2)}) collective-permute-start(bf16[960,256]{1,0:T(8,128)(2,1)S(1)} %collective-permute-done.3.rest_2_), channel_id=1, source_target_pairs={{0,4},{4,0},{1,5},{5,1},{2,6},{6,2},{3,7},{7,3},{8,12},{12,8},{9,1... | collective-permute-start | bytes 1474568 | tf_op jit(solution)/shard_map/ppermute | solution.py:198

commit v2 on v1

v2 whole, which is shorter than its diff:
```python
import functools

import jax
import jax.numpy as jnp
from jax import lax
from jax.experimental import pallas as pl
from jax.experimental.pallas import tpu as pltpu
from jax.sharding import Mesh
from jax.sharding import PartitionSpec as P

TAB = 8
HOT = 8
Y, Z, C, X = "y", "z", "c", "x"
ALL = (Y, Z, C, X)
LO = 256
HEAD_ROWS = 128
BF = jnp.bfloat16
F8 = jnp.float8_e4m3fn
F32 = jnp.float32
VM = pl.BlockSpec(memory_space=pltpu.VMEM)
SM = pl.BlockSpec(memory_space=pltpu.SMEM)
LANES = (((1,), (1,)), ((), ()))


def mm(a, b):
    return jnp.dot(a, b, preferred_element_type=F32)


def mm_t(a, b):
    return lax.dot_general(a, b, LANES, preferred_element_type=F32)


def relu(a):
    return jnp.maximum(a, 0.0)


def cost(micros):
    return pl.CostEstimate(flops=int(micros * 1.0e9), bytes_accessed=1 << 20, transcendentals=0)


def params(mib):
    return pltpu.CompilerParams(vmem_limit_bytes=mib << 20)


def prepare_kernel(peers, idx_ref, len_ref, out_ref):
    lens = len_ref[...]
    parts = [jnp.where(lens > h, idx_ref[:, h, :], -1) for h in range(HOT)]
    rows = jnp.concatenate(parts, axis=1)
    for t in range(TAB):
        out_ref[t * peers : (t + 1) * peers, :] = jnp.broadcast_to(
            rows[t : t + 1, :], (peers, rows.shape[1])
        )


def pack_kernel(
    meta_ref, w1_ref, w2_ref, w3_ref, w4_ref, dense_ref, b1_ref, b2_ref, b3_ref, pack_ref, half_ref, bottom_ref
):
    core = meta_ref[2]
    tail = w1_ref[HEAD_ROWS:, :]
    pack_ref[0, 0:HEAD_ROWS, :] = w1_ref[0:HEAD_ROWS, :]
    pack_ref[1, 0:HEAD_ROWS, :] = jnp.concatenate(
        [tail, jnp.zeros((HEAD_ROWS - tail.shape[0], tail.shape[1]), BF)], axis=0
    )
    for h in range(2):
        at = HEAD_ROWS
        half = w2_ref.shape[0] // 2
        pack_ref[h, at : at + half, :] = w2_ref[h * half : (h + 1) * half, :]
        at += half
        half = w3_ref.shape[0] // 2
        quarter = half // 2
        for q in range(2):
            first = h * half + q * quarter
            pack_ref[h, at : at + quarter, q * 128 : (q + 1) * 128] = w3_ref[first : first + quarter, :]
        at += quarter
        half = w4_ref.shape[1] // 2
        pack_ref[h, at : at + w4_ref.shape[0], :] = w4_ref[:, h * half : (h + 1) * half]
    half_ref[...] = pack_ref[core]
    lower = relu(mm(dense_ref[...], b1_ref[...])).astype(BF)
    middle = relu(mm(lower, b2_ref[...])).astype(BF)
    bottom_ref[...] = relu(mm(middle, b3_ref[...]))


def lookup_kernel(meta_ref, idx_ref, own_ref, other_ref, out_ref, code_ref, lo_ref, count_ref):
    peers, width = idx_ref.shape
    bags = width // HOT
    span = own_ref.shape[0]
    held = 2 * span
    his = held // LO
    rows = count_ref.shape[0]
    per_chunk = rows // bags
    z, core = meta_ref[1], meta_ref[2]
    rel = idx_ref[...] - z * held
    valid = (rel >= 0) & (rel < held)
    rel = rel ^ (core * span)
    bag = lax.broadcasted_iota(jnp.int32, (peers, width), 1) % bags
    code_ref[...] = jnp.where(valid, (rel // LO) * bags + bag, -1)
    lo_ref[...] = rel % LO
    one, zero = jnp.ones((), BF), jnp.zeros((), BF)

    def one_hot(height, ref, peer):
        ids = lax.broadcasted_iota(jnp.int16, (height, width), 0)
        return jnp.where(ids == ref[pl.ds(peer, 1), :].astype(jnp.int16), one, zero).astype(F8)

    @pl.loop(0, peers // per_chunk)
    def _(chunk):
        for g in range(per_chunk):
            peer = chunk * per_chunk + g
            left = one_hot(his * bags, code_ref, peer)
            counts = mm_t(left, one_hot(LO, lo_ref, peer)).astype(BF)
            for hi in range(his):
                count_ref[g * bags : (g + 1) * bags, hi * LO : (hi + 1) * LO] = counts[
                    hi * bags : (hi + 1) * bags
                ]
        total = mm(count_ref[:, :span], own_ref[...]) + mm(count_ref[:, span:], other_ref[...])
        out_ref[pl.ds(pl.multiple_of(chunk * rows, rows), rows), :] = total


def top_kernel(
    meta_ref, bags_ref, bottom_ref, last_ref, own_ref, side_ref, mirror_ref, near_ref, far_ref,
    out_ref, in_ref, a1_ref, a2_ref, a3_ref,
):
    core, x = meta_ref[2], meta_ref[3]
    reps = last_ref.shape[0]
    peers = bags_ref.shape[0] // TAB
    bottom = bottom_ref[...]
    vectors = [bottom]
    for t in range(TAB):
        total = bags_ref[t * peers]
        for k in range(1, peers):
            total = total + bags_ref[t * peers + k]
        vectors.append(total)
    lane = lax.broadcasted_iota(jnp.int32, bottom.shape, 1)
    pairs = jnp.zeros(bottom.shape, F32)
    at = 0
    for i in range(TAB + 1):
        for j in range(i + 1, TAB + 1):
            dots = jnp.sum(vectors[i] * vectors[j], axis=1, keepdims=True)
            pairs = jnp.where(lane == at, dots, pairs)
            at += 1
    in_ref[0] = bottom.astype(BF)
    in_ref[1] = pairs.astype(BF)

    def whole(ref):
        return [(h, ref.at[h]) for h in range(2)]

    before, after = lax.rem(x + reps - 1, reps), lax.rem(x + 1, reps)
    shards = (
        (x, whole(own_ref)),
        (jnp.where(core == 0, before, after), whole(side_ref)),
        (jnp.where(core == 0, after, before), whole(mirror_ref)),
        (lax.rem(x + 2, reps), [(core, near_ref), (1 - core, far_ref)]),
    )
    for owner, halves in shards:
        y = sum(mm(in_ref[h], w[0:HEAD_ROWS, :]) for h, w in halves)
        a1_ref[owner] = relu(y).astype(BF)
    base = HEAD_ROWS
    for owner, halves in shards:
        y = sum(
            mm(a1_ref[2 * h + q], w[base + q * 256 : base + (q + 1) * 256, :])
            for h, w in halves
            for q in range(2)
        )
        a2_ref[owner] = relu(y).astype(BF)
    base += 512
    for owner, halves in shards:
        y = sum(
            mm(a2_ref[2 * h + q], w[base : base + 256, q * 128 : (q + 1) * 128])
            for h, w in halves
            for q in range(2)
        )
        a3_ref[owner] = relu(y).astype(BF)
    base += 256
    logit = jnp.zeros(out_ref.shape, F32)
    for owner, halves in shards:
        y = sum(
            mm_t(a3_ref[2 * h + q], w[base : base + 64, q * 128 : (q + 1) * 128])
            for h, w in halves
            for q in range(2)
        )
        logit = logit + mm_t(last_ref[owner], relu(y).astype(BF))
    out_ref[...] = logit


def shifted(a, axis, k):
    n = lax.axis_size(axis)
    return lax.ppermute(a, axis, [(i, (i + k) % n) for i in range(n)])


def body(tables, indices, bag_lengths, dense, b1, b2, b3, w1, w2, w3, w4, last):
    samples, width = indices.shape[0], tables.shape[1]
    reps = lax.axis_size(X)
    along_z = lax.axis_size(Z)
    peers = lax.axis_size((Y, Z))
    meta = jnp.stack([lax.axis_index(a) for a in ALL]).astype(jnp.int32)
    rows = pl.pallas_call(
        functools.partial(prepare_kernel, along_z),
        out_shape=jax.ShapeDtypeStruct((peers, HOT * samples), jnp.int32),
        in_specs=[VM] * 2,
        out_specs=VM,
        compiler_params=params(8),
        cost_estimate=cost(1),
        name="prepare",
    )(jnp.transpose(indices, (1, 2, 0)), jnp.transpose(bag_lengths))
    rows, tables, meta = lax.optimization_barrier((rows, tables, meta))
    wanted = lax.all_to_all(rows, (Y, Z), 0, 0, tiled=True)
    other = shifted(tables, C, 1)
    w4t = jnp.transpose(w4)
    pack_rows = HEAD_ROWS + w2.shape[0] // 2 + w3.shape[0] // 4 + w4t.shape[0]
    pack, half, bottom = pl.pallas_call(
        pack_kernel,
        out_shape=(
            jax.ShapeDtypeStruct((2, pack_rows, w2.shape[1]), BF),
            jax.ShapeDtypeStruct((pack_rows, w2.shape[1]), BF),
            jax.ShapeDtypeStruct((samples, width), F32),
        ),
        in_specs=[SM] + [VM] * 8,
        out_specs=(VM, VM, VM),
        compiler_params=params(12),
        cost_estimate=cost(3),
        name="pack",
    )(meta, w1, w2, w3, w4t, dense, b1, b2, b3)
    sides = [(i, (i + 1) % reps) for i in range(reps)]
    sides += [(reps + i, reps + (i - 1) % reps) for i in range(reps)]
    side = lax.ppermute(pack, (C, X), sides)
    near = shifted(half, X, 2)
    partial_bags = pl.pallas_call(
        lookup_kernel,
        out_shape=jax.ShapeDtypeStruct((peers * samples, width), F32),
        in_specs=[SM] + [VM] * 3,
        out_specs=VM,
        scratch_shapes=[
            pltpu.VMEM(wanted.shape, jnp.int32),
            pltpu.VMEM(wanted.shape, jnp.int32),
            pltpu.VMEM((512, 2 * tables.shape[0]), BF),
        ],
        compiler_params=params(24),
        cost_estimate=cost(40),
        name="lookup",
    )(meta, wanted, tables, other)
    partial_bags, side = lax.optimization_barrier((partial_bags, side))
    mirror = shifted(side, C, 1)
    far = shifted(near, C, 1)
    bags = lax.all_to_all(
        partial_bags.reshape(peers, samples, width), (Y, Z), 0, 0, tiled=True
    )
    logit = pl.pallas_call(
        top_kernel,
        out_shape=jax.ShapeDtypeStruct((1, samples), F32),
        in_specs=[SM] + [VM] * 8,
        out_specs=VM,
        scratch_shapes=[
            pltpu.VMEM((2, samples, width), BF),
            pltpu.VMEM((reps, samples, w1.shape[1]), BF),
            pltpu.VMEM((reps, samples, w2.shape[1]), BF),
            pltpu.VMEM((reps, samples, w3.shape[1]), BF),
        ],
        compiler_params=params(16),
        cost_estimate=cost(5),
        name="top",
    )(meta, bags, bottom, last.reshape(reps, 1, -1), pack, side, mirror, near, far)
    return logit.reshape(samples)


def solution(mesh):
    torus = Mesh(mesh.devices.reshape(8, 8, 2, mesh.shape["rep"]), ALL)
    in_specs = (
        P((Y, Z, C), None),
        P(ALL, None, None),
        P(ALL, None),
        P(ALL, None),
        P(),
        P(),
        P(),
        P(None, X),
        P(None, X),
        P(None, X),
        P(None, X),
        P(),
    )
    return jax.shard_map(body, mesh=torus, in_specs=in_specs, out_specs=P(ALL), check_vma=False)
```

time: 90.3 us -> 76.5 us (0.85)
  the two profiles are of different devices: /device:TPU:16 before, /device:TPU:1 now
where the time goes in v2:
time: 76.5 us; the launch traced here: 76 us
  starting transfers between devices  50 us (65%)
  waiting for transfers between devices  13.3 us (17%)
  Pallas kernels  10.7 us (14%)
  local copies, waits for them, and re-layouts  1.81 us (2%)
    ppermute x4, starting transfers between devices, shifted(): return lax.ppermute(a, axis, [(i, (i + k) % n) for i in range(n)])  22.5 us
    all_to_all x1, starting transfers between devices, body(): lax.all_to_all(partial_bags.reshape(peers, samples, width), (Y, Z), 0, 0,...  12.1 us
    all_to_all x1, starting transfers between devices, body(): wanted = lax.all_to_all(rows, (Y, Z), 0, 0, tiled=True)  10.9 us
    ppermute x4, waiting for transfers between devices, shifted(): return lax.ppermute(a, axis, [(i, (i + k) % n) for i in range(n)])  7.23 us
    pallas_call x1, Pallas kernels, body(): pl.pallas_call(lookup_kernel, out_shape=jax.ShapeDtypeStruct((peers * sam...  4.99 us
    all_to_all x1, waiting for transfers between devices, body(): wanted = lax.all_to_all(rows, (Y, Z), 0, 0, tiled=True)  4.66 us
    ppermute x1, starting transfers between devices, body(): side = lax.ppermute(pack, (C, X), sides)  4.37 us
    pallas_call x1, Pallas kernels, body(): pl.pallas_call(top_kernel, out_shape=jax.ShapeDtypeStruct((1, samples), F...  3.32 us
  transfers between devices with their start and end apart: 7, of which 4 were waited for; matrix products, arithmetic and copies ran while one was open for 0% of the time, Pallas kernels for 9%

profile of v2, /device:TPU:1, one launch (start us, length us, event | category | flops | bytes accessed | tf_op | source)
XLA Modules:
  0.0 76.0 jit_solution(9749041847662595694)
XLA Ops:
  0.0 0.7 copy-done.9
  0.7 0.8 copy-done.7
  1.5 0.7 prepare.1
  2.2 0.1 pad_add_fusion.meta_ref
  2.3 0.2 copy-done.1
  2.5 8.8 %collective-permute-start = (bf16[2048,128]{1,0:T(8,128)(2,1)S(1)}, bf16[2048,128]{1,0:T(8,128)(2,1)S(1)}, u32[]{:S(2)}, u32[]{:S(2)}) collective-permute-start(bf16[2048,128]{1,0:T(8,128)(2,1)S(1)} %copy-done.1), channel_id=1, source_target_pairs={{0,4},{4,0},{1,5},{5,1},{2,6},{6,2},{3,7},{7,3},{8,12},{12,8},{9,1... | collective-permute-start | bytes 1572872 | tf_op jit(solution)/shard_map/ppermute | solution.py:186
  11.3 0.0 copy-start.10
  11.3 10.9 %all-to-all-start = ((s32[64,1,128]{2,1,0:T(1,128)}), s32[64,1,128]{2,1,0:T(1,128)S(1)}, u32[]{:S(2)}, u32[]{:S(2)}) async-start(s32[64,1,128]{2,1,0:T(1,128)} %bitcast.7), calls=%async_computation | async-start | bytes 65536 | tf_op jit(solution)/shard_map/all_to_all | solution.py:205
  22.3 1.7 %pack.1 = (bf16[2,960,256]{2,1,0:T(8,128)(2,1)S(1)}, bf16[960,256]{1,0:T(8,128)(2,1)}, f32[16,128]{1,0:T(8,128)S(1)}) custom-call(s32[4]{0:T(128)S(1)} %pad_add_fusion.meta_ref, bf16[164,256]{1,0:T(8,128)(2,1)S(1)} %copy-done.4, bf16[1024,256]{1,0:T(8,128)(2,1)S(1)} %copy-done, bf16[1024,128]{1,0:T(8,128)(2,1)S(1)} %copy-done.2, ...), custom_call_target="tpu_custom_call" | custom-call | flops 3000000000 | bytes 1048576 | tf_op jit(solution)/shard_map/pack/pallas_call | solution.py:209
  24.0 4.4 %collective-permute-start.1 = (bf16[2,960,256]{2,1,0:T(8,128)(2,1)S(1)}, bf16[2,960,256]{2,1,0:T(8,128)(2,1)S(1)}, u32[]{:S(2)}, u32[]{:S(2)}) collective-permute-start(bf16[2,960,256]{2,1,0:T(8,128)(2,1)S(1)} %get-tuple-element.16.own_ref), channel_id=1, source_target_pairs={{0,1},{1,2},{2,3},{3,0},{4,7},{5,4},{6,5},{7,6},{8,9},{9,10},{10,1... | collective-permute-start | bytes 2949128 | tf_op jit(solution)/shard_map/ppermute | solution.py:224
  28.4 4.7 %all-to-all-done = s32[64,1,128]{2,1,0:T(1,128)S(1)} async-done(((s32[64,1,128]{2,1,0:T(1,128)}), s32[64,1,128]{2,1,0:T(1,128)S(1)}, u32[]{:S(2)}, u32[]{:S(2)}) %all-to-all-start) | async-done | bytes 32800 | tf_op jit(solution)/shard_map/all_to_all | solution.py:205
  33.1 0.0 collective-permute-done.other_ref
  33.1 5.0 %lookup.1 = f32[1024,128]{1,0:T(8,128)} custom-call(s32[4]{0:T(128)S(1)} %pad_add_fusion.meta_ref, s32[64,128]{1,0:T(8,128)S(1)} %bitcast.13, bf16[2048,128]{1,0:T(8,128)(2,1)S(1)} %copy-done.1, bf16[2048,128]{1,0:T(8,128)(2,1)S(1)} %collective-permute-done.other_ref), custom_call_target="tpu_custom_call" | custom-call | flops 40000000000 | bytes 1048576 | tf_op jit(solution)/shard_map/lookup/pallas_call | solution.py:226
  38.1 1.4 %collective-permute-done.1.side_ref = bf16[2,960,256]{2,1,0:T(8,128)(2,1)S(1)} collective-permute-done((bf16[2,960,256]{2,1,0:T(8,128)(2,1)S(1)}, bf16[2,960,256]{2,1,0:T(8,128)(2,1)S(1)}, u32[]{:S(2)}, u32[]{:S(2)}) %collective-permute-start.1) | collective-permute-done | bytes 983072 | tf_op jit(solution)/shard_map/ppermute | solution.py:224
  39.4 12.1 %all-to-all-start.1 = ((f32[64,16,128]{2,1,0:T(8,128)}), f32[64,16,128]{2,1,0:T(8,128)S(1)}, u32[]{:S(2)}, u32[]{:S(2)}) async-start(f32[64,16,128]{2,1,0:T(8,128)} %bitcast.10), calls=%async_computation.1 | async-start | bytes 1048576 | tf_op jit(solution)/shard_map/all_to_all | solution.py:243
  51.6 0.0 copy-start.11
  51.6 4.4 %collective-permute-start.3 = (bf16[960,256]{1,0:T(8,128)(2,1)}, bf16[960,256]{1,0:T(8,128)(2,1)}, u32[]{:S(2)}, u32[]{:S(2)}) collective-permute-start(bf16[960,256]{1,0:T(8,128)(2,1)} %get-tuple-element.20), channel_id=1, source_target_pairs={{0,2},{1,3},{2,0},{3,1},{4,6},{5,7},{6,4},{7,5},{8,10},{9,11},{10,... | collective-permute-start | bytes 1474568 | tf_op jit(solution)/shard_map/ppermute | solution.py:186
  56.0 3.9 %collective-permute-start.2 = (bf16[2,960,256]{2,1,0:T(8,128)(2,1)S(1)}, bf16[2,960,256]{2,1,0:T(8,128)(2,1)S(1)}, u32[]{:S(2)}, u32[]{:S(2)}) collective-permute-start(bf16[2,960,256]{2,1,0:T(8,128)(2,1)S(1)} %collective-permute-done.1.side_ref), channel_id=1, source_target_pairs={{0,4},{4,0},{1,5},{5,1},{2,6},{6,2},{3,7},{7,3},{8,12},{12,8},{9,1... | collective-permute-start | bytes 2949128 | tf_op jit(solution)/shard_map/ppermute | solution.py:186
  59.9 5.5 %collective-permute-done.3.near_ref = bf16[960,256]{1,0:T(8,128)(2,1)} collective-permute-done((bf16[960,256]{1,0:T(8,128)(2,1)}, bf16[960,256]{1,0:T(8,128)(2,1)}, u32[]{:S(2)}, u32[]{:S(2)}) %collective-permute-start.3) | collective-permute-done | bytes 491552 | tf_op jit(solution)/shard_map/ppermute | solution.py:186
  65.4 5.5 %collective-permute-start.4 = (bf16[960,256]{1,0:T(8,128)(2,1)}, bf16[960,256]{1,0:T(8,128)(2,1)}, u32[]{:S(2)}, u32[]{:S(2)}) collective-permute-start(bf16[960,256]{1,0:T(8,128)(2,1)} %collective-permute-done.3.near_ref), channel_id=1, source_target_pairs={{0,4},{4,0},{1,5},{5,1},{2,6},{6,2},{3,7},{7,3},{8,12},{12,8},{9,1... | collective-permute-start | bytes 1474568 | tf_op jit(solution)/shard_map/ppermute | solution.py:186
  70.8 0.1 reshape.14.last_ref
  70.9 1.7 %collective-permute-done.4.far_ref = bf16[960,256]{1,0:T(8,128)(2,1)} collective-permute-done((bf16[960,256]{1,0:T(8,128)(2,1)}, bf16[960,256]{1,0:T(8,128)(2,1)}, u32[]{:S(2)}, u32[]{:S(2)}) %collective-permute-start.4) | collective-permute-done | bytes 491552 | tf_op jit(solution)/shard_map/ppermute | solution.py:186
  72.6 0.0 collective-permute-done.2.mirror_ref
  72.7 3.3 %top.1 = f32[1,16]{1,0:T(1,128)} custom-call(s32[4]{0:T(128)S(1)} %pad_add_fusion.meta_ref, f32[64,16,128]{2,1,0:T(8,128)S(1)} %all-to-all-done.1.bags_ref, f32[16,128]{1,0:T(8,128)S(1)} %get-tuple-element.18.bottom_ref, bf16[4,1,64]{2,1,0:T(2,128)(2,1)S(1)} %reshape.14.last_ref, bf16[2,960,256]{2,1,0:T(8,128)(2,1)S(1)} %get-tuple-element.16.own_ref, ...), custom_call_target="tpu_custom_call" | custom-call | flops 5000000000 | bytes 1048576 | tf_op jit(solution)/shard_map/top/pallas_call | solution.py:246
  (20 shorter events, 0.0 us)
Async XLA Ops:
  0.0 0.7 copy-start.9
  0.7 0.8 copy-start.7
  1.4 1.1 %copy-start.1 = (bf16[2048,128]{1,0:T(8,128)(2,1)S(1)}, bf16[2048,128]{1,0:T(8,128)(2,1)}, u32[]{:S(2)}) copy-start(bf16[2048,128]{1,0:T(8,128)(2,1)} %own_ref) | copy-start | bytes 1572868
  1.4 20.8 %copy-start = (bf16[1024,256]{1,0:T(8,128)(2,1)S(1)}, bf16[1024,256]{1,0:T(8,128)(2,1)}, u32[]{:S(2)}) copy-start(bf16[1024,256]{1,0:T(8,128)(2,1)} %w2_ref.1) | copy-start | bytes 1572868
  1.5 20.8 %copy-start.2 = (bf16[1024,128]{1,0:T(8,128)(2,1)S(1)}, bf16[1024,128]{1,0:T(8,128)(2,1)}, u32[]{:S(2)}) copy-start(bf16[1024,128]{1,0:T(8,128)(2,1)} %w3_ref.1) | copy-start | bytes 786436
  1.5 20.8 %copy-start.3 = (bf16[512,256]{1,0:T(8,128)(2,1)S(1)}, bf16[512,256]{1,0:T(8,128)(2,1)}, u32[]{:S(2)}) copy-start(bf16[512,256]{1,0:T(8,128)(2,1)} %b2_ref.1) | copy-start | bytes 786436
  1.5 20.8 %copy-start.4 = (bf16[164,256]{1,0:T(8,128)(2,1)S(1)}, bf16[164,256]{1,0:T(8,128)(2,1)}, u32[]{:S(2)}) copy-start(bf16[164,256]{1,0:T(8,128)(2,1)} %w1_ref.1) | copy-start | bytes 251908
  1.5 20.8 %copy-start.6 = (bf16[256,128]{1,0:T(8,128)(2,1)S(1)}, bf16[256,128]{1,0:T(8,128)(2,1)}, u32[]{:S(2)}) copy-start(bf16[256,128]{1,0:T(8,128)(2,1)} %b3_ref.1) | copy-start | bytes 196612
  1.5 20.8 %copy-start.8 = (bf16[13,512]{1,0:T(8,128)(2,1)S(1)}, bf16[13,512]{1,0:T(8,128)(2,1)}, u32[]{:S(2)}) copy-start(bf16[13,512]{1,0:T(8,128)(2,1)} %b1_ref.1) | copy-start | bytes 39940
  2.2 20.1 %copy-start.5 = (bf16[512,64]{0,1:T(8,128)(2,1)S(1)}, bf16[512,64]{0,1:T(8,128)(2,1)}, u32[]{:S(2)}) copy-start(bf16[512,64]{0,1:T(8,128)(2,1)} %param.22) | copy-start | bytes 196612
  2.5 30.6 %collective-permute-start = (bf16[2048,128]{1,0:T(8,128)(2,1)S(1)}, bf16[2048,128]{1,0:T(8,128)(2,1)S(1)}, u32[]{:S(2)}, u32[]{:S(2)}) collective-permute-start(bf16[2048,128]{1,0:T(8,128)(2,1)S(1)} %copy-done.1), channel_id=1, source_target_pairs={{0,4},{4,0},{1,5},{5,1},{2,6},{6,2},{3,7},{7,3},{8,12},{12,8},{9,1... | collective-permute-start | bytes 1572872 | tf_op jit(solution)/shard_map/ppermute | solution.py:186
  11.3 11.0 %copy-start.10 = (bf16[16,13]{1,0:T(8,128)(2,1)S(1)}, bf16[16,13]{1,0:T(8,128)(2,1)}, u32[]{:S(2)}) copy-start(bf16[16,13]{1,0:T(8,128)(2,1)} %dense_ref.1) | copy-start | bytes 1252
  11.3 21.8 %all-to-all-start = ((s32[64,1,128]{2,1,0:T(1,128)}), s32[64,1,128]{2,1,0:T(1,128)S(1)}, u32[]{:S(2)}, u32[]{:S(2)}) async-start(s32[64,1,128]{2,1,0:T(1,128)} %bitcast.7), calls=%async_computation | async-start | bytes 65536 | tf_op jit(solution)/shard_map/all_to_all | solution.py:205
  24.0 15.4 %collective-permute-start.1 = (bf16[2,960,256]{2,1,0:T(8,128)(2,1)S(1)}, bf16[2,960,256]{2,1,0:T(8,128)(2,1)S(1)}, u32[]{:S(2)}, u32[]{:S(2)}) collective-permute-start(bf16[2,960,256]{2,1,0:T(8,128)(2,1)S(1)} %get-tuple-element.16.own_ref), channel_id=1, source_target_pairs={{0,1},{1,2},{2,3},{3,0},{4,7},{5,4},{6,5},{7,6},{8,9},{9,10},{10,1... | collective-permute-start | bytes 2949128 | tf_op jit(solution)/shard_map/ppermute | solution.py:224
  39.4 33.2 %all-to-all-start.1 = ((f32[64,16,128]{2,1,0:T(8,128)}), f32[64,16,128]{2,1,0:T(8,128)S(1)}, u32[]{:S(2)}, u32[]{:S(2)}) async-start(f32[64,16,128]{2,1,0:T(8,128)} %bitcast.10), calls=%async_computation.1 | async-start | bytes 1048576 | tf_op jit(solution)/shard_map/all_to_all | solution.py:243
  51.6 19.3 %copy-start.11 = (bf16[256]{0:T(256)(128)(2,1)S(1)}, bf16[256]{0:T(256)(128)(2,1)}, u32[]{:S(2)}) copy-start(bf16[256]{0:T(256)(128)(2,1)} %param.23) | copy-start | bytes 1540
  51.6 13.8 %collective-permute-start.3 = (bf16[960,256]{1,0:T(8,128)(2,1)}, bf16[960,256]{1,0:T(8,128)(2,1)}, u32[]{:S(2)}, u32[]{:S(2)}) collective-permute-start(bf16[960,256]{1,0:T(8,128)(2,1)} %get-tuple-element.20), channel_id=1, source_target_pairs={{0,2},{1,3},{2,0},{3,1},{4,6},{5,7},{6,4},{7,5},{8,10},{9,11},{10,... | collective-permute-start | bytes 1474568 | tf_op jit(solution)/shard_map/ppermute | solution.py:186
  56.0 16.7 %collective-permute-start.2 = (bf16[2,960,256]{2,1,0:T(8,128)(2,1)S(1)}, bf16[2,960,256]{2,1,0:T(8,128)(2,1)S(1)}, u32[]{:S(2)}, u32[]{:S(2)}) collective-permute-start(bf16[2,960,256]{2,1,0:T(8,128)(2,1)S(1)} %collective-permute-done.1.side_ref), channel_id=1, source_target_pairs={{0,4},{4,0},{1,5},{5,1},{2,6},{6,2},{3,7},{7,3},{8,12},{12,8},{9,1... | collective-permute-start | bytes 2949128 | tf_op jit(solution)/shard_map/ppermute | solution.py:186
  65.4 7.3 %collective-permute-start.4 = (bf16[960,256]{1,0:T(8,128)(2,1)}, bf16[960,256]{1,0:T(8,128)(2,1)}, u32[]{:S(2)}, u32[]{:S(2)}) collective-permute-start(bf16[960,256]{1,0:T(8,128)(2,1)} %collective-permute-done.3.near_ref), channel_id=1, source_target_pairs={{0,4},{4,0},{1,5},{5,1},{2,6},{6,2},{3,7},{7,3},{8,12},{12,8},{9,1... | collective-permute-start | bytes 1474568 | tf_op jit(solution)/shard_map/ppermute | solution.py:186

commit v3 on v2

--- a/solution.py
+++ b/solution.py
@@ -184,6 +184,24 @@
 def shifted(a, axis, k):
     n = lax.axis_size(axis)
     return lax.ppermute(a, axis, [(i, (i + k) % n) for i in range(n)])
+
+
+def hold_kernel(in_ref, out_ref):
+    pass
+
+
+def held(a, micros, space):
+    spec = pl.BlockSpec(memory_space=space)
+    return pl.pallas_call(
+        hold_kernel,
+        out_shape=jax.ShapeDtypeStruct(a.shape, a.dtype),
+        in_specs=[spec],
+        out_specs=spec,
+        input_output_aliases={0: 0},
+        compiler_params=params(4),
+        cost_estimate=cost(micros),
+        name="held",
+    )(a)
 
 
 def body(tables, indices, bag_lengths, dense, b1, b2, b3, w1, w2, w3, w4, last):
@@ -215,7 +233,7 @@
         ),
         in_specs=[SM] + [VM] * 8,
         out_specs=(VM, VM, VM),
-        compiler_params=params(12),
+        compiler_params=params(10),
         cost_estimate=cost(3),
         name="pack",
     )(meta, w1, w2, w3, w4t, dense, b1, b2, b3)
@@ -233,11 +251,11 @@
             pltpu.VMEM(wanted.shape, jnp.int32),
             pltpu.VMEM((512, 2 * tables.shape[0]), BF),
         ],
-        compiler_params=params(24),
+        compiler_params=params(14),
         cost_estimate=cost(40),
         name="lookup",
     )(meta, wanted, tables, other)
-    partial_bags, side = lax.optimization_barrier((partial_bags, side))
+    side, near = held(side, 60, pltpu.VMEM), held(near, 60, pl.ANY)
     mirror = shifted(side, C, 1)
     far = shifted(near, C, 1)
     bags = lax.all_to_all(
@@ -254,7 +272,7 @@
             pltpu.VMEM((reps, samples, w2.shape[1]), BF),
             pltpu.VMEM((reps, samples, w3.shape[1]), BF),
         ],
-        compiler_params=params(16),
+        compiler_params=params(10),
         cost_estimate=cost(5),
         name="top",
     )(meta, bags, bottom, last.reshape(reps, 1, -1), pack, side, mirror, near, far)

time: 76.5 us -> 71 us (0.928)
  the two profiles are of different devices: /device:TPU:1 before, /device:TPU:16 now
where the time goes in v3:
time: 71 us; the launch traced here: 70.5 us
  starting transfers between devices  42.7 us (60%)
  waiting for transfers between devices  14.6 us (21%)
  Pallas kernels  11.4 us (16%)
  local copies, waits for them, and re-layouts  1.57 us (2%)
    all_to_all x1, starting transfers between devices, body(): wanted = lax.all_to_all(rows, (Y, Z), 0, 0, tiled=True)  16.5 us
    all_to_all x1, starting transfers between devices, body(): lax.all_to_all(partial_bags.reshape(peers, samples, width), (Y, Z), 0, 0,...  12.4 us
    all_to_all x1, waiting for transfers between devices, body(): lax.all_to_all(partial_bags.reshape(peers, samples, width), (Y, Z), 0, 0,...  11.8 us
    ppermute x4, starting transfers between devices, shifted(): return lax.ppermute(a, axis, [(i, (i + k) % n) for i in range(n)])  10.4 us
    pallas_call x1, Pallas kernels, body(): pl.pallas_call(lookup_kernel, out_shape=jax.ShapeDtypeStruct((peers * sam...  5.62 us
    ppermute x1, starting transfers between devices, body(): side = lax.ppermute(pack, (C, X), sides)  3.39 us
    pallas_call x1, Pallas kernels, body(): pl.pallas_call(top_kernel, out_shape=jax.ShapeDtypeStruct((1, samples), F...  3.32 us
    ppermute x4, waiting for transfers between devices, shifted(): return lax.ppermute(a, axis, [(i, (i + k) % n) for i in range(n)])  2.47 us
  transfers between devices with their start and end apart: 7, of which 4 were waited for; matrix products, arithmetic and copies ran while one was open for 0% of the time, Pallas kernels for 10%

profile of v3, /device:TPU:16, one launch (start us, length us, event | category | flops | bytes accessed | tf_op | source)
XLA Modules:
  0.0 70.5 jit_solution(18411652050131770205)
XLA Ops:
  0.0 0.7 copy-done.8
  0.7 0.8 %copy-done.6 = s32[16,8,8]{0,2,1:T(8,128)S(1)} copy-done((s32[16,8,8]{0,2,1:T(8,128)S(1)}, s32[16,8,8]{0,2,1:T(8,128)}, u32[]{:S(2)}) %copy-start.6) | copy-done | bytes 4120
  1.5 0.7 prepare.1
  2.2 0.1 pad_add_fusion.meta_ref
  2.3 1.9 %collective-permute-start = (bf16[2048,128]{1,0:T(8,128)(2,1)}, bf16[2048,128]{1,0:T(8,128)(2,1)}, u32[]{:S(2)}, u32[]{:S(2)}) collective-permute-start(bf16[2048,128]{1,0:T(8,128)(2,1)} %own_ref), channel_id=1, source_target_pairs={{0,4},{4,0},{1,5},{5,1},{2,6},{6,2},{3,7},{7,3},{8,12},{12,8},{9,1... | collective-permute-start | bytes 1572872 | tf_op jit(solution)/shard_map/ppermute | solution.py:186
  4.2 0.0 copy-start.9
  4.2 16.5 %all-to-all-start = ((s32[64,1,128]{2,1,0:T(1,128)}), s32[64,1,128]{2,1,0:T(1,128)S(1)}, u32[]{:S(2)}, u32[]{:S(2)}) async-start(s32[64,1,128]{2,1,0:T(1,128)} %bitcast.7), calls=%async_computation | async-start | bytes 65536 | tf_op jit(solution)/shard_map/all_to_all | solution.py:223
  20.8 1.7 %pack.1 = (bf16[2,960,256]{2,1,0:T(8,128)(2,1)S(1)}, bf16[960,256]{1,0:T(8,128)(2,1)}, f32[16,128]{1,0:T(8,128)S(1)}) custom-call(s32[4]{0:T(128)S(1)} %pad_add_fusion.meta_ref, bf16[164,256]{1,0:T(8,128)(2,1)S(1)} %copy-done.3, bf16[1024,256]{1,0:T(8,128)(2,1)S(1)} %copy-done, bf16[1024,128]{1,0:T(8,128)(2,1)S(1)} %copy-done.1, ...), custom_call_target="tpu_custom_call" | custom-call | flops 3000000000 | bytes 1048576 | tf_op jit(solution)/shard_map/pack/pallas_call | solution.py:227
  22.5 3.4 %collective-permute-start.1 = (bf16[2,960,256]{2,1,0:T(8,128)(2,1)S(1)}, bf16[2,960,256]{2,1,0:T(8,128)(2,1)S(1)}, u32[]{:S(2)}, u32[]{:S(2)}) collective-permute-start(bf16[2,960,256]{2,1,0:T(8,128)(2,1)S(1)} %get-tuple-element.15.own_ref), channel_id=1, source_target_pairs={{0,1},{1,2},{2,3},{3,0},{4,7},{5,4},{6,5},{7,6},{8,9},{9,10},{10,1... | collective-permute-start | bytes 2949128 | tf_op jit(solution)/shard_map/ppermute | solution.py:242
  25.9 4.6 %collective-permute-start.3 = (bf16[960,256]{1,0:T(8,128)(2,1)}, bf16[960,256]{1,0:T(8,128)(2,1)}, u32[]{:S(2)}, u32[]{:S(2)}) collective-permute-start(bf16[960,256]{1,0:T(8,128)(2,1)} %get-tuple-element.16), channel_id=1, source_target_pairs={{0,2},{1,3},{2,0},{3,1},{4,6},{5,7},{6,4},{7,5},{8,10},{9,11},{10,... | collective-permute-start | bytes 1474568 | tf_op jit(solution)/shard_map/ppermute | solution.py:186
  30.5 0.3 all-to-all-done
  30.9 0.0 collective-permute-done.other_ref
  30.9 5.6 %lookup.1 = f32[1024,128]{1,0:T(8,128)} custom-call(s32[4]{0:T(128)S(1)} %pad_add_fusion.meta_ref, s32[64,128]{1,0:T(8,128)S(1)} %bitcast.13, bf16[2048,128]{1,0:T(8,128)(2,1)} %own_ref, bf16[2048,128]{1,0:T(8,128)(2,1)} %collective-permute-done.other_ref), custom_call_target="tpu_custom_call" | custom-call | flops 40000000000 | bytes 1048576 | tf_op jit(solution)/shard_map/lookup/pallas_call | solution.py:244
  36.5 12.4 %all-to-all-start.1 = ((f32[64,16,128]{2,1,0:T(8,128)}), f32[64,16,128]{2,1,0:T(8,128)S(1)}, u32[]{:S(2)}, u32[]{:S(2)}) async-start(f32[64,16,128]{2,1,0:T(8,128)} %bitcast.9), calls=%async_computation.1 | async-start | bytes 1048576 | tf_op jit(solution)/shard_map/all_to_all | solution.py:261
  48.9 0.0 collective-permute-done.1.in_ref
  48.9 0.0 copy-start.10
  48.9 1.9 %collective-permute-start.2 = (bf16[2,960,256]{2,1,0:T(8,128)(2,1)S(1)}, bf16[2,960,256]{2,1,0:T(8,128)(2,1)S(1)}, u32[]{:S(2)}, u32[]{:S(2)}) collective-permute-start(bf16[2,960,256]{2,1,0:T(8,128)(2,1)S(1)} %held.2.side_ref), channel_id=1, source_target_pairs={{0,4},{4,0},{1,5},{5,1},{2,6},{6,2},{3,7},{7,3},{8,12},{12,8},{9,1... | collective-permute-start | bytes 2949128 | tf_op jit(solution)/shard_map/ppermute | solution.py:186
  50.8 0.5 collective-permute-done.3.in_ref
  51.3 2.0 %collective-permute-start.4 = (bf16[960,256]{1,0:T(8,128)(2,1)}, bf16[960,256]{1,0:T(8,128)(2,1)}, u32[]{:S(2)}, u32[]{:S(2)}) collective-permute-start(bf16[960,256]{1,0:T(8,128)(2,1)} %held.3.near_ref), channel_id=1, source_target_pairs={{0,4},{4,0},{1,5},{5,1},{2,6},{6,2},{3,7},{7,3},{8,12},{12,8},{9,1... | collective-permute-start | bytes 1474568 | tf_op jit(solution)/shard_map/ppermute | solution.py:186
  53.3 0.1 reshape.14.last_ref
  53.4 2.0 %collective-permute-done.4.far_ref = bf16[960,256]{1,0:T(8,128)(2,1)} collective-permute-done((bf16[960,256]{1,0:T(8,128)(2,1)}, bf16[960,256]{1,0:T(8,128)(2,1)}, u32[]{:S(2)}, u32[]{:S(2)}) %collective-permute-start.4) | collective-permute-done | bytes 491552 | tf_op jit(solution)/shard_map/ppermute | solution.py:186
  55.4 11.8 %all-to-all-done.1.bags_ref = f32[64,16,128]{2,1,0:T(8,128)S(1)} async-done(((f32[64,16,128]{2,1,0:T(8,128)}), f32[64,16,128]{2,1,0:T(8,128)S(1)}, u32[]{:S(2)}, u32[]{:S(2)}) %all-to-all-start.1) | async-done | bytes 524320 | tf_op jit(solution)/shard_map/all_to_all | solution.py:261
  67.2 0.0 collective-permute-done.2.mirror_ref
  67.2 3.3 %top.1 = f32[1,16]{1,0:T(1,128)} custom-call(s32[4]{0:T(128)S(1)} %pad_add_fusion.meta_ref, f32[64,16,128]{2,1,0:T(8,128)S(1)} %all-to-all-done.1.bags_ref, f32[16,128]{1,0:T(8,128)S(1)} %get-tuple-element.14.bottom_ref, bf16[4,1,64]{2,1,0:T(2,128)(2,1)S(1)} %reshape.14.last_ref, bf16[2,960,256]{2,1,0:T(8,128)(2,1)S(1)} %get-tuple-element.15.own_ref, ...), custom_call_target="tpu_custom_call" | custom-call | flops 5000000000 | bytes 1048576 | tf_op jit(solution)/shard_map/top/pallas_call | solution.py:264
  (20 shorter events, 0.0 us)
Async XLA Ops:
  0.0 0.7 copy-start.8
  0.7 0.8 %copy-start.6 = (s32[16,8,8]{0,2,1:T(8,128)S(1)}, s32[16,8,8]{0,2,1:T(8,128)}, u32[]{:S(2)}) copy-start(s32[16,8,8]{0,2,1:T(8,128)} %param.13) | copy-start | bytes 12292
  1.4 19.2 %copy-start = (bf16[1024,256]{1,0:T(8,128)(2,1)S(1)}, bf16[1024,256]{1,0:T(8,128)(2,1)}, u32[]{:S(2)}) copy-start(bf16[1024,256]{1,0:T(8,128)(2,1)} %w2_ref.1) | copy-start | bytes 1572868
  1.4 19.2 %copy-start.1 = (bf16[1024,128]{1,0:T(8,128)(2,1)S(1)}, bf16[1024,128]{1,0:T(8,128)(2,1)}, u32[]{:S(2)}) copy-start(bf16[1024,128]{1,0:T(8,128)(2,1)} %w3_ref.1) | copy-start | bytes 786436
  1.5 19.3 %copy-start.2 = (bf16[512,256]{1,0:T(8,128)(2,1)S(1)}, bf16[512,256]{1,0:T(8,128)(2,1)}, u32[]{:S(2)}) copy-start(bf16[512,256]{1,0:T(8,128)(2,1)} %b2_ref.1) | copy-start | bytes 786436
  1.5 19.3 %copy-start.3 = (bf16[164,256]{1,0:T(8,128)(2,1)S(1)}, bf16[164,256]{1,0:T(8,128)(2,1)}, u32[]{:S(2)}) copy-start(bf16[164,256]{1,0:T(8,128)(2,1)} %w1_ref.1) | copy-start | bytes 251908
  1.5 19.3 %copy-start.5 = (bf16[256,128]{1,0:T(8,128)(2,1)S(1)}, bf16[256,128]{1,0:T(8,128)(2,1)}, u32[]{:S(2)}) copy-start(bf16[256,128]{1,0:T(8,128)(2,1)} %b3_ref.1) | copy-start | bytes 196612
  1.5 19.3 %copy-start.7 = (bf16[13,512]{1,0:T(8,128)(2,1)S(1)}, bf16[13,512]{1,0:T(8,128)(2,1)}, u32[]{:S(2)}) copy-start(bf16[13,512]{1,0:T(8,128)(2,1)} %b1_ref.1) | copy-start | bytes 39940
  2.2 18.6 %copy-start.4 = (bf16[512,64]{0,1:T(8,128)(2,1)S(1)}, bf16[512,64]{0,1:T(8,128)(2,1)}, u32[]{:S(2)}) copy-start(bf16[512,64]{0,1:T(8,128)(2,1)} %param.22) | copy-start | bytes 196612
  2.3 28.6 %collective-permute-start = (bf16[2048,128]{1,0:T(8,128)(2,1)}, bf16[2048,128]{1,0:T(8,128)(2,1)}, u32[]{:S(2)}, u32[]{:S(2)}) collective-permute-start(bf16[2048,128]{1,0:T(8,128)(2,1)} %own_ref), channel_id=1, source_target_pairs={{0,4},{4,0},{1,5},{5,1},{2,6},{6,2},{3,7},{7,3},{8,12},{12,8},{9,1... | collective-permute-start | bytes 1572872 | tf_op jit(solution)/shard_map/ppermute | solution.py:186
  4.2 16.6 %copy-start.9 = (bf16[16,13]{1,0:T(8,128)(2,1)S(1)}, bf16[16,13]{1,0:T(8,128)(2,1)}, u32[]{:S(2)}) copy-start(bf16[16,13]{1,0:T(8,128)(2,1)} %dense_ref.1) | copy-start | bytes 1252
  4.2 26.7 %all-to-all-start = ((s32[64,1,128]{2,1,0:T(1,128)}), s32[64,1,128]{2,1,0:T(1,128)S(1)}, u32[]{:S(2)}, u32[]{:S(2)}) async-start(s32[64,1,128]{2,1,0:T(1,128)} %bitcast.7), calls=%async_computation | async-start | bytes 65536 | tf_op jit(solution)/shard_map/all_to_all | solution.py:223
  22.5 26.4 %collective-permute-start.1 = (bf16[2,960,256]{2,1,0:T(8,128)(2,1)S(1)}, bf16[2,960,256]{2,1,0:T(8,128)(2,1)S(1)}, u32[]{:S(2)}, u32[]{:S(2)}) collective-permute-start(bf16[2,960,256]{2,1,0:T(8,128)(2,1)S(1)} %get-tuple-element.15.own_ref), channel_id=1, source_target_pairs={{0,1},{1,2},{2,3},{3,0},{4,7},{5,4},{6,5},{7,6},{8,9},{9,10},{10,1... | collective-permute-start | bytes 2949128 | tf_op jit(solution)/shard_map/ppermute | solution.py:242
  25.9 25.4 %collective-permute-start.3 = (bf16[960,256]{1,0:T(8,128)(2,1)}, bf16[960,256]{1,0:T(8,128)(2,1)}, u32[]{:S(2)}, u32[]{:S(2)}) collective-permute-start(bf16[960,256]{1,0:T(8,128)(2,1)} %get-tuple-element.16), channel_id=1, source_target_pairs={{0,2},{1,3},{2,0},{3,1},{4,6},{5,7},{6,4},{7,5},{8,10},{9,11},{10,... | collective-permute-start | bytes 1474568 | tf_op jit(solution)/shard_map/ppermute | solution.py:186
  36.5 30.7 %all-to-all-start.1 = ((f32[64,16,128]{2,1,0:T(8,128)}), f32[64,16,128]{2,1,0:T(8,128)S(1)}, u32[]{:S(2)}, u32[]{:S(2)}) async-start(f32[64,16,128]{2,1,0:T(8,128)} %bitcast.9), calls=%async_computation.1 | async-start | bytes 1048576 | tf_op jit(solution)/shard_map/all_to_all | solution.py:261
  48.9 4.4 %copy-start.10 = (bf16[256]{0:T(256)(128)(2,1)S(1)}, bf16[256]{0:T(256)(128)(2,1)}, u32[]{:S(2)}) copy-start(bf16[256]{0:T(256)(128)(2,1)} %param.23) | copy-start | bytes 1540
  48.9 18.3 %collective-permute-start.2 = (bf16[2,960,256]{2,1,0:T(8,128)(2,1)S(1)}, bf16[2,960,256]{2,1,0:T(8,128)(2,1)S(1)}, u32[]{:S(2)}, u32[]{:S(2)}) collective-permute-start(bf16[2,960,256]{2,1,0:T(8,128)(2,1)S(1)} %held.2.side_ref), channel_id=1, source_target_pairs={{0,4},{4,0},{1,5},{5,1},{2,6},{6,2},{3,7},{7,3},{8,12},{12,8},{9,1... | collective-permute-start | bytes 2949128 | tf_op jit(solution)/shard_map/ppermute | solution.py:186
  51.3 4.1 %collective-permute-start.4 = (bf16[960,256]{1,0:T(8,128)(2,1)}, bf16[960,256]{1,0:T(8,128)(2,1)}, u32[]{:S(2)}, u32[]{:S(2)}) collective-permute-start(bf16[960,256]{1,0:T(8,128)(2,1)} %held.3.near_ref), channel_id=1, source_target_pairs={{0,4},{4,0},{1,5},{5,1},{2,6},{6,2},{3,7},{7,3},{8,12},{12,8},{9,1... | collective-permute-start | bytes 1474568 | tf_op jit(solution)/shard_map/ppermute | solution.py:186

commit v4 on v3

--- a/solution.py
+++ b/solution.py
@@ -10,8 +10,8 @@
 
 TAB = 8
 HOT = 8
-Y, Z, C, X = "y", "z", "c", "x"
-ALL = (Y, Z, C, X)
+Y, Z, N, C, X = "y", "z", "n", "c", "x"
+ALL = (Y, Z, N, C, X)
 LO = 256
 HEAD_ROWS = 128
 BF = jnp.bfloat16
@@ -42,7 +42,15 @@
     return pltpu.CompilerParams(vmem_limit_bytes=mib << 20)
 
 
-def prepare_kernel(peers, idx_ref, len_ref, out_ref):
+def prepare_kernel(peers, idx_hbm, len_hbm, out_ref, idx_ref, len_ref, sem):
+    copies = [
+        pltpu.make_async_copy(idx_hbm, idx_ref, sem.at[0]),
+        pltpu.make_async_copy(len_hbm, len_ref, sem.at[1]),
+    ]
+    for copy in copies:
+        copy.start()
+    for copy in copies:
+        copy.wait()
     lens = len_ref[...]
     parts = [jnp.where(lens > h, idx_ref[:, h, :], -1) for h in range(HOT)]
     rows = jnp.concatenate(parts, axis=1)
@@ -55,7 +63,7 @@
 def pack_kernel(
     meta_ref, w1_ref, w2_ref, w3_ref, w4_ref, dense_ref, b1_ref, b2_ref, b3_ref, pack_ref, half_ref, bottom_ref
 ):
-    core = meta_ref[2]
+    core = meta_ref[3]
     tail = w1_ref[HEAD_ROWS:, :]
     pack_ref[0, 0:HEAD_ROWS, :] = w1_ref[0:HEAD_ROWS, :]
     pack_ref[1, 0:HEAD_ROWS, :] = jnp.concatenate(
@@ -80,18 +88,18 @@
     bottom_ref[...] = relu(mm(middle, b3_ref[...]))
 
 
-def lookup_kernel(meta_ref, idx_ref, own_ref, other_ref, out_ref, code_ref, lo_ref, count_ref):
+def lookup_kernel(meta_ref, idx_ref, same_ref, other_ref, out_ref, code_ref, lo_ref, count_ref):
     peers, width = idx_ref.shape
     bags = width // HOT
-    span = own_ref.shape[0]
-    held = 2 * span
+    near, span = same_ref.shape[0], same_ref.shape[1]
+    held = 2 * near * span
     his = held // LO
     rows = count_ref.shape[0]
     per_chunk = rows // bags
-    z, core = meta_ref[1], meta_ref[2]
+    z, n, core = meta_ref[1], meta_ref[2], meta_ref[3]
     rel = idx_ref[...] - z * held
     valid = (rel >= 0) & (rel < held)
-    rel = rel ^ (core * span)
+    rel = rel ^ ((n * 2 + core) * span)
     bag = lax.broadcasted_iota(jnp.int32, (peers, width), 1) % bags
     code_ref[...] = jnp.where(valid, (rel // LO) * bags + bag, -1)
     lo_ref[...] = rel % LO
@@ -111,7 +119,8 @@
                 count_ref[g * bags : (g + 1) * bags, hi * LO : (hi + 1) * LO] = counts[
                     hi * bags : (hi + 1) * bags
                 ]
-        total = mm(count_ref[:, :span], own_ref[...]) + mm(count_ref[:, span:], other_ref[...])
+        blocks = [ref[k] for k in range(near) for ref in (same_ref, other_ref)]
+        total = sum(mm(count_ref[:, k * span : (k + 1) * span], b) for k, b in enumerate(blocks))
         out_ref[pl.ds(pl.multiple_of(chunk * rows, rows), rows), :] = total
 
 
@@ -119,7 +128,7 @@
     meta_ref, bags_ref, bottom_ref, last_ref, own_ref, side_ref, mirror_ref, near_ref, far_ref,
     out_ref, in_ref, a1_ref, a2_ref, a3_ref,
 ):
-    core, x = meta_ref[2], meta_ref[3]
+    core, x = meta_ref[3], meta_ref[4]
     reps = last_ref.shape[0]
     peers = bags_ref.shape[0] // TAB
     bottom = bottom_ref[...]
@@ -208,20 +217,27 @@
     samples, width = indices.shape[0], tables.shape[1]
     reps = lax.axis_size(X)
     along_z = lax.axis_size(Z)
+    pair = lax.axis_size(N)
     peers = lax.axis_size((Y, Z))
     meta = jnp.stack([lax.axis_index(a) for a in ALL]).astype(jnp.int32)
     rows = pl.pallas_call(
         functools.partial(prepare_kernel, along_z),
         out_shape=jax.ShapeDtypeStruct((peers, HOT * samples), jnp.int32),
-        in_specs=[VM] * 2,
+        in_specs=[pl.BlockSpec(memory_space=pl.ANY)] * 2,
         out_specs=VM,
+        scratch_shapes=[
+            pltpu.VMEM((TAB, HOT, samples), jnp.int32),
+            pltpu.VMEM((TAB, samples), jnp.int32),
+            pltpu.SemaphoreType.DMA((2,)),
+        ],
         compiler_params=params(8),
         cost_estimate=cost(1),
         name="prepare",
     )(jnp.transpose(indices, (1, 2, 0)), jnp.transpose(bag_lengths))
     rows, tables, meta = lax.optimization_barrier((rows, tables, meta))
     wanted = lax.all_to_all(rows, (Y, Z), 0, 0, tiled=True)
-    other = shifted(tables, C, 1)
+    wanted = held(wanted, 60, pltpu.VMEM)
+    beside = shifted(tables, N, 1)
     w4t = jnp.transpose(w4)
     pack_rows = HEAD_ROWS + w2.shape[0] // 2 + w3.shape[0] // 4 + w4t.shape[0]
     pack, half, bottom = pl.pallas_call(
@@ -239,6 +255,9 @@
     )(meta, w1, w2, w3, w4t, dense, b1, b2, b3)
     sides = [(i, (i + 1) % reps) for i in range(reps)]
     sides += [(reps + i, reps + (i - 1) % reps) for i in range(reps)]
+    beside, bottom = lax.optimization_barrier((beside, bottom))
+    same = jnp.stack([tables, beside])
+    other = shifted(same, C, 1)
     side = lax.ppermute(pack, (C, X), sides)
     near = shifted(half, X, 2)
     partial_bags = pl.pallas_call(
@@ -249,13 +268,16 @@
         scratch_shapes=[
             pltpu.VMEM(wanted.shape, jnp.int32),
             pltpu.VMEM(wanted.shape, jnp.int32),
-            pltpu.VMEM((512, 2 * tables.shape[0]), BF),
+            pltpu.VMEM((256, 2 * pair * tables.shape[0]), BF),
         ],
         compiler_params=params(14),
         cost_estimate=cost(40),
         name="lookup",
-    )(meta, wanted, tables, other)
-    side, near = held(side, 60, pltpu.VMEM), held(near, 60, pl.ANY)
+    )(meta, wanted, same, other)
+    side, _ = lax.optimization_barrier((side, partial_bags))
+    side = held(side, 60, pl.ANY)
+    near, _ = lax.optimization_barrier((near, side))
+    near = held(near, 60, pl.ANY)
     mirror = shifted(side, C, 1)
     far = shifted(near, C, 1)
     bags = lax.all_to_all(
@@ -280,9 +302,9 @@
 
 
 def solution(mesh):
-    torus = Mesh(mesh.devices.reshape(8, 8, 2, mesh.shape["rep"]), ALL)
+    torus = Mesh(mesh.devices.reshape(8, 4, 2, 2, mesh.shape["rep"]), ALL)
     in_specs = (
-        P((Y, Z, C), None),
+        P((Y, Z, N, C), None),
         P(ALL, None, None),
         P(ALL, None),
         P(ALL, None),

time: 71 us -> 73.6 us (1.037)
  the two profiles are of different devices: /device:TPU:16 before, /device:TPU:8 now
where the time goes in v4:
time: 73.6 us; the launch traced here: 73 us
  starting transfers between devices  46 us (63%)
  waiting for transfers between devices  13 us (18%)
  Pallas kernels  10.9 us (15%)
  local copies, waits for them, and re-layouts  1.81 us (2%)
  other arithmetic  1.14 us (2%)
    all_to_all x1, starting transfers between devices, body(): wanted = lax.all_to_all(rows, (Y, Z), 0, 0, tiled=True)  15.3 us
    ppermute x5, starting transfers between devices, shifted(): return lax.ppermute(a, axis, [(i, (i + k) % n) for i in range(n)])  15.2 us
    all_to_all x1, starting transfers between devices, body(): lax.all_to_all(partial_bags.reshape(peers, samples, width), (Y, Z), 0, 0,...  12.2 us
    all_to_all x1, waiting for transfers between devices, body(): lax.all_to_all(partial_bags.reshape(peers, samples, width), (Y, Z), 0, 0,...  8.75 us
    pallas_call x1, Pallas kernels, body(): pl.pallas_call(lookup_kernel, out_shape=jax.ShapeDtypeStruct((peers * sam...  4.92 us
    ppermute x5, waiting for transfers between devices, shifted(): return lax.ppermute(a, axis, [(i, (i + k) % n) for i in range(n)])  4.2 us
    pallas_call x1, Pallas kernels, body(): pl.pallas_call(top_kernel, out_shape=jax.ShapeDtypeStruct((1, samples), F...  3.46 us
    ppermute x1, starting transfers between devices, body(): side = lax.ppermute(pack, (C, X), sides)  3.39 us
  transfers between devices with their start and end apart: 8, of which 3 were waited for; matrix products, arithmetic and copies ran while one was open for 2% of the time, Pallas kernels for 9%

profile of v4, /device:TPU:8, one launch (start us, length us, event | category | flops | bytes accessed | tf_op | source)
XLA Modules:
  0.0 73.0 jit_solution(15650847981944832531)
XLA Ops:
  0.0 0.8 %copy-done.6 = s32[16,8,8]{0,2,1:T(8,128)S(1)} copy-done((s32[16,8,8]{0,2,1:T(8,128)S(1)}, s32[16,8,8]{0,2,1:T(8,128)}, u32[]{:S(2)}) %copy-start.6) | copy-done | bytes 4120
  0.8 0.7 copy-done.8
  1.5 0.8 %prepare.1 = s32[32,128]{1,0:T(8,128)} custom-call(s32[8,8,16]{2,1,0:T(8,128)S(1)} %bitcast.18, s32[8,16]{1,0:T(8,128)S(1)} %bitcast.19), custom_call_target="tpu_custom_call" | custom-call | flops 1000000000 | bytes 1048576 | tf_op jit(solution)/shard_map/prepare/pallas_call | solution.py:223
  2.2 0.1 stack.32.meta_ref
  2.3 0.2 copy-done.10
  2.5 4.3 %collective-permute-start = (bf16[2048,128]{1,0:T(8,128)(2,1)S(1)}, bf16[2048,128]{1,0:T(8,128)(2,1)}, u32[]{:S(2)}, u32[]{:S(2)}) collective-permute-start(bf16[2048,128]{1,0:T(8,128)(2,1)S(1)} %copy-done.10), channel_id=1, source_target_pairs={{0,8},{8,0},{1,9},{9,1},{2,10},{10,2},{3,11},{11,3},{4,12},{12,4},... | collective-permute-start | bytes 1572872 | tf_op jit(solution)/shard_map/ppermute | solution.py:195
  6.8 0.0 copy-start.7
  6.8 0.0 copy-start.9
  6.8 15.3 %all-to-all-start = ((s32[32,1,128]{2,1,0:T(1,128)}), s32[32,1,128]{2,1,0:T(1,128)S(1)}, u32[]{:S(2)}, u32[]{:S(2)}) async-start(s32[32,1,128]{2,1,0:T(1,128)} %bitcast.8), calls=%async_computation | async-start | bytes 32768 | tf_op jit(solution)/shard_map/all_to_all | solution.py:238
  22.2 1.7 %pack.1 = (bf16[2,960,256]{2,1,0:T(8,128)(2,1)S(1)}, bf16[960,256]{1,0:T(8,128)(2,1)}, f32[16,128]{1,0:T(8,128)S(1)}) custom-call(s32[5]{0:T(128)S(1)} %stack.32.meta_ref, bf16[164,256]{1,0:T(8,128)(2,1)S(1)} %copy-done.3, bf16[1024,256]{1,0:T(8,128)(2,1)S(1)} %copy-done, bf16[1024,128]{1,0:T(8,128)(2,1)S(1)} %copy-done.1, bf16[64,512]{1,0:T(8,128)(2,1)S(1)} %bitcast.17, ...), custom_call_target="tpu_custom_call" | custom-call | flops 3000000000 | bytes 1048576 | tf_op jit(solution)/shard_map/pack/pallas_call | solution.py:243
  23.9 3.4 %collective-permute-start.2 = (bf16[2,960,256]{2,1,0:T(8,128)(2,1)S(1)}, bf16[2,960,256]{2,1,0:T(8,128)(2,1)}, u32[]{:S(2)}, u32[]{:S(2)}) collective-permute-start(bf16[2,960,256]{2,1,0:T(8,128)(2,1)S(1)} %get-tuple-element.21.own_ref), channel_id=1, source_target_pairs={{0,1},{1,2},{2,3},{3,0},{4,7},{5,4},{6,5},{7,6},{8,9},{9,10},{10,1... | collective-permute-start | bytes 2949128 | tf_op jit(solution)/shard_map/ppermute | solution.py:261
  27.3 4.6 %collective-permute-start.4 = (bf16[960,256]{1,0:T(8,128)(2,1)}, bf16[960,256]{1,0:T(8,128)(2,1)}, u32[]{:S(2)}, u32[]{:S(2)}) collective-permute-start(bf16[960,256]{1,0:T(8,128)(2,1)} %get-tuple-element.23), channel_id=1, source_target_pairs={{0,2},{1,3},{2,0},{3,1},{4,6},{5,7},{6,4},{7,5},{8,10},{9,11},{10,... | collective-permute-start | bytes 1474568 | tf_op jit(solution)/shard_map/ppermute | solution.py:195
  31.9 1.1 %pad_maximum_fusion.same_ref = bf16[2,2048,128]{2,1,0:T(8,128)(2,1)S(1)} fusion(bf16[1,2048,128]{2,1,0:T(8,128)(2,1)} %bitcast.12, bf16[1,2048,128]{2,1,0:T(8,128)(2,1)S(1)} %bitcast.20), kind=kLoop, calls=%fused_computation | loop fusion | flops 524288 | bytes 2097152 | tf_op jit(solution)/shard_map/stack | solution.py:259
  33.1 1.9 %collective-permute-start.1 = (bf16[2,2048,128]{2,1,0:T(8,128)(2,1)S(1)}, bf16[2,2048,128]{2,1,0:T(8,128)(2,1)S(1)}, u32[]{:S(2)}, u32[]{:S(2)}) collective-permute-start(bf16[2,2048,128]{2,1,0:T(8,128)(2,1)S(1)} %pad_maximum_fusion.same_ref), channel_id=1, source_target_pairs={{0,4},{4,0},{1,5},{5,1},{2,6},{6,2},{3,7},{7,3},{8,12},{12,8},{9,1... | collective-permute-start | bytes 3145736 | tf_op jit(solution)/shard_map/ppermute | solution.py:195
  35.0 2.6 %collective-permute-done.1.other_ref = bf16[2,2048,128]{2,1,0:T(8,128)(2,1)S(1)} collective-permute-done((bf16[2,2048,128]{2,1,0:T(8,128)(2,1)S(1)}, bf16[2,2048,128]{2,1,0:T(8,128)(2,1)S(1)}, u32[]{:S(2)}, u32[]{:S(2)}) %collective-permute-start.1) | collective-permute-done | bytes 1048608 | tf_op jit(solution)/shard_map/ppermute | solution.py:195
  37.6 4.9 %lookup.1 = f32[512,128]{1,0:T(8,128)} custom-call(s32[5]{0:T(128)S(1)} %stack.32.meta_ref, s32[32,128]{1,0:T(8,128)S(1)} %held.3.idx_ref, bf16[2,2048,128]{2,1,0:T(8,128)(2,1)S(1)} %pad_maximum_fusion.same_ref, bf16[2,2048,128]{2,1,0:T(8,128)(2,1)S(1)} %collective-permute-done.1.other_ref), custom_call_target="tpu_custom_call" | custom-call | flops 40000000000 | bytes 1048576 | tf_op jit(solution)/shard_map/lookup/pallas_call | solution.py:263
  42.6 12.2 %all-to-all-start.1 = ((f32[32,16,128]{2,1,0:T(8,128)}), f32[32,16,128]{2,1,0:T(8,128)S(1)}, u32[]{:S(2)}, u32[]{:S(2)}) async-start(f32[32,16,128]{2,1,0:T(8,128)} %bitcast.13), calls=%async_computation.1 | async-start | bytes 524288 | tf_op jit(solution)/shard_map/all_to_all | solution.py:283
  54.8 0.0 copy-start.11
  54.8 1.9 %collective-permute-start.3 = (bf16[2,960,256]{2,1,0:T(8,128)(2,1)}, bf16[2,960,256]{2,1,0:T(8,128)(2,1)S(1)}, u32[]{:S(2)}, u32[]{:S(2)}) collective-permute-start(bf16[2,960,256]{2,1,0:T(8,128)(2,1)} %held.4.side_ref), channel_id=1, source_target_pairs={{0,4},{4,0},{1,5},{5,1},{2,6},{6,2},{3,7},{7,3},{8,12},{12,8},{9,1... | collective-permute-start | bytes 2949128 | tf_op jit(solution)/shard_map/ppermute | solution.py:195
  56.7 2.4 %collective-permute-start.5 = (bf16[960,256]{1,0:T(8,128)(2,1)}, bf16[960,256]{1,0:T(8,128)(2,1)S(1)}, u32[]{:S(2)}, u32[]{:S(2)}) collective-permute-start(bf16[960,256]{1,0:T(8,128)(2,1)} %held.5.near_ref), channel_id=1, source_target_pairs={{0,4},{4,0},{1,5},{5,1},{2,6},{6,2},{3,7},{7,3},{8,12},{12,8},{9,1... | collective-permute-start | bytes 1474568 | tf_op jit(solution)/shard_map/ppermute | solution.py:195
  59.1 0.1 reshape.14.last_ref
  59.2 1.6 %collective-permute-done.5.far_ref = bf16[960,256]{1,0:T(8,128)(2,1)S(1)} collective-permute-done((bf16[960,256]{1,0:T(8,128)(2,1)}, bf16[960,256]{1,0:T(8,128)(2,1)S(1)}, u32[]{:S(2)}, u32[]{:S(2)}) %collective-permute-start.5) | collective-permute-done | bytes 491552 | tf_op jit(solution)/shard_map/ppermute | solution.py:195
  60.8 8.7 %all-to-all-done.1.bags_ref = f32[32,16,128]{2,1,0:T(8,128)S(1)} async-done(((f32[32,16,128]{2,1,0:T(8,128)}), f32[32,16,128]{2,1,0:T(8,128)S(1)}, u32[]{:S(2)}, u32[]{:S(2)}) %all-to-all-start.1) | async-done | bytes 262176 | tf_op jit(solution)/shard_map/all_to_all | solution.py:283
  69.6 3.5 %top.1 = f32[1,16]{1,0:T(1,128)} custom-call(s32[5]{0:T(128)S(1)} %stack.32.meta_ref, f32[32,16,128]{2,1,0:T(8,128)S(1)} %all-to-all-done.1.bags_ref, f32[16,128]{1,0:T(8,128)S(1)} %get-tuple-element.20.bottom_ref, bf16[4,1,64]{2,1,0:T(2,128)(2,1)S(1)} %reshape.14.last_ref, bf16[2,960,256]{2,1,0:T(8,128)(2,1)S(1)} %get-tuple-element.21.own_ref, ...), custom_call_target="tpu_custom_call" | custom-call | flops 5000000000 | bytes 1048576 | tf_op jit(solution)/shard_map/top/pallas_call | solution.py:286
  (26 shorter events, 0.1 us)
Async XLA Ops:
  0.0 0.8 %copy-start.6 = (s32[16,8,8]{0,2,1:T(8,128)S(1)}, s32[16,8,8]{0,2,1:T(8,128)}, u32[]{:S(2)}) copy-start(s32[16,8,8]{0,2,1:T(8,128)} %param.13) | copy-start | bytes 12292
  0.8 0.7 copy-start.8
  1.4 1.0 %copy-start.10 = (bf16[2048,128]{1,0:T(8,128)(2,1)S(1)}, bf16[2048,128]{1,0:T(8,128)(2,1)}, u32[]{:S(2)}) copy-start(bf16[2048,128]{1,0:T(8,128)(2,1)} %param.12) | copy-start | bytes 1572868
  1.4 20.6 %copy-start = (bf16[1024,256]{1,0:T(8,128)(2,1)S(1)}, bf16[1024,256]{1,0:T(8,128)(2,1)}, u32[]{:S(2)}) copy-start(bf16[1024,256]{1,0:T(8,128)(2,1)} %w2_ref.1) | copy-start | bytes 1572868
  1.5 20.6 %copy-start.1 = (bf16[1024,128]{1,0:T(8,128)(2,1)S(1)}, bf16[1024,128]{1,0:T(8,128)(2,1)}, u32[]{:S(2)}) copy-start(bf16[1024,128]{1,0:T(8,128)(2,1)} %w3_ref.1) | copy-start | bytes 786436
  1.5 20.7 %copy-start.2 = (bf16[512,256]{1,0:T(8,128)(2,1)S(1)}, bf16[512,256]{1,0:T(8,128)(2,1)}, u32[]{:S(2)}) copy-start(bf16[512,256]{1,0:T(8,128)(2,1)} %b2_ref.1) | copy-start | bytes 786436
  1.5 20.7 %copy-start.3 = (bf16[164,256]{1,0:T(8,128)(2,1)S(1)}, bf16[164,256]{1,0:T(8,128)(2,1)}, u32[]{:S(2)}) copy-start(bf16[164,256]{1,0:T(8,128)(2,1)} %w1_ref.1) | copy-start | bytes 251908
  1.5 20.7 %copy-start.4 = (bf16[512,64]{0,1:T(8,128)(2,1)S(1)}, bf16[512,64]{0,1:T(8,128)(2,1)}, u32[]{:S(2)}) copy-start(bf16[512,64]{0,1:T(8,128)(2,1)} %param.22) | copy-start | bytes 196612
  1.5 20.7 %copy-start.5 = (bf16[256,128]{1,0:T(8,128)(2,1)S(1)}, bf16[256,128]{1,0:T(8,128)(2,1)}, u32[]{:S(2)}) copy-start(bf16[256,128]{1,0:T(8,128)(2,1)} %b3_ref.1) | copy-start | bytes 196612
  2.5 29.4 %collective-permute-start = (bf16[2048,128]{1,0:T(8,128)(2,1)S(1)}, bf16[2048,128]{1,0:T(8,128)(2,1)}, u32[]{:S(2)}, u32[]{:S(2)}) collective-permute-start(bf16[2048,128]{1,0:T(8,128)(2,1)S(1)} %copy-done.10), channel_id=1, source_target_pairs={{0,8},{8,0},{1,9},{9,1},{2,10},{10,2},{3,11},{11,3},{4,12},{12,4},... | collective-permute-start | bytes 1572872 | tf_op jit(solution)/shard_map/ppermute | solution.py:195
  6.8 15.4 %copy-start.7 = (bf16[13,512]{1,0:T(8,128)(2,1)S(1)}, bf16[13,512]{1,0:T(8,128)(2,1)}, u32[]{:S(2)}) copy-start(bf16[13,512]{1,0:T(8,128)(2,1)} %b1_ref.1) | copy-start | bytes 39940
  6.8 15.4 %copy-start.9 = (bf16[16,13]{1,0:T(8,128)(2,1)S(1)}, bf16[16,13]{1,0:T(8,128)(2,1)}, u32[]{:S(2)}) copy-start(bf16[16,13]{1,0:T(8,128)(2,1)} %dense_ref.1) | copy-start | bytes 1252
  6.8 28.2 %all-to-all-start = ((s32[32,1,128]{2,1,0:T(1,128)}), s32[32,1,128]{2,1,0:T(1,128)S(1)}, u32[]{:S(2)}, u32[]{:S(2)}) async-start(s32[32,1,128]{2,1,0:T(1,128)} %bitcast.8), calls=%async_computation | async-start | bytes 32768 | tf_op jit(solution)/shard_map/all_to_all | solution.py:238
  23.9 30.9 %collective-permute-start.2 = (bf16[2,960,256]{2,1,0:T(8,128)(2,1)S(1)}, bf16[2,960,256]{2,1,0:T(8,128)(2,1)}, u32[]{:S(2)}, u32[]{:S(2)}) collective-permute-start(bf16[2,960,256]{2,1,0:T(8,128)(2,1)S(1)} %get-tuple-element.21.own_ref), channel_id=1, source_target_pairs={{0,1},{1,2},{2,3},{3,0},{4,7},{5,4},{6,5},{7,6},{8,9},{9,10},{10,1... | collective-permute-start | bytes 2949128 | tf_op jit(solution)/shard_map/ppermute | solution.py:261
  27.3 29.4 %collective-permute-start.4 = (bf16[960,256]{1,0:T(8,128)(2,1)}, bf16[960,256]{1,0:T(8,128)(2,1)}, u32[]{:S(2)}, u32[]{:S(2)}) collective-permute-start(bf16[960,256]{1,0:T(8,128)(2,1)} %get-tuple-element.23), channel_id=1, source_target_pairs={{0,2},{1,3},{2,0},{3,1},{4,6},{5,7},{6,4},{7,5},{8,10},{9,11},{10,... | collective-permute-start | bytes 1474568 | tf_op jit(solution)/shard_map/ppermute | solution.py:195
  33.1 4.6 %collective-permute-start.1 = (bf16[2,2048,128]{2,1,0:T(8,128)(2,1)S(1)}, bf16[2,2048,128]{2,1,0:T(8,128)(2,1)S(1)}, u32[]{:S(2)}, u32[]{:S(2)}) collective-permute-start(bf16[2,2048,128]{2,1,0:T(8,128)(2,1)S(1)} %pad_maximum_fusion.same_ref), channel_id=1, source_target_pairs={{0,4},{4,0},{1,5},{5,1},{2,6},{6,2},{3,7},{7,3},{8,12},{12,8},{9,1... | collective-permute-start | bytes 3145736 | tf_op jit(solution)/shard_map/ppermute | solution.py:195
  42.6 27.0 %all-to-all-start.1 = ((f32[32,16,128]{2,1,0:T(8,128)}), f32[32,16,128]{2,1,0:T(8,128)S(1)}, u32[]{:S(2)}, u32[]{:S(2)}) async-start(f32[32,16,128]{2,1,0:T(8,128)} %bitcast.13), calls=%async_computation.1 | async-start | bytes 524288 | tf_op jit(solution)/shard_map/all_to_all | solution.py:283
  54.8 4.4 %copy-start.11 = (bf16[256]{0:T(256)(128)(2,1)S(1)}, bf16[256]{0:T(256)(128)(2,1)}, u32[]{:S(2)}) copy-start(bf16[256]{0:T(256)(128)(2,1)} %param.23) | copy-start | bytes 1540
  54.8 14.8 %collective-permute-start.3 = (bf16[2,960,256]{2,1,0:T(8,128)(2,1)}, bf16[2,960,256]{2,1,0:T(8,128)(2,1)S(1)}, u32[]{:S(2)}, u32[]{:S(2)}) collective-permute-start(bf16[2,960,256]{2,1,0:T(8,128)(2,1)} %held.4.side_ref), channel_id=1, source_target_pairs={{0,4},{4,0},{1,5},{5,1},{2,6},{6,2},{3,7},{7,3},{8,12},{12,8},{9,1... | collective-permute-start | bytes 2949128 | tf_op jit(solution)/shard_map/ppermute | solution.py:195
  56.7 4.1 %collective-permute-start.5 = (bf16[960,256]{1,0:T(8,128)(2,1)}, bf16[960,256]{1,0:T(8,128)(2,1)S(1)}, u32[]{:S(2)}, u32[]{:S(2)}) collective-permute-start(bf16[960,256]{1,0:T(8,128)(2,1)} %held.5.near_ref), channel_id=1, source_target_pairs={{0,4},{4,0},{1,5},{5,1},{2,6},{6,2},{3,7},{7,3},{8,12},{12,8},{9,1... | collective-permute-start | bytes 1474568 | tf_op jit(solution)/shard_map/ppermute | solution.py:195

commit v5 on v3

--- a/solution.py
+++ b/solution.py
@@ -42,7 +42,15 @@
     return pltpu.CompilerParams(vmem_limit_bytes=mib << 20)
 
 
-def prepare_kernel(peers, idx_ref, len_ref, out_ref):
+def prepare_kernel(peers, idx_hbm, len_hbm, out_ref, idx_ref, len_ref, sem):
+    copies = [
+        pltpu.make_async_copy(idx_hbm, idx_ref, sem.at[0]),
+        pltpu.make_async_copy(len_hbm, len_ref, sem.at[1]),
+    ]
+    for copy in copies:
+        copy.start()
+    for copy in copies:
+        copy.wait()
     lens = len_ref[...]
     parts = [jnp.where(lens > h, idx_ref[:, h, :], -1) for h in range(HOT)]
     rows = jnp.concatenate(parts, axis=1)
@@ -53,9 +61,8 @@
 
 
 def pack_kernel(
-    meta_ref, w1_ref, w2_ref, w3_ref, w4_ref, dense_ref, b1_ref, b2_ref, b3_ref, pack_ref, half_ref, bottom_ref
+    w1_ref, w2_ref, w3_ref, w4_ref, dense_ref, b1_ref, b2_ref, b3_ref, pack_ref, bottom_ref
 ):
-    core = meta_ref[2]
     tail = w1_ref[HEAD_ROWS:, :]
     pack_ref[0, 0:HEAD_ROWS, :] = w1_ref[0:HEAD_ROWS, :]
     pack_ref[1, 0:HEAD_ROWS, :] = jnp.concatenate(
@@ -74,10 +81,13 @@
         at += quarter
         half = w4_ref.shape[1] // 2
         pack_ref[h, at : at + w4_ref.shape[0], :] = w4_ref[:, h * half : (h + 1) * half]
-    half_ref[...] = pack_ref[core]
     lower = relu(mm(dense_ref[...], b1_ref[...])).astype(BF)
     middle = relu(mm(lower, b2_ref[...])).astype(BF)
     bottom_ref[...] = relu(mm(middle, b3_ref[...]))
+
+
+def pick_kernel(meta_ref, side_ref, half_ref):
+    half_ref[...] = side_ref[meta_ref[2]]
 
 
 def lookup_kernel(meta_ref, idx_ref, own_ref, other_ref, out_ref, code_ref, lo_ref, count_ref):
@@ -213,34 +223,39 @@
     rows = pl.pallas_call(
         functools.partial(prepare_kernel, along_z),
         out_shape=jax.ShapeDtypeStruct((peers, HOT * samples), jnp.int32),
-        in_specs=[VM] * 2,
+        in_specs=[pl.BlockSpec(memory_space=pltpu.HBM)] * 2,
         out_specs=VM,
-        compiler_params=params(8),
+        scratch_shapes=[
+            pltpu.VMEM((TAB, HOT, samples), jnp.int32),
+            pltpu.VMEM((TAB, samples), jnp.int32),
+            pltpu.SemaphoreType.DMA((2,)),
+        ],
+        compiler_params=params(60),
         cost_estimate=cost(1),
         name="prepare",
     )(jnp.transpose(indices, (1, 2, 0)), jnp.transpose(bag_lengths))
     rows, tables, meta = lax.optimization_barrier((rows, tables, meta))
     wanted = lax.all_to_all(rows, (Y, Z), 0, 0, tiled=True)
-    other = shifted(tables, C, 1)
+    wanted = held(wanted, 60, pltpu.VMEM)
     w4t = jnp.transpose(w4)
     pack_rows = HEAD_ROWS + w2.shape[0] // 2 + w3.shape[0] // 4 + w4t.shape[0]
-    pack, half, bottom = pl.pallas_call(
+    pack, bottom = pl.pallas_call(
         pack_kernel,
         out_shape=(
             jax.ShapeDtypeStruct((2, pack_rows, w2.shape[1]), BF),
-            jax.ShapeDtypeStruct((pack_rows, w2.shape[1]), BF),
             jax.ShapeDtypeStruct((samples, width), F32),
         ),
-        in_specs=[SM] + [VM] * 8,
-        out_specs=(VM, VM, VM),
-        compiler_params=params(10),
+        in_specs=[VM] * 8,
+        out_specs=(VM, VM),
+        compiler_params=params(8),
         cost_estimate=cost(3),
         name="pack",
-    )(meta, w1, w2, w3, w4t, dense, b1, b2, b3)
+    )(w1, w2, w3, w4t, dense, b1, b2, b3)
     sides = [(i, (i + 1) % reps) for i in range(reps)]
     sides += [(reps + i, reps + (i - 1) % reps) for i in range(reps)]
+    tables, pack = lax.optimization_barrier((tables, pack))
+    other = shifted(tables, C, 1)
     side = lax.ppermute(pack, (C, X), sides)
-    near = shifted(half, X, 2)
     partial_bags = pl.pallas_call(
         lookup_kernel,
         out_shape=jax.ShapeDtypeStruct((peers * samples, width), F32),
@@ -255,8 +270,18 @@
         cost_estimate=cost(40),
         name="lookup",
     )(meta, wanted, tables, other)
-    side, near = held(side, 60, pltpu.VMEM), held(near, 60, pl.ANY)
+    side = held(side, 60, pltpu.VMEM)
     mirror = shifted(side, C, 1)
+    half = pl.pallas_call(
+        pick_kernel,
+        out_shape=jax.ShapeDtypeStruct((pack_rows, w2.shape[1]), BF),
+        in_specs=[SM, VM],
+        out_specs=VM,
+        compiler_params=params(4),
+        cost_estimate=cost(1),
+        name="pick",
+    )(meta, side)
+    near = lax.ppermute(half, (C, X), sides)
     far = shifted(near, C, 1)
     bags = lax.all_to_all(
         partial_bags.reshape(peers, samples, width), (Y, Z), 0, 0, tiled=True

time: 71 us -> 67 us (0.944)
  the two profiles are of different devices: /device:TPU:16 before, /device:TPU:1 now
where the time goes in v5:
time: 67 us; the launch traced here: 66.4 us
  starting transfers between devices  41.8 us (62%)
  waiting for transfers between devices  12.7 us (19%)
  Pallas kernels  11.4 us (17%)
    all_to_all x1, starting transfers between devices, body(): wanted = lax.all_to_all(rows, (Y, Z), 0, 0, tiled=True)  17.3 us
    all_to_all x1, starting transfers between devices, body(): lax.all_to_all(partial_bags.reshape(peers, samples, width), (Y, Z), 0, 0,...  9.38 us
    ppermute x3, starting transfers between devices, shifted(): return lax.ppermute(a, axis, [(i, (i + k) % n) for i in range(n)])  8.3 us
    pallas_call x1, Pallas kernels, body(): pl.pallas_call(lookup_kernel, out_shape=jax.ShapeDtypeStruct((peers * sam...  5.5 us
    ppermute x1, waiting for transfers between devices, body(): near = lax.ppermute(half, (C, X), sides)  5.34 us
    ppermute x1, starting transfers between devices, body(): side = lax.ppermute(pack, (C, X), sides)  4.39 us
    all_to_all x1, waiting for transfers between devices, body(): lax.all_to_all(partial_bags.reshape(peers, samples, width), (Y, Z), 0, 0,...  4.32 us
    pallas_call x1, Pallas kernels, body(): pl.pallas_call(top_kernel, out_shape=jax.ShapeDtypeStruct((1, samples), F...  3.32 us
  transfers between devices with their start and end apart: 7, of which 3 were waited for; matrix products, arithmetic and copies ran while one was open for 0% of the time, Pallas kernels for 10%

profile of v5, /device:TPU:1, one launch (start us, length us, event | category | flops | bytes accessed | tf_op | source)
XLA Modules:
  0.0 66.4 jit_solution(6917631786921253072)
XLA Ops:
  0.0 0.0 copy-start.3
  0.0 1.6 %prepare.1 = s32[64,128]{1,0:T(8,128)} custom-call(s32[8,8,16]{2,1,0:T(8,128)} %bitcast.16, s32[8,16]{1,0:T(8,128)} %bitcast.17), custom_call_target="tpu_custom_call" | custom-call | flops 1000000000 | bytes 1048576 | tf_op jit(solution)/shard_map/prepare/pallas_call | solution.py:223
  1.6 0.0 copy-start.4
  1.6 0.1 pad_add_fusion.meta_ref
  1.7 17.3 %all-to-all-start = ((s32[64,1,128]{2,1,0:T(1,128)}), s32[64,1,128]{2,1,0:T(1,128)S(1)}, u32[]{:S(2)}, u32[]{:S(2)}) async-start(s32[64,1,128]{2,1,0:T(1,128)} %bitcast.15), calls=%async_computation | async-start | bytes 65536 | tf_op jit(solution)/shard_map/all_to_all | solution.py:238
  19.1 0.4 pack.1
  19.5 2.9 %collective-permute-start = (bf16[2048,128]{1,0:T(8,128)(2,1)}, bf16[2048,128]{1,0:T(8,128)(2,1)S(1)}, u32[]{:S(2)}, u32[]{:S(2)}) collective-permute-start(bf16[2048,128]{1,0:T(8,128)(2,1)} %own_ref), channel_id=1, source_target_pairs={{0,4},{4,0},{1,5},{5,1},{2,6},{6,2},{3,7},{7,3},{8,12},{12,8},{9,1... | collective-permute-start | bytes 1572872 | tf_op jit(solution)/shard_map/ppermute | solution.py:196
  22.4 4.4 %collective-permute-start.1 = (bf16[2,960,256]{2,1,0:T(8,128)(2,1)S(1)}, bf16[2,960,256]{2,1,0:T(8,128)(2,1)S(1)}, u32[]{:S(2)}, u32[]{:S(2)}) collective-permute-start(bf16[2,960,256]{2,1,0:T(8,128)(2,1)S(1)} %get-tuple-element.18.own_ref), channel_id=1, source_target_pairs={{0,1},{1,2},{2,3},{3,0},{4,7},{5,4},{6,5},{7,6},{8,9},{9,10},{10,1... | collective-permute-start | bytes 2949128 | tf_op jit(solution)/shard_map/ppermute | solution.py:258
  26.8 3.1 %all-to-all-done = s32[64,1,128]{2,1,0:T(1,128)S(1)} async-done(((s32[64,1,128]{2,1,0:T(1,128)}), s32[64,1,128]{2,1,0:T(1,128)S(1)}, u32[]{:S(2)}, u32[]{:S(2)}) %all-to-all-start) | async-done | bytes 32800 | tf_op jit(solution)/shard_map/all_to_all | solution.py:238
  29.8 0.0 collective-permute-done.other_ref
  29.8 5.5 %lookup.1 = f32[1024,128]{1,0:T(8,128)} custom-call(s32[4]{0:T(128)S(1)} %pad_add_fusion.meta_ref, s32[64,128]{1,0:T(8,128)S(1)} %held.2.idx_ref, bf16[2048,128]{1,0:T(8,128)(2,1)} %own_ref, bf16[2048,128]{1,0:T(8,128)(2,1)S(1)} %collective-permute-done.other_ref), custom_call_target="tpu_custom_call" | custom-call | flops 40000000000 | bytes 1048576 | tf_op jit(solution)/shard_map/lookup/pallas_call | solution.py:259
  35.4 9.4 %all-to-all-start.1 = ((f32[64,16,128]{2,1,0:T(8,128)}), f32[64,16,128]{2,1,0:T(8,128)S(1)}, u32[]{:S(2)}, u32[]{:S(2)}) async-start(f32[64,16,128]{2,1,0:T(8,128)} %bitcast.10), calls=%async_computation.1 | async-start | bytes 1048576 | tf_op jit(solution)/shard_map/all_to_all | solution.py:286
  44.7 0.0 collective-permute-done.1.in_ref
  44.8 0.0 copy-start.8
  44.8 0.6 pick.1
  45.4 2.5 %collective-permute-start.3 = (bf16[960,256]{1,0:T(8,128)(2,1)S(1)}, bf16[960,256]{1,0:T(8,128)(2,1)}, u32[]{:S(2)}, u32[]{:S(2)}) collective-permute-start(bf16[960,256]{1,0:T(8,128)(2,1)S(1)} %pick.1), channel_id=1, source_target_pairs={{0,1},{1,2},{2,3},{3,0},{4,7},{5,4},{6,5},{7,6},{8,9},{9,10},{10,1... | collective-permute-start | bytes 1474568 | tf_op jit(solution)/shard_map/ppermute | solution.py:284
  47.8 2.2 %collective-permute-start.2 = (bf16[2,960,256]{2,1,0:T(8,128)(2,1)S(1)}, bf16[2,960,256]{2,1,0:T(8,128)(2,1)S(1)}, u32[]{:S(2)}, u32[]{:S(2)}) collective-permute-start(bf16[2,960,256]{2,1,0:T(8,128)(2,1)S(1)} %held.3.side_ref), channel_id=1, source_target_pairs={{0,4},{4,0},{1,5},{5,1},{2,6},{6,2},{3,7},{7,3},{8,12},{12,8},{9,1... | collective-permute-start | bytes 2949128 | tf_op jit(solution)/shard_map/ppermute | solution.py:196
  50.0 5.3 %collective-permute-done.3.near_ref = bf16[960,256]{1,0:T(8,128)(2,1)} collective-permute-done((bf16[960,256]{1,0:T(8,128)(2,1)S(1)}, bf16[960,256]{1,0:T(8,128)(2,1)}, u32[]{:S(2)}, u32[]{:S(2)}) %collective-permute-start.3) | collective-permute-done | bytes 491552 | tf_op jit(solution)/shard_map/ppermute | solution.py:284
  55.3 3.3 %collective-permute-start.4 = (bf16[960,256]{1,0:T(8,128)(2,1)}, bf16[960,256]{1,0:T(8,128)(2,1)}, u32[]{:S(2)}, u32[]{:S(2)}) collective-permute-start(bf16[960,256]{1,0:T(8,128)(2,1)} %collective-permute-done.3.near_ref), channel_id=1, source_target_pairs={{0,4},{4,0},{1,5},{5,1},{2,6},{6,2},{3,7},{7,3},{8,12},{12,8},{9,1... | collective-permute-start | bytes 1474568 | tf_op jit(solution)/shard_map/ppermute | solution.py:196
  58.6 0.1 reshape.14.last_ref
  58.7 4.3 %all-to-all-done.1.bags_ref = f32[64,16,128]{2,1,0:T(8,128)S(1)} async-done(((f32[64,16,128]{2,1,0:T(8,128)}), f32[64,16,128]{2,1,0:T(8,128)S(1)}, u32[]{:S(2)}, u32[]{:S(2)}) %all-to-all-start.1) | async-done | bytes 524320 | tf_op jit(solution)/shard_map/all_to_all | solution.py:286
  63.0 0.0 collective-permute-done.4.far_ref
  63.0 0.0 collective-permute-done.2.mirror_ref
  63.0 3.3 %top.1 = f32[1,16]{1,0:T(1,128)} custom-call(s32[4]{0:T(128)S(1)} %pad_add_fusion.meta_ref, f32[64,16,128]{2,1,0:T(8,128)S(1)} %all-to-all-done.1.bags_ref, f32[16,128]{1,0:T(8,128)S(1)} %get-tuple-element.17.bottom_ref, bf16[4,1,64]{2,1,0:T(2,128)(2,1)S(1)} %reshape.14.last_ref, bf16[2,960,256]{2,1,0:T(8,128)(2,1)S(1)} %get-tuple-element.18.own_ref, ...), custom_call_target="tpu_custom_call" | custom-call | flops 5000000000 | bytes 1048576 | tf_op jit(solution)/shard_map/top/pallas_call | solution.py:289
  (17 shorter events, 0.0 us)
Async XLA Ops:
  0.0 19.0 %copy-start = (bf16[1024,256]{1,0:T(8,128)(2,1)S(1)}, bf16[1024,256]{1,0:T(8,128)(2,1)}, u32[]{:S(2)}) copy-start(bf16[1024,256]{1,0:T(8,128)(2,1)} %w2_ref.1) | copy-start | bytes 1572868
  0.0 19.0 %copy-start.1 = (bf16[1024,128]{1,0:T(8,128)(2,1)S(1)}, bf16[1024,128]{1,0:T(8,128)(2,1)}, u32[]{:S(2)}) copy-start(bf16[1024,128]{1,0:T(8,128)(2,1)} %w3_ref.1) | copy-start | bytes 786436
  0.0 19.0 %copy-start.2 = (bf16[512,256]{1,0:T(8,128)(2,1)S(1)}, bf16[512,256]{1,0:T(8,128)(2,1)}, u32[]{:S(2)}) copy-start(bf16[512,256]{1,0:T(8,128)(2,1)} %b2_ref.1) | copy-start | bytes 786436
  0.0 19.0 %copy-start.3 = (bf16[164,256]{1,0:T(8,128)(2,1)S(1)}, bf16[164,256]{1,0:T(8,128)(2,1)}, u32[]{:S(2)}) copy-start(bf16[164,256]{1,0:T(8,128)(2,1)} %w1_ref.1) | copy-start | bytes 251908
  0.0 19.0 %copy-start.5 = (bf16[256,128]{1,0:T(8,128)(2,1)S(1)}, bf16[256,128]{1,0:T(8,128)(2,1)}, u32[]{:S(2)}) copy-start(bf16[256,128]{1,0:T(8,128)(2,1)} %b3_ref.1) | copy-start | bytes 196612
  0.0 19.0 %copy-start.6 = (bf16[13,512]{1,0:T(8,128)(2,1)S(1)}, bf16[13,512]{1,0:T(8,128)(2,1)}, u32[]{:S(2)}) copy-start(bf16[13,512]{1,0:T(8,128)(2,1)} %b1_ref.1) | copy-start | bytes 39940
  1.6 17.4 %copy-start.4 = (bf16[512,64]{0,1:T(8,128)(2,1)S(1)}, bf16[512,64]{0,1:T(8,128)(2,1)}, u32[]{:S(2)}) copy-start(bf16[512,64]{0,1:T(8,128)(2,1)} %param.22) | copy-start | bytes 196612
  1.7 17.4 %copy-start.7 = (bf16[16,13]{1,0:T(8,128)(2,1)S(1)}, bf16[16,13]{1,0:T(8,128)(2,1)}, u32[]{:S(2)}) copy-start(bf16[16,13]{1,0:T(8,128)(2,1)} %dense_ref.1) | copy-start | bytes 1252
  1.7 28.1 %all-to-all-start = ((s32[64,1,128]{2,1,0:T(1,128)}), s32[64,1,128]{2,1,0:T(1,128)S(1)}, u32[]{:S(2)}, u32[]{:S(2)}) async-start(s32[64,1,128]{2,1,0:T(1,128)} %bitcast.15), calls=%async_computation | async-start | bytes 65536 | tf_op jit(solution)/shard_map/all_to_all | solution.py:238
  19.5 10.3 %collective-permute-start = (bf16[2048,128]{1,0:T(8,128)(2,1)}, bf16[2048,128]{1,0:T(8,128)(2,1)S(1)}, u32[]{:S(2)}, u32[]{:S(2)}) collective-permute-start(bf16[2048,128]{1,0:T(8,128)(2,1)} %own_ref), channel_id=1, source_target_pairs={{0,4},{4,0},{1,5},{5,1},{2,6},{6,2},{3,7},{7,3},{8,12},{12,8},{9,1... | collective-permute-start | bytes 1572872 | tf_op jit(solution)/shard_map/ppermute | solution.py:196
  22.4 22.4 %collective-permute-start.1 = (bf16[2,960,256]{2,1,0:T(8,128)(2,1)S(1)}, bf16[2,960,256]{2,1,0:T(8,128)(2,1)S(1)}, u32[]{:S(2)}, u32[]{:S(2)}) collective-permute-start(bf16[2,960,256]{2,1,0:T(8,128)(2,1)S(1)} %get-tuple-element.18.own_ref), channel_id=1, source_target_pairs={{0,1},{1,2},{2,3},{3,0},{4,7},{5,4},{6,5},{7,6},{8,9},{9,10},{10,1... | collective-permute-start | bytes 2949128 | tf_op jit(solution)/shard_map/ppermute | solution.py:258
  35.4 27.7 %all-to-all-start.1 = ((f32[64,16,128]{2,1,0:T(8,128)}), f32[64,16,128]{2,1,0:T(8,128)S(1)}, u32[]{:S(2)}, u32[]{:S(2)}) async-start(f32[64,16,128]{2,1,0:T(8,128)} %bitcast.10), calls=%async_computation.1 | async-start | bytes 1048576 | tf_op jit(solution)/shard_map/all_to_all | solution.py:286
  44.8 13.9 %copy-start.8 = (bf16[256]{0:T(256)(128)(2,1)S(1)}, bf16[256]{0:T(256)(128)(2,1)}, u32[]{:S(2)}) copy-start(bf16[256]{0:T(256)(128)(2,1)} %param.23) | copy-start | bytes 1540
  45.4 10.0 %collective-permute-start.3 = (bf16[960,256]{1,0:T(8,128)(2,1)S(1)}, bf16[960,256]{1,0:T(8,128)(2,1)}, u32[]{:S(2)}, u32[]{:S(2)}) collective-permute-start(bf16[960,256]{1,0:T(8,128)(2,1)S(1)} %pick.1), channel_id=1, source_target_pairs={{0,1},{1,2},{2,3},{3,0},{4,7},{5,4},{6,5},{7,6},{8,9},{9,10},{10,1... | collective-permute-start | bytes 1474568 | tf_op jit(solution)/shard_map/ppermute | solution.py:284
  47.8 15.2 %collective-permute-start.2 = (bf16[2,960,256]{2,1,0:T(8,128)(2,1)S(1)}, bf16[2,960,256]{2,1,0:T(8,128)(2,1)S(1)}, u32[]{:S(2)}, u32[]{:S(2)}) collective-permute-start(bf16[2,960,256]{2,1,0:T(8,128)(2,1)S(1)} %held.3.side_ref), channel_id=1, source_target_pairs={{0,4},{4,0},{1,5},{5,1},{2,6},{6,2},{3,7},{7,3},{8,12},{12,8},{9,1... | collective-permute-start | bytes 2949128 | tf_op jit(solution)/shard_map/ppermute | solution.py:196
  55.3 7.7 %collective-permute-start.4 = (bf16[960,256]{1,0:T(8,128)(2,1)}, bf16[960,256]{1,0:T(8,128)(2,1)}, u32[]{:S(2)}, u32[]{:S(2)}) collective-permute-start(bf16[960,256]{1,0:T(8,128)(2,1)} %collective-permute-done.3.near_ref), channel_id=1, source_target_pairs={{0,4},{4,0},{1,5},{5,1},{2,6},{6,2},{3,7},{7,3},{8,12},{12,8},{9,1... | collective-permute-start | bytes 1474568 | tf_op jit(solution)/shard_map/ppermute | solution.py:196

commit v6 on v5

--- a/solution.py
+++ b/solution.py
@@ -86,10 +86,6 @@
     bottom_ref[...] = relu(mm(middle, b3_ref[...]))
 
 
-def pick_kernel(meta_ref, side_ref, half_ref):
-    half_ref[...] = side_ref[meta_ref[2]]
-
-
 def lookup_kernel(meta_ref, idx_ref, own_ref, other_ref, out_ref, code_ref, lo_ref, count_ref):
     peers, width = idx_ref.shape
     bags = width // HOT
@@ -126,7 +122,7 @@
 
 
 def top_kernel(
-    meta_ref, bags_ref, bottom_ref, last_ref, own_ref, side_ref, mirror_ref, near_ref, far_ref,
+    meta_ref, bags_ref, bottom_ref, last_ref, own_ref, side_ref, mirror_ref, across_ref,
     out_ref, in_ref, a1_ref, a2_ref, a3_ref,
 ):
     core, x = meta_ref[2], meta_ref[3]
@@ -158,7 +154,7 @@
         (x, whole(own_ref)),
         (jnp.where(core == 0, before, after), whole(side_ref)),
         (jnp.where(core == 0, after, before), whole(mirror_ref)),
-        (lax.rem(x + 2, reps), [(core, near_ref), (1 - core, far_ref)]),
+        (lax.rem(x + 2, reps), whole(across_ref)),
     )
     for owner, halves in shards:
         y = sum(mm(in_ref[h], w[0:HEAD_ROWS, :]) for h, w in halves)
@@ -272,24 +268,14 @@
     )(meta, wanted, tables, other)
     side = held(side, 60, pltpu.VMEM)
     mirror = shifted(side, C, 1)
-    half = pl.pallas_call(
-        pick_kernel,
-        out_shape=jax.ShapeDtypeStruct((pack_rows, w2.shape[1]), BF),
-        in_specs=[SM, VM],
-        out_specs=VM,
-        compiler_params=params(4),
-        cost_estimate=cost(1),
-        name="pick",
-    )(meta, side)
-    near = lax.ppermute(half, (C, X), sides)
-    far = shifted(near, C, 1)
+    across = lax.ppermute(side, (C, X), sides)
     bags = lax.all_to_all(
         partial_bags.reshape(peers, samples, width), (Y, Z), 0, 0, tiled=True
     )
     logit = pl.pallas_call(
         top_kernel,
         out_shape=jax.ShapeDtypeStruct((1, samples), F32),
-        in_specs=[SM] + [VM] * 8,
+        in_specs=[SM] + [VM] * 7,
         out_specs=VM,
         scratch_shapes=[
             pltpu.VMEM((2, samples, width), BF),
@@ -300,7 +286,7 @@
         compiler_params=params(10),
         cost_estimate=cost(5),
         name="top",
-    )(meta, bags, bottom, last.reshape(reps, 1, -1), pack, side, mirror, near, far)
+    )(meta, bags, bottom, last.reshape(reps, 1, -1), pack, side, mirror, across)
     return logit.reshape(samples)
 
 

time: 67 us -> 67 us (level)
  waiting for transfers between devices: 12.7 us -> 16.6 us
  starting transfers between devices: 41.8 us -> 38.5 us
    all_to_all x1, waiting for transfers between devices: 4.32 us -> 13.5 us  [body(): lax.all_to_all(partial_bags.reshape(peers, samples, width), (Y, Z), 0, 0,...]
    ppermute x1, waiting for transfers between devices: 5.34 us -> 0.01 us  [body(): across = lax.ppermute(side, (C, X), sides)]
    ppermute x3 -> x2, starting transfers between devices: 8.3 us -> 4.79 us  [shifted(): return lax.ppermute(a, axis, [(i, (i + k) % n) for i in range(n)])]
  transfers between devices with their start and end apart: 7 -> 6, of which waited for: 3 -> 2; matrix products, arithmetic and copies ran while one was open for 0% -> 0% of each run, Pallas kernels for 10% -> 9%
where the time goes in v6:
time: 67 us; the launch traced here: 66.4 us
  starting transfers between devices  38.5 us (57%)
  waiting for transfers between devices  16.6 us (25%)
  Pallas kernels  10.9 us (16%)
    all_to_all x1, starting transfers between devices, body(): wanted = lax.all_to_all(rows, (Y, Z), 0, 0, tiled=True)  17.3 us
    all_to_all x1, waiting for transfers between devices, body(): lax.all_to_all(partial_bags.reshape(peers, samples, width), (Y, Z), 0, 0,...  13.5 us
    all_to_all x1, starting transfers between devices, body(): lax.all_to_all(partial_bags.reshape(peers, samples, width), (Y, Z), 0, 0,...  9.41 us
    pallas_call x1, Pallas kernels, body(): pl.pallas_call(lookup_kernel, out_shape=jax.ShapeDtypeStruct((peers * sam...  5.53 us
    ppermute x2, starting transfers between devices, shifted(): return lax.ppermute(a, axis, [(i, (i + k) % n) for i in range(n)])  4.79 us
    ppermute x1, starting transfers between devices, body(): side = lax.ppermute(pack, (C, X), sides)  4.39 us
    pallas_call x1, Pallas kernels, body(): pl.pallas_call(top_kernel, out_shape=jax.ShapeDtypeStruct((1, samples), F...  3.34 us
    all_to_all x1, waiting for transfers between devices, body(): wanted = lax.all_to_all(rows, (Y, Z), 0, 0, tiled=True)  3.03 us
  transfers between devices with their start and end apart: 6, of which 2 were waited for; matrix products, arithmetic and copies ran while one was open for 0% of the time, Pallas kernels for 9%

profile of v6, /device:TPU:1, one launch (start us, length us, event | category | flops | bytes accessed | tf_op | source)
XLA Modules:
  0.0 66.4 jit_solution(2589359422253540581)
XLA Ops:
  0.0 0.0 copy-start.3
  0.0 0.0 copy-start.5
  0.0 0.0 copy-start.6
  0.0 1.6 %prepare.1 = s32[64,128]{1,0:T(8,128)} custom-call(s32[8,8,16]{2,1,0:T(8,128)} %bitcast.16, s32[8,16]{1,0:T(8,128)} %bitcast.17), custom_call_target="tpu_custom_call" | custom-call | flops 1000000000 | bytes 1048576 | tf_op jit(solution)/shard_map/prepare/pallas_call | solution.py:219
  1.6 0.0 copy-start.4
  1.6 0.1 pad_add_fusion.meta_ref
  1.7 17.3 %all-to-all-start = ((s32[64,1,128]{2,1,0:T(1,128)}), s32[64,1,128]{2,1,0:T(1,128)S(1)}, u32[]{:S(2)}, u32[]{:S(2)}) async-start(s32[64,1,128]{2,1,0:T(1,128)} %bitcast.15), calls=%async_computation | async-start | bytes 65536 | tf_op jit(solution)/shard_map/all_to_all | solution.py:234
  19.0 0.0 copy-done
  19.1 0.4 pack.1
  19.5 2.9 %collective-permute-start = (bf16[2048,128]{1,0:T(8,128)(2,1)}, bf16[2048,128]{1,0:T(8,128)(2,1)S(1)}, u32[]{:S(2)}, u32[]{:S(2)}) collective-permute-start(bf16[2048,128]{1,0:T(8,128)(2,1)} %own_ref), channel_id=1, source_target_pairs={{0,4},{4,0},{1,5},{5,1},{2,6},{6,2},{3,7},{7,3},{8,12},{12,8},{9,1... | collective-permute-start | bytes 1572872 | tf_op jit(solution)/shard_map/ppermute | solution.py:192
  22.4 4.4 %collective-permute-start.1 = (bf16[2,960,256]{2,1,0:T(8,128)(2,1)S(1)}, bf16[2,960,256]{2,1,0:T(8,128)(2,1)S(1)}, u32[]{:S(2)}, u32[]{:S(2)}) collective-permute-start(bf16[2,960,256]{2,1,0:T(8,128)(2,1)S(1)} %get-tuple-element.18.own_ref), channel_id=1, source_target_pairs={{0,1},{1,2},{2,3},{3,0},{4,7},{5,4},{6,5},{7,6},{8,9},{9,10},{10,1... | collective-permute-start | bytes 2949128 | tf_op jit(solution)/shard_map/ppermute | solution.py:254
  26.8 3.0 %all-to-all-done = s32[64,1,128]{2,1,0:T(1,128)S(1)} async-done(((s32[64,1,128]{2,1,0:T(1,128)}), s32[64,1,128]{2,1,0:T(1,128)S(1)}, u32[]{:S(2)}, u32[]{:S(2)}) %all-to-all-start) | async-done | bytes 32800 | tf_op jit(solution)/shard_map/all_to_all | solution.py:234
  29.8 0.0 collective-permute-done.other_ref
  29.8 5.5 %lookup.1 = f32[1024,128]{1,0:T(8,128)} custom-call(s32[4]{0:T(128)S(1)} %pad_add_fusion.meta_ref, s32[64,128]{1,0:T(8,128)S(1)} %held.2.idx_ref, bf16[2048,128]{1,0:T(8,128)(2,1)} %own_ref, bf16[2048,128]{1,0:T(8,128)(2,1)S(1)} %collective-permute-done.other_ref), custom_call_target="tpu_custom_call" | custom-call | flops 40000000000 | bytes 1048576 | tf_op jit(solution)/shard_map/lookup/pallas_call | solution.py:255
  35.3 9.4 %all-to-all-start.1 = ((f32[64,16,128]{2,1,0:T(8,128)}), f32[64,16,128]{2,1,0:T(8,128)S(1)}, u32[]{:S(2)}, u32[]{:S(2)}) async-start(f32[64,16,128]{2,1,0:T(8,128)} %bitcast.10), calls=%async_computation.1 | async-start | bytes 1048576 | tf_op jit(solution)/shard_map/all_to_all | solution.py:272
  44.8 0.0 copy-start.8
  44.8 0.0 collective-permute-done.1.in_ref
  44.8 1.9 %collective-permute-start.2 = (bf16[2,960,256]{2,1,0:T(8,128)(2,1)S(1)}, bf16[2,960,256]{2,1,0:T(8,128)(2,1)S(1)}, u32[]{:S(2)}, u32[]{:S(2)}) collective-permute-start(bf16[2,960,256]{2,1,0:T(8,128)(2,1)S(1)} %held.3.side_ref), channel_id=1, source_target_pairs={{0,4},{4,0},{1,5},{5,1},{2,6},{6,2},{3,7},{7,3},{8,12},{12,8},{9,1... | collective-permute-start | bytes 2949128 | tf_op jit(solution)/shard_map/ppermute | solution.py:192
  46.7 2.7 %collective-permute-start.3 = (bf16[2,960,256]{2,1,0:T(8,128)(2,1)S(1)}, bf16[2,960,256]{2,1,0:T(8,128)(2,1)}, u32[]{:S(2)}, u32[]{:S(2)}) collective-permute-start(bf16[2,960,256]{2,1,0:T(8,128)(2,1)S(1)} %held.3.side_ref), channel_id=1, source_target_pairs={{0,1},{1,2},{2,3},{3,0},{4,7},{5,4},{6,5},{7,6},{8,9},{9,10},{10,1... | collective-permute-start | bytes 2949128 | tf_op jit(solution)/shard_map/ppermute | solution.py:271
  49.4 0.1 reshape.14.last_ref
  49.5 13.5 %all-to-all-done.1.bags_ref = f32[64,16,128]{2,1,0:T(8,128)S(1)} async-done(((f32[64,16,128]{2,1,0:T(8,128)}), f32[64,16,128]{2,1,0:T(8,128)S(1)}, u32[]{:S(2)}, u32[]{:S(2)}) %all-to-all-start.1) | async-done | bytes 524320 | tf_op jit(solution)/shard_map/all_to_all | solution.py:272
  63.0 0.0 collective-permute-done.2.mirror_ref
  63.0 0.0 collective-permute-done.3.across_ref
  63.0 3.3 %top.1 = f32[1,16]{1,0:T(1,128)} custom-call(s32[4]{0:T(128)S(1)} %pad_add_fusion.meta_ref, f32[64,16,128]{2,1,0:T(8,128)S(1)} %all-to-all-done.1.bags_ref, f32[16,128]{1,0:T(8,128)S(1)} %get-tuple-element.17.bottom_ref, bf16[4,1,64]{2,1,0:T(2,128)(2,1)S(1)} %reshape.14.last_ref, bf16[2,960,256]{2,1,0:T(8,128)(2,1)S(1)} %get-tuple-element.18.own_ref, ...), custom_call_target="tpu_custom_call" | custom-call | flops 5000000000 | bytes 1048576 | tf_op jit(solution)/shard_map/top/pallas_call | solution.py:275
  (14 shorter events, 0.0 us)
Async XLA Ops:
  0.0 19.0 %copy-start = (bf16[1024,256]{1,0:T(8,128)(2,1)S(1)}, bf16[1024,256]{1,0:T(8,128)(2,1)}, u32[]{:S(2)}) copy-start(bf16[1024,256]{1,0:T(8,128)(2,1)} %w2_ref.1) | copy-start | bytes 1572868
  0.0 19.0 %copy-start.1 = (bf16[1024,128]{1,0:T(8,128)(2,1)S(1)}, bf16[1024,128]{1,0:T(8,128)(2,1)}, u32[]{:S(2)}) copy-start(bf16[1024,128]{1,0:T(8,128)(2,1)} %w3_ref.1) | copy-start | bytes 786436
  0.0 19.0 %copy-start.2 = (bf16[512,256]{1,0:T(8,128)(2,1)S(1)}, bf16[512,256]{1,0:T(8,128)(2,1)}, u32[]{:S(2)}) copy-start(bf16[512,256]{1,0:T(8,128)(2,1)} %b2_ref.1) | copy-start | bytes 786436
  0.0 19.0 %copy-start.3 = (bf16[164,256]{1,0:T(8,128)(2,1)S(1)}, bf16[164,256]{1,0:T(8,128)(2,1)}, u32[]{:S(2)}) copy-start(bf16[164,256]{1,0:T(8,128)(2,1)} %w1_ref.1) | copy-start | bytes 251908
  0.0 19.0 %copy-start.5 = (bf16[256,128]{1,0:T(8,128)(2,1)S(1)}, bf16[256,128]{1,0:T(8,128)(2,1)}, u32[]{:S(2)}) copy-start(bf16[256,128]{1,0:T(8,128)(2,1)} %b3_ref.1) | copy-start | bytes 196612
  0.0 19.0 %copy-start.6 = (bf16[13,512]{1,0:T(8,128)(2,1)S(1)}, bf16[13,512]{1,0:T(8,128)(2,1)}, u32[]{:S(2)}) copy-start(bf16[13,512]{1,0:T(8,128)(2,1)} %b1_ref.1) | copy-start | bytes 39940
  1.6 17.4 %copy-start.4 = (bf16[512,64]{0,1:T(8,128)(2,1)S(1)}, bf16[512,64]{0,1:T(8,128)(2,1)}, u32[]{:S(2)}) copy-start(bf16[512,64]{0,1:T(8,128)(2,1)} %param.22) | copy-start | bytes 196612
  1.7 17.4 %copy-start.7 = (bf16[16,13]{1,0:T(8,128)(2,1)S(1)}, bf16[16,13]{1,0:T(8,128)(2,1)}, u32[]{:S(2)}) copy-start(bf16[16,13]{1,0:T(8,128)(2,1)} %dense_ref.1) | copy-start | bytes 1252
  1.7 28.1 %all-to-all-start = ((s32[64,1,128]{2,1,0:T(1,128)}), s32[64,1,128]{2,1,0:T(1,128)S(1)}, u32[]{:S(2)}, u32[]{:S(2)}) async-start(s32[64,1,128]{2,1,0:T(1,128)} %bitcast.15), calls=%async_computation | async-start | bytes 65536 | tf_op jit(solution)/shard_map/all_to_all | solution.py:234
  19.5 10.3 %collective-permute-start = (bf16[2048,128]{1,0:T(8,128)(2,1)}, bf16[2048,128]{1,0:T(8,128)(2,1)S(1)}, u32[]{:S(2)}, u32[]{:S(2)}) collective-permute-start(bf16[2048,128]{1,0:T(8,128)(2,1)} %own_ref), channel_id=1, source_target_pairs={{0,4},{4,0},{1,5},{5,1},{2,6},{6,2},{3,7},{7,3},{8,12},{12,8},{9,1... | collective-permute-start | bytes 1572872 | tf_op jit(solution)/shard_map/ppermute | solution.py:192
  22.4 22.4 %collective-permute-start.1 = (bf16[2,960,256]{2,1,0:T(8,128)(2,1)S(1)}, bf16[2,960,256]{2,1,0:T(8,128)(2,1)S(1)}, u32[]{:S(2)}, u32[]{:S(2)}) collective-permute-start(bf16[2,960,256]{2,1,0:T(8,128)(2,1)S(1)} %get-tuple-element.18.own_ref), channel_id=1, source_target_pairs={{0,1},{1,2},{2,3},{3,0},{4,7},{5,4},{6,5},{7,6},{8,9},{9,10},{10,1... | collective-permute-start | bytes 2949128 | tf_op jit(solution)/shard_map/ppermute | solution.py:254
  35.3 27.7 %all-to-all-start.1 = ((f32[64,16,128]{2,1,0:T(8,128)}), f32[64,16,128]{2,1,0:T(8,128)S(1)}, u32[]{:S(2)}, u32[]{:S(2)}) async-start(f32[64,16,128]{2,1,0:T(8,128)} %bitcast.10), calls=%async_computation.1 | async-start | bytes 1048576 | tf_op jit(solution)/shard_map/all_to_all | solution.py:272
  44.8 4.6 %copy-start.8 = (bf16[256]{0:T(256)(128)(2,1)S(1)}, bf16[256]{0:T(256)(128)(2,1)}, u32[]{:S(2)}) copy-start(bf16[256]{0:T(256)(128)(2,1)} %param.23) | copy-start | bytes 1540
  44.8 18.2 %collective-permute-start.2 = (bf16[2,960,256]{2,1,0:T(8,128)(2,1)S(1)}, bf16[2,960,256]{2,1,0:T(8,128)(2,1)S(1)}, u32[]{:S(2)}, u32[]{:S(2)}) collective-permute-start(bf16[2,960,256]{2,1,0:T(8,128)(2,1)S(1)} %held.3.side_ref), channel_id=1, source_target_pairs={{0,4},{4,0},{1,5},{5,1},{2,6},{6,2},{3,7},{7,3},{8,12},{12,8},{9,1... | collective-permute-start | bytes 2949128 | tf_op jit(solution)/shard_map/ppermute | solution.py:192
  46.7 16.3 %collective-permute-start.3 = (bf16[2,960,256]{2,1,0:T(8,128)(2,1)S(1)}, bf16[2,960,256]{2,1,0:T(8,128)(2,1)}, u32[]{:S(2)}, u32[]{:S(2)}) collective-permute-start(bf16[2,960,256]{2,1,0:T(8,128)(2,1)S(1)} %held.3.side_ref), channel_id=1, source_target_pairs={{0,1},{1,2},{2,3},{3,0},{4,7},{5,4},{6,5},{7,6},{8,9},{9,10},{10,1... | collective-permute-start | bytes 2949128 | tf_op jit(solution)/shard_map/ppermute | solution.py:271

commit v7 on v4

--- a/solution.py
+++ b/solution.py
@@ -61,9 +61,8 @@
 
 
 def pack_kernel(
-    meta_ref, w1_ref, w2_ref, w3_ref, w4_ref, dense_ref, b1_ref, b2_ref, b3_ref, pack_ref, half_ref, bottom_ref
+    w1_ref, w2_ref, w3_ref, w4_ref, dense_ref, b1_ref, b2_ref, b3_ref, pack_ref, bottom_ref
 ):
-    core = meta_ref[3]
     tail = w1_ref[HEAD_ROWS:, :]
     pack_ref[0, 0:HEAD_ROWS, :] = w1_ref[0:HEAD_ROWS, :]
     pack_ref[1, 0:HEAD_ROWS, :] = jnp.concatenate(
@@ -82,7 +81,6 @@
         at += quarter
         half = w4_ref.shape[1] // 2
         pack_ref[h, at : at + w4_ref.shape[0], :] = w4_ref[:, h * half : (h + 1) * half]
-    half_ref[...] = pack_ref[core]
     lower = relu(mm(dense_ref[...], b1_ref[...])).astype(BF)
     middle = relu(mm(lower, b2_ref[...])).astype(BF)
     bottom_ref[...] = relu(mm(middle, b3_ref[...]))
@@ -125,7 +123,7 @@
 
 
 def top_kernel(
-    meta_ref, bags_ref, bottom_ref, last_ref, own_ref, side_ref, mirror_ref, near_ref, far_ref,
+    meta_ref, bags_ref, bottom_ref, last_ref, own_ref, side_ref, across_ref, mirror_ref,
     out_ref, in_ref, a1_ref, a2_ref, a3_ref,
 ):
     core, x = meta_ref[3], meta_ref[4]
@@ -157,7 +155,7 @@
         (x, whole(own_ref)),
         (jnp.where(core == 0, before, after), whole(side_ref)),
         (jnp.where(core == 0, after, before), whole(mirror_ref)),
-        (lax.rem(x + 2, reps), [(core, near_ref), (1 - core, far_ref)]),
+        (lax.rem(x + 2, reps), whole(across_ref)),
     )
     for owner, halves in shards:
         y = sum(mm(in_ref[h], w[0:HEAD_ROWS, :]) for h, w in halves)
@@ -223,14 +221,14 @@
     rows = pl.pallas_call(
         functools.partial(prepare_kernel, along_z),
         out_shape=jax.ShapeDtypeStruct((peers, HOT * samples), jnp.int32),
-        in_specs=[pl.BlockSpec(memory_space=pl.ANY)] * 2,
+        in_specs=[pl.BlockSpec(memory_space=pltpu.HBM)] * 2,
         out_specs=VM,
         scratch_shapes=[
             pltpu.VMEM((TAB, HOT, samples), jnp.int32),
             pltpu.VMEM((TAB, samples), jnp.int32),
             pltpu.SemaphoreType.DMA((2,)),
         ],
-        compiler_params=params(8),
+        compiler_params=params(60),
         cost_estimate=cost(1),
         name="prepare",
     )(jnp.transpose(indices, (1, 2, 0)), jnp.transpose(bag_lengths))
@@ -240,26 +238,24 @@
     beside = shifted(tables, N, 1)
     w4t = jnp.transpose(w4)
     pack_rows = HEAD_ROWS + w2.shape[0] // 2 + w3.shape[0] // 4 + w4t.shape[0]
-    pack, half, bottom = pl.pallas_call(
+    pack, bottom = pl.pallas_call(
         pack_kernel,
         out_shape=(
             jax.ShapeDtypeStruct((2, pack_rows, w2.shape[1]), BF),
-            jax.ShapeDtypeStruct((pack_rows, w2.shape[1]), BF),
             jax.ShapeDtypeStruct((samples, width), F32),
         ),
-        in_specs=[SM] + [VM] * 8,
-        out_specs=(VM, VM, VM),
-        compiler_params=params(10),
+        in_specs=[VM] * 8,
+        out_specs=(VM, VM),
+        compiler_params=params(8),
         cost_estimate=cost(3),
         name="pack",
-    )(meta, w1, w2, w3, w4t, dense, b1, b2, b3)
+    )(w1, w2, w3, w4t, dense, b1, b2, b3)
     sides = [(i, (i + 1) % reps) for i in range(reps)]
     sides += [(reps + i, reps + (i - 1) % reps) for i in range(reps)]
-    beside, bottom = lax.optimization_barrier((beside, bottom))
+    beside, pack = lax.optimization_barrier((beside, pack))
     same = jnp.stack([tables, beside])
     other = shifted(same, C, 1)
     side = lax.ppermute(pack, (C, X), sides)
-    near = shifted(half, X, 2)
     partial_bags = pl.pallas_call(
         lookup_kernel,
         out_shape=jax.ShapeDtypeStruct((peers * samples, width), F32),
@@ -271,22 +267,20 @@
             pltpu.VMEM((256, 2 * pair * tables.shape[0]), BF),
         ],
         compiler_params=params(14),
-        cost_estimate=cost(40),
+        cost_estimate=cost(1),
         name="lookup",
     )(meta, wanted, same, other)
-    side, _ = lax.optimization_barrier((side, partial_bags))
     side = held(side, 60, pl.ANY)
-    near, _ = lax.optimization_barrier((near, side))
-    near = held(near, 60, pl.ANY)
+    across = lax.ppermute(side, (C, X), sides)
     mirror = shifted(side, C, 1)
-    far = shifted(near, C, 1)
     bags = lax.all_to_all(
         partial_bags.reshape(peers, samples, width), (Y, Z), 0, 0, tiled=True
     )
+    bags = held(bags, 300, pltpu.VMEM)
     logit = pl.pallas_call(
         top_kernel,
         out_shape=jax.ShapeDtypeStruct((1, samples), F32),
-        in_specs=[SM] + [VM] * 8,
+        in_specs=[SM] + [VM] * 7,
         out_specs=VM,
         scratch_shapes=[
             pltpu.VMEM((2, samples, width), BF),
@@ -297,7 +291,7 @@
         compiler_params=params(10),
         cost_estimate=cost(5),
         name="top",
-    )(meta, bags, bottom, last.reshape(reps, 1, -1), pack, side, mirror, near, far)
+    )(meta, bags, bottom, last.reshape(reps, 1, -1), pack, side, across, mirror)
     return logit.reshape(samples)
 
 

time: 73.6 us -> 68.1 us (0.925)
  the two profiles are of different devices: /device:TPU:8 before, /device:TPU:1 now
where the time goes in v7:
time: 68.1 us; the launch traced here: 67.5 us
  starting transfers between devices  42.5 us (62%)
  waiting for transfers between devices  12 us (18%)
  Pallas kernels  10.9 us (16%)
  other arithmetic  1.15 us (2%)
  local copies, waits for them, and re-layouts  0.76 us (1%)
    all_to_all x1, starting transfers between devices, body(): wanted = lax.all_to_all(rows, (Y, Z), 0, 0, tiled=True)  14.8 us
    all_to_all x1, starting transfers between devices, body(): lax.all_to_all(partial_bags.reshape(peers, samples, width), (Y, Z), 0, 0,...  10.8 us
    ppermute x3, starting transfers between devices, shifted(): return lax.ppermute(a, axis, [(i, (i + k) % n) for i in range(n)])  10.1 us
    all_to_all x1, waiting for transfers between devices, body(): lax.all_to_all(partial_bags.reshape(peers, samples, width), (Y, Z), 0, 0,...  8.93 us
    pallas_call x1, Pallas kernels, body(): pl.pallas_call(lookup_kernel, out_shape=jax.ShapeDtypeStruct((peers * sam...  4.94 us
    ppermute x1, starting transfers between devices, body(): side = lax.ppermute(pack, (C, X), sides)  4.39 us
    pallas_call x1, Pallas kernels, body(): pl.pallas_call(top_kernel, out_shape=jax.ShapeDtypeStruct((1, samples), F...  3.92 us
    ppermute x1, starting transfers between devices, body(): across = lax.ppermute(side, (C, X), sides)  2.46 us
  transfers between devices with their start and end apart: 7, of which 3 were waited for; matrix products, arithmetic and copies ran while one was open for 2% of the time, Pallas kernels for 8%

profile of v7, /device:TPU:1, one launch (start us, length us, event | category | flops | bytes accessed | tf_op | source)
XLA Modules:
  0.0 67.5 jit_solution(5443815768275258577)
XLA Ops:
  0.0 1.6 %prepare.1 = s32[32,128]{1,0:T(8,128)} custom-call(s32[8,8,16]{2,1,0:T(8,128)} %bitcast.20, s32[8,16]{1,0:T(8,128)} %bitcast.21), custom_call_target="tpu_custom_call" | custom-call | flops 1000000000 | bytes 1048576 | tf_op jit(solution)/shard_map/prepare/pallas_call | solution.py:221
  1.6 0.1 stack.32.meta_ref
  1.7 4.8 %collective-permute-start = (bf16[2048,128]{1,0:T(8,128)(2,1)S(1)}, bf16[2048,128]{1,0:T(8,128)(2,1)}, u32[]{:S(2)}, u32[]{:S(2)}) collective-permute-start(bf16[2048,128]{1,0:T(8,128)(2,1)S(1)} %copy-done.8), channel_id=1, source_target_pairs={{0,8},{8,0},{1,9},{9,1},{2,10},{10,2},{3,11},{11,3},{4,12},{12,4},... | collective-permute-start | bytes 1572872 | tf_op jit(solution)/shard_map/ppermute | solution.py:193
  6.6 0.0 copy-start.9
  6.6 0.0 copy-start.6
  6.6 14.8 %all-to-all-start = ((s32[32,1,128]{2,1,0:T(1,128)}), s32[32,1,128]{2,1,0:T(1,128)S(1)}, u32[]{:S(2)}, u32[]{:S(2)}) async-start(s32[32,1,128]{2,1,0:T(1,128)} %bitcast.19), calls=%async_computation | async-start | bytes 32768 | tf_op jit(solution)/shard_map/all_to_all | solution.py:236
  21.4 0.0 copy-start.7
  21.4 0.1 reshape.14.last_ref
  21.5 0.5 copy-done.7
  22.1 0.4 pack.1
  22.5 0.0 collective-permute-done
  22.5 1.2 %pad_maximum_fusion.same_ref = bf16[2,2048,128]{2,1,0:T(8,128)(2,1)S(1)} fusion(bf16[1,2048,128]{2,1,0:T(8,128)(2,1)} %bitcast.12, bf16[1,2048,128]{2,1,0:T(8,128)(2,1)S(1)} %bitcast.18), kind=kLoop, calls=%fused_computation | loop fusion | flops 524288 | bytes 2097152 | tf_op jit(solution)/shard_map/stack | solution.py:256
  23.7 3.1 %collective-permute-start.1 = (bf16[2,2048,128]{2,1,0:T(8,128)(2,1)S(1)}, bf16[2,2048,128]{2,1,0:T(8,128)(2,1)S(1)}, u32[]{:S(2)}, u32[]{:S(2)}) collective-permute-start(bf16[2,2048,128]{2,1,0:T(8,128)(2,1)S(1)} %pad_maximum_fusion.same_ref), channel_id=1, source_target_pairs={{0,4},{4,0},{1,5},{5,1},{2,6},{6,2},{3,7},{7,3},{8,12},{12,8},{9,1... | collective-permute-start | bytes 3145736 | tf_op jit(solution)/shard_map/ppermute | solution.py:193
  26.8 4.4 %collective-permute-start.2 = (bf16[2,960,256]{2,1,0:T(8,128)(2,1)S(1)}, bf16[2,960,256]{2,1,0:T(8,128)(2,1)}, u32[]{:S(2)}, u32[]{:S(2)}) collective-permute-start(bf16[2,960,256]{2,1,0:T(8,128)(2,1)S(1)} %get-tuple-element.18.own_ref), channel_id=1, source_target_pairs={{0,1},{1,2},{2,3},{3,0},{4,7},{5,4},{6,5},{7,6},{8,9},{9,10},{10,1... | collective-permute-start | bytes 2949128 | tf_op jit(solution)/shard_map/ppermute | solution.py:258
  31.2 1.2 %all-to-all-done = s32[32,1,128]{2,1,0:T(1,128)S(1)} async-done(((s32[32,1,128]{2,1,0:T(1,128)}), s32[32,1,128]{2,1,0:T(1,128)S(1)}, u32[]{:S(2)}, u32[]{:S(2)}) %all-to-all-start) | async-done | bytes 16416 | tf_op jit(solution)/shard_map/all_to_all | solution.py:236
  32.4 0.0 collective-permute-done.1.other_ref
  32.4 4.9 %lookup.1 = f32[512,128]{1,0:T(8,128)} custom-call(s32[5]{0:T(128)S(1)} %stack.32.meta_ref, s32[32,128]{1,0:T(8,128)S(1)} %held.3.idx_ref, bf16[2,2048,128]{2,1,0:T(8,128)(2,1)S(1)} %pad_maximum_fusion.same_ref, bf16[2,2048,128]{2,1,0:T(8,128)(2,1)S(1)} %collective-permute-done.1.other_ref), custom_call_target="tpu_custom_call" | custom-call | flops 1000000000 | bytes 1048576 | tf_op jit(solution)/shard_map/lookup/pallas_call | solution.py:259
  37.3 10.8 %all-to-all-start.1 = ((f32[32,16,128]{2,1,0:T(8,128)}), f32[32,16,128]{2,1,0:T(8,128)S(1)}, u32[]{:S(2)}, u32[]{:S(2)}) async-start(f32[32,16,128]{2,1,0:T(8,128)} %bitcast.13), calls=%async_computation.1 | async-start | bytes 524288 | tf_op jit(solution)/shard_map/all_to_all | solution.py:276
  48.1 0.0 collective-permute-done.2.in_ref
  48.1 2.5 %collective-permute-start.3 = (bf16[2,960,256]{2,1,0:T(8,128)(2,1)}, bf16[2,960,256]{2,1,0:T(8,128)(2,1)}, u32[]{:S(2)}, u32[]{:S(2)}) collective-permute-start(bf16[2,960,256]{2,1,0:T(8,128)(2,1)} %held.5.side_ref), channel_id=1, source_target_pairs={{0,1},{1,2},{2,3},{3,0},{4,7},{5,4},{6,5},{7,6},{8,9},{9,10},{10,1... | collective-permute-start | bytes 2949128 | tf_op jit(solution)/shard_map/ppermute | solution.py:274
  50.6 2.2 %collective-permute-start.4 = (bf16[2,960,256]{2,1,0:T(8,128)(2,1)}, bf16[2,960,256]{2,1,0:T(8,128)(2,1)}, u32[]{:S(2)}, u32[]{:S(2)}) collective-permute-start(bf16[2,960,256]{2,1,0:T(8,128)(2,1)} %held.5.side_ref), channel_id=1, source_target_pairs={{0,4},{4,0},{1,5},{5,1},{2,6},{6,2},{3,7},{7,3},{8,12},{12,8},{9,1... | collective-permute-start | bytes 2949128 | tf_op jit(solution)/shard_map/ppermute | solution.py:193
  52.8 8.9 %all-to-all-done.1.in_ref = f32[32,16,128]{2,1,0:T(8,128)S(1)} async-done(((f32[32,16,128]{2,1,0:T(8,128)}), f32[32,16,128]{2,1,0:T(8,128)S(1)}, u32[]{:S(2)}, u32[]{:S(2)}) %all-to-all-start.1) | async-done | bytes 262176 | tf_op jit(solution)/shard_map/all_to_all | solution.py:276
  61.7 1.9 %collective-permute-done.3.across_ref = bf16[2,960,256]{2,1,0:T(8,128)(2,1)} collective-permute-done((bf16[2,960,256]{2,1,0:T(8,128)(2,1)}, bf16[2,960,256]{2,1,0:T(8,128)(2,1)}, u32[]{:S(2)}, u32[]{:S(2)}) %collective-permute-start.3) | collective-permute-done | bytes 983072 | tf_op jit(solution)/shard_map/ppermute | solution.py:274
  63.6 3.9 %top.1 = f32[1,16]{1,0:T(1,128)} custom-call(s32[5]{0:T(128)S(1)} %stack.32.meta_ref, f32[32,16,128]{2,1,0:T(8,128)S(1)} %held.4.bags_ref, f32[16,128]{1,0:T(8,128)S(1)} %get-tuple-element.17.bottom_ref, bf16[4,1,64]{2,1,0:T(2,128)(2,1)S(1)} %reshape.14.last_ref, bf16[2,960,256]{2,1,0:T(8,128)(2,1)S(1)} %get-tuple-element.18.own_ref, ...), custom_call_target="tpu_custom_call" | custom-call | flops 5000000000 | bytes 1048576 | tf_op jit(solution)/shard_map/top/pallas_call | solution.py:280
  (20 shorter events, 0.0 us)
Async XLA Ops:
  0.0 1.7 %copy-start.8 = (bf16[2048,128]{1,0:T(8,128)(2,1)S(1)}, bf16[2048,128]{1,0:T(8,128)(2,1)}, u32[]{:S(2)}) copy-start(bf16[2048,128]{1,0:T(8,128)(2,1)} %param.12) | copy-start | bytes 1572868
  0.0 21.5 %copy-start = (bf16[1024,256]{1,0:T(8,128)(2,1)S(1)}, bf16[1024,256]{1,0:T(8,128)(2,1)}, u32[]{:S(2)}) copy-start(bf16[1024,256]{1,0:T(8,128)(2,1)} %w2_ref.1) | copy-start | bytes 1572868
  0.0 21.5 %copy-start.1 = (bf16[1024,128]{1,0:T(8,128)(2,1)S(1)}, bf16[1024,128]{1,0:T(8,128)(2,1)}, u32[]{:S(2)}) copy-start(bf16[1024,128]{1,0:T(8,128)(2,1)} %w3_ref.1) | copy-start | bytes 786436
  0.0 21.5 %copy-start.2 = (bf16[512,256]{1,0:T(8,128)(2,1)S(1)}, bf16[512,256]{1,0:T(8,128)(2,1)}, u32[]{:S(2)}) copy-start(bf16[512,256]{1,0:T(8,128)(2,1)} %b2_ref.1) | copy-start | bytes 786436
  0.0 21.5 %copy-start.3 = (bf16[164,256]{1,0:T(8,128)(2,1)S(1)}, bf16[164,256]{1,0:T(8,128)(2,1)}, u32[]{:S(2)}) copy-start(bf16[164,256]{1,0:T(8,128)(2,1)} %w1_ref.1) | copy-start | bytes 251908
  0.0 21.5 %copy-start.4 = (bf16[512,64]{0,1:T(8,128)(2,1)S(1)}, bf16[512,64]{0,1:T(8,128)(2,1)}, u32[]{:S(2)}) copy-start(bf16[512,64]{0,1:T(8,128)(2,1)} %param.22) | copy-start | bytes 196612
  0.0 21.5 %copy-start.5 = (bf16[256,128]{1,0:T(8,128)(2,1)S(1)}, bf16[256,128]{1,0:T(8,128)(2,1)}, u32[]{:S(2)}) copy-start(bf16[256,128]{1,0:T(8,128)(2,1)} %b3_ref.1) | copy-start | bytes 196612
  1.7 20.8 %collective-permute-start = (bf16[2048,128]{1,0:T(8,128)(2,1)S(1)}, bf16[2048,128]{1,0:T(8,128)(2,1)}, u32[]{:S(2)}, u32[]{:S(2)}) collective-permute-start(bf16[2048,128]{1,0:T(8,128)(2,1)S(1)} %copy-done.8), channel_id=1, source_target_pairs={{0,8},{8,0},{1,9},{9,1},{2,10},{10,2},{3,11},{11,3},{4,12},{12,4},... | collective-permute-start | bytes 1572872 | tf_op jit(solution)/shard_map/ppermute | solution.py:193
  6.6 14.8 %copy-start.9 = (bf16[256]{0:T(256)(128)(2,1)S(1)}, bf16[256]{0:T(256)(128)(2,1)}, u32[]{:S(2)}) copy-start(bf16[256]{0:T(256)(128)(2,1)} %param.23) | copy-start | bytes 1540
  6.6 15.0 %copy-start.6 = (bf16[13,512]{1,0:T(8,128)(2,1)S(1)}, bf16[13,512]{1,0:T(8,128)(2,1)}, u32[]{:S(2)}) copy-start(bf16[13,512]{1,0:T(8,128)(2,1)} %b1_ref.1) | copy-start | bytes 39940
  6.6 25.8 %all-to-all-start = ((s32[32,1,128]{2,1,0:T(1,128)}), s32[32,1,128]{2,1,0:T(1,128)S(1)}, u32[]{:S(2)}, u32[]{:S(2)}) async-start(s32[32,1,128]{2,1,0:T(1,128)} %bitcast.19), calls=%async_computation | async-start | bytes 32768 | tf_op jit(solution)/shard_map/all_to_all | solution.py:236
  21.4 0.7 %copy-start.7 = (bf16[16,13]{1,0:T(8,128)(2,1)S(1)}, bf16[16,13]{1,0:T(8,128)(2,1)}, u32[]{:S(2)}) copy-start(bf16[16,13]{1,0:T(8,128)(2,1)} %dense_ref.1) | copy-start | bytes 1252
  23.7 8.7 %collective-permute-start.1 = (bf16[2,2048,128]{2,1,0:T(8,128)(2,1)S(1)}, bf16[2,2048,128]{2,1,0:T(8,128)(2,1)S(1)}, u32[]{:S(2)}, u32[]{:S(2)}) collective-permute-start(bf16[2,2048,128]{2,1,0:T(8,128)(2,1)S(1)} %pad_maximum_fusion.same_ref), channel_id=1, source_target_pairs={{0,4},{4,0},{1,5},{5,1},{2,6},{6,2},{3,7},{7,3},{8,12},{12,8},{9,1... | collective-permute-start | bytes 3145736 | tf_op jit(solution)/shard_map/ppermute | solution.py:193
  26.8 21.3 %collective-permute-start.2 = (bf16[2,960,256]{2,1,0:T(8,128)(2,1)S(1)}, bf16[2,960,256]{2,1,0:T(8,128)(2,1)}, u32[]{:S(2)}, u32[]{:S(2)}) collective-permute-start(bf16[2,960,256]{2,1,0:T(8,128)(2,1)S(1)} %get-tuple-element.18.own_ref), channel_id=1, source_target_pairs={{0,1},{1,2},{2,3},{3,0},{4,7},{5,4},{6,5},{7,6},{8,9},{9,10},{10,1... | collective-permute-start | bytes 2949128 | tf_op jit(solution)/shard_map/ppermute | solution.py:258
  37.3 24.4 %all-to-all-start.1 = ((f32[32,16,128]{2,1,0:T(8,128)}), f32[32,16,128]{2,1,0:T(8,128)S(1)}, u32[]{:S(2)}, u32[]{:S(2)}) async-start(f32[32,16,128]{2,1,0:T(8,128)} %bitcast.13), calls=%async_computation.1 | async-start | bytes 524288 | tf_op jit(solution)/shard_map/all_to_all | solution.py:276
  48.1 15.5 %collective-permute-start.3 = (bf16[2,960,256]{2,1,0:T(8,128)(2,1)}, bf16[2,960,256]{2,1,0:T(8,128)(2,1)}, u32[]{:S(2)}, u32[]{:S(2)}) collective-permute-start(bf16[2,960,256]{2,1,0:T(8,128)(2,1)} %held.5.side_ref), channel_id=1, source_target_pairs={{0,1},{1,2},{2,3},{3,0},{4,7},{5,4},{6,5},{7,6},{8,9},{9,10},{10,1... | collective-permute-start | bytes 2949128 | tf_op jit(solution)/shard_map/ppermute | solution.py:274
  50.6 13.0 %collective-permute-start.4 = (bf16[2,960,256]{2,1,0:T(8,128)(2,1)}, bf16[2,960,256]{2,1,0:T(8,128)(2,1)}, u32[]{:S(2)}, u32[]{:S(2)}) collective-permute-start(bf16[2,960,256]{2,1,0:T(8,128)(2,1)} %held.5.side_ref), channel_id=1, source_target_pairs={{0,4},{4,0},{1,5},{5,1},{2,6},{6,2},{3,7},{7,3},{8,12},{12,8},{9,1... | collective-permute-start | bytes 2949128 | tf_op jit(solution)/shard_map/ppermute | solution.py:193

commit v8 on v6

--- a/solution.py
+++ b/solution.py
@@ -122,7 +122,7 @@
 
 
 def top_kernel(
-    meta_ref, bags_ref, bottom_ref, last_ref, own_ref, side_ref, mirror_ref, across_ref,
+    meta_ref, bags_ref, bottom_ref, last_ref, own_ref, side_ref, across_ref, mirror_ref,
     out_ref, in_ref, a1_ref, a2_ref, a3_ref,
 ):
     core, x = meta_ref[2], meta_ref[3]
@@ -267,11 +267,12 @@
         name="lookup",
     )(meta, wanted, tables, other)
     side = held(side, 60, pltpu.VMEM)
+    across = lax.ppermute(side, (C, X), sides)
     mirror = shifted(side, C, 1)
-    across = lax.ppermute(side, (C, X), sides)
     bags = lax.all_to_all(
         partial_bags.reshape(peers, samples, width), (Y, Z), 0, 0, tiled=True
     )
+    bags = held(bags, 15, pltpu.VMEM)
     logit = pl.pallas_call(
         top_kernel,
         out_shape=jax.ShapeDtypeStruct((1, samples), F32),
@@ -286,7 +287,7 @@
         compiler_params=params(10),
         cost_estimate=cost(5),
         name="top",
-    )(meta, bags, bottom, last.reshape(reps, 1, -1), pack, side, mirror, across)
+    )(meta, bags, bottom, last.reshape(reps, 1, -1), pack, side, across, mirror)
     return logit.reshape(samples)
 
 

time: 67 us -> 67.2 us (level)
  no operation moved by 1% of the time
where the time goes in v8:
time: 67.2 us; the launch traced here: 66.5 us
  starting transfers between devices  38.9 us (58%)
  waiting for transfers between devices  16.4 us (24%)
  Pallas kernels  10.8 us (16%)
    all_to_all x1, starting transfers between devices, body(): wanted = lax.all_to_all(rows, (Y, Z), 0, 0, tiled=True)  17.3 us
    all_to_all x1, waiting for transfers between devices, body(): lax.all_to_all(partial_bags.reshape(peers, samples, width), (Y, Z), 0, 0,...  13.6 us
    all_to_all x1, starting transfers between devices, body(): lax.all_to_all(partial_bags.reshape(peers, samples, width), (Y, Z), 0, 0,...  9.62 us
    pallas_call x1, Pallas kernels, body(): pl.pallas_call(lookup_kernel, out_shape=jax.ShapeDtypeStruct((peers * sam...  5.5 us
    ppermute x2, starting transfers between devices, shifted(): return lax.ppermute(a, axis, [(i, (i + k) % n) for i in range(n)])  5.15 us
    ppermute x1, starting transfers between devices, body(): side = lax.ppermute(pack, (C, X), sides)  4.39 us
    pallas_call x1, Pallas kernels, body(): pl.pallas_call(top_kernel, out_shape=jax.ShapeDtypeStruct((1, samples), F...  3.34 us
    all_to_all x1, waiting for transfers between devices, body(): wanted = lax.all_to_all(rows, (Y, Z), 0, 0, tiled=True)  2.8 us
  transfers between devices with their start and end apart: 6, of which 2 were waited for; matrix products, arithmetic and copies ran while one was open for 0% of the time, Pallas kernels for 9%

profile of v8, /device:TPU:1, one launch (start us, length us, event | category | flops | bytes accessed | tf_op | source)
XLA Modules:
  0.0 66.5 jit_solution(8734260461959954465)
XLA Ops:
  0.0 0.0 copy-start.3
  0.0 0.0 copy-start.5
  0.0 0.0 copy-start.6
  0.0 1.6 %prepare.1 = s32[64,128]{1,0:T(8,128)} custom-call(s32[8,8,16]{2,1,0:T(8,128)} %bitcast.16, s32[8,16]{1,0:T(8,128)} %bitcast.17), custom_call_target="tpu_custom_call" | custom-call | flops 1000000000 | bytes 1048576 | tf_op jit(solution)/shard_map/prepare/pallas_call | solution.py:219
  1.6 0.0 copy-start.4
  1.6 0.1 pad_add_fusion.meta_ref
  1.7 17.3 %all-to-all-start = ((s32[64,1,128]{2,1,0:T(1,128)}), s32[64,1,128]{2,1,0:T(1,128)S(1)}, u32[]{:S(2)}, u32[]{:S(2)}) async-start(s32[64,1,128]{2,1,0:T(1,128)} %bitcast.15), calls=%async_computation | async-start | bytes 65536 | tf_op jit(solution)/shard_map/all_to_all | solution.py:234
  19.0 0.0 copy-done
  19.0 0.0 copy-done.1
  19.1 0.4 pack.1
  19.5 3.0 %collective-permute-start = (bf16[2048,128]{1,0:T(8,128)(2,1)}, bf16[2048,128]{1,0:T(8,128)(2,1)S(1)}, u32[]{:S(2)}, u32[]{:S(2)}) collective-permute-start(bf16[2048,128]{1,0:T(8,128)(2,1)} %own_ref), channel_id=1, source_target_pairs={{0,4},{4,0},{1,5},{5,1},{2,6},{6,2},{3,7},{7,3},{8,12},{12,8},{9,1... | collective-permute-start | bytes 1572872 | tf_op jit(solution)/shard_map/ppermute | solution.py:192
  22.5 4.4 %collective-permute-start.1 = (bf16[2,960,256]{2,1,0:T(8,128)(2,1)S(1)}, bf16[2,960,256]{2,1,0:T(8,128)(2,1)S(1)}, u32[]{:S(2)}, u32[]{:S(2)}) collective-permute-start(bf16[2,960,256]{2,1,0:T(8,128)(2,1)S(1)} %get-tuple-element.18.own_ref), channel_id=1, source_target_pairs={{0,1},{1,2},{2,3},{3,0},{4,7},{5,4},{6,5},{7,6},{8,9},{9,10},{10,1... | collective-permute-start | bytes 2949128 | tf_op jit(solution)/shard_map/ppermute | solution.py:254
  26.9 0.1 reshape.14.last_ref
  27.0 2.8 %all-to-all-done = s32[64,1,128]{2,1,0:T(1,128)S(1)} async-done(((s32[64,1,128]{2,1,0:T(1,128)}), s32[64,1,128]{2,1,0:T(1,128)S(1)}, u32[]{:S(2)}, u32[]{:S(2)}) %all-to-all-start) | async-done | bytes 32800 | tf_op jit(solution)/shard_map/all_to_all | solution.py:234
  29.8 0.0 collective-permute-done.other_ref
  29.8 5.5 %lookup.1 = f32[1024,128]{1,0:T(8,128)} custom-call(s32[4]{0:T(128)S(1)} %pad_add_fusion.meta_ref, s32[64,128]{1,0:T(8,128)S(1)} %held.3.idx_ref, bf16[2048,128]{1,0:T(8,128)(2,1)} %own_ref, bf16[2048,128]{1,0:T(8,128)(2,1)S(1)} %collective-permute-done.other_ref), custom_call_target="tpu_custom_call" | custom-call | flops 40000000000 | bytes 1048576 | tf_op jit(solution)/shard_map/lookup/pallas_call | solution.py:255
  35.3 9.6 %all-to-all-start.1 = ((f32[64,16,128]{2,1,0:T(8,128)}), f32[64,16,128]{2,1,0:T(8,128)S(1)}, u32[]{:S(2)}, u32[]{:S(2)}) async-start(f32[64,16,128]{2,1,0:T(8,128)} %bitcast.10), calls=%async_computation.1 | async-start | bytes 1048576 | tf_op jit(solution)/shard_map/all_to_all | solution.py:272
  44.9 0.0 collective-permute-done.1.in_ref
  44.9 2.5 %collective-permute-start.2 = (bf16[2,960,256]{2,1,0:T(8,128)(2,1)S(1)}, bf16[2,960,256]{2,1,0:T(8,128)(2,1)S(1)}, u32[]{:S(2)}, u32[]{:S(2)}) collective-permute-start(bf16[2,960,256]{2,1,0:T(8,128)(2,1)S(1)} %held.5.side_ref), channel_id=1, source_target_pairs={{0,1},{1,2},{2,3},{3,0},{4,7},{5,4},{6,5},{7,6},{8,9},{9,10},{10,1... | collective-permute-start | bytes 2949128 | tf_op jit(solution)/shard_map/ppermute | solution.py:270
  47.4 2.2 %collective-permute-start.3 = (bf16[2,960,256]{2,1,0:T(8,128)(2,1)S(1)}, bf16[2,960,256]{2,1,0:T(8,128)(2,1)}, u32[]{:S(2)}, u32[]{:S(2)}) collective-permute-start(bf16[2,960,256]{2,1,0:T(8,128)(2,1)S(1)} %held.5.side_ref), channel_id=1, source_target_pairs={{0,4},{4,0},{1,5},{5,1},{2,6},{6,2},{3,7},{7,3},{8,12},{12,8},{9,1... | collective-permute-start | bytes 2949128 | tf_op jit(solution)/shard_map/ppermute | solution.py:192
  49.6 13.6 %all-to-all-done.1.in_ref = f32[64,16,128]{2,1,0:T(8,128)S(1)} async-done(((f32[64,16,128]{2,1,0:T(8,128)}), f32[64,16,128]{2,1,0:T(8,128)S(1)}, u32[]{:S(2)}, u32[]{:S(2)}) %all-to-all-start.1) | async-done | bytes 524320 | tf_op jit(solution)/shard_map/all_to_all | solution.py:272
  63.2 0.0 collective-permute-done.2.across_ref
  63.2 0.0 collective-permute-done.3.mirror_ref
  63.2 3.3 %top.1 = f32[1,16]{1,0:T(1,128)} custom-call(s32[4]{0:T(128)S(1)} %pad_add_fusion.meta_ref, f32[64,16,128]{2,1,0:T(8,128)S(1)} %held.4.bags_ref, f32[16,128]{1,0:T(8,128)S(1)} %get-tuple-element.17.bottom_ref, bf16[4,1,64]{2,1,0:T(2,128)(2,1)S(1)} %reshape.14.last_ref, bf16[2,960,256]{2,1,0:T(8,128)(2,1)S(1)} %get-tuple-element.18.own_ref, ...), custom_call_target="tpu_custom_call" | custom-call | flops 5000000000 | bytes 1048576 | tf_op jit(solution)/shard_map/top/pallas_call | solution.py:276
  (15 shorter events, 0.0 us)
Async XLA Ops:
  0.0 19.0 %copy-start = (bf16[1024,256]{1,0:T(8,128)(2,1)S(1)}, bf16[1024,256]{1,0:T(8,128)(2,1)}, u32[]{:S(2)}) copy-start(bf16[1024,256]{1,0:T(8,128)(2,1)} %w2_ref.1) | copy-start | bytes 1572868
  0.0 19.0 %copy-start.1 = (bf16[1024,128]{1,0:T(8,128)(2,1)S(1)}, bf16[1024,128]{1,0:T(8,128)(2,1)}, u32[]{:S(2)}) copy-start(bf16[1024,128]{1,0:T(8,128)(2,1)} %w3_ref.1) | copy-start | bytes 786436
  0.0 19.0 %copy-start.2 = (bf16[512,256]{1,0:T(8,128)(2,1)S(1)}, bf16[512,256]{1,0:T(8,128)(2,1)}, u32[]{:S(2)}) copy-start(bf16[512,256]{1,0:T(8,128)(2,1)} %b2_ref.1) | copy-start | bytes 786436
  0.0 19.0 %copy-start.3 = (bf16[164,256]{1,0:T(8,128)(2,1)S(1)}, bf16[164,256]{1,0:T(8,128)(2,1)}, u32[]{:S(2)}) copy-start(bf16[164,256]{1,0:T(8,128)(2,1)} %w1_ref.1) | copy-start | bytes 251908
  0.0 19.0 %copy-start.5 = (bf16[256,128]{1,0:T(8,128)(2,1)S(1)}, bf16[256,128]{1,0:T(8,128)(2,1)}, u32[]{:S(2)}) copy-start(bf16[256,128]{1,0:T(8,128)(2,1)} %b3_ref.1) | copy-start | bytes 196612
  0.0 19.0 %copy-start.6 = (bf16[13,512]{1,0:T(8,128)(2,1)S(1)}, bf16[13,512]{1,0:T(8,128)(2,1)}, u32[]{:S(2)}) copy-start(bf16[13,512]{1,0:T(8,128)(2,1)} %b1_ref.1) | copy-start | bytes 39940
  1.6 17.4 %copy-start.4 = (bf16[512,64]{0,1:T(8,128)(2,1)S(1)}, bf16[512,64]{0,1:T(8,128)(2,1)}, u32[]{:S(2)}) copy-start(bf16[512,64]{0,1:T(8,128)(2,1)} %param.22) | copy-start | bytes 196612
  1.7 17.4 %copy-start.7 = (bf16[16,13]{1,0:T(8,128)(2,1)S(1)}, bf16[16,13]{1,0:T(8,128)(2,1)}, u32[]{:S(2)}) copy-start(bf16[16,13]{1,0:T(8,128)(2,1)} %dense_ref.1) | copy-start | bytes 1252
  1.7 28.1 %all-to-all-start = ((s32[64,1,128]{2,1,0:T(1,128)}), s32[64,1,128]{2,1,0:T(1,128)S(1)}, u32[]{:S(2)}, u32[]{:S(2)}) async-start(s32[64,1,128]{2,1,0:T(1,128)} %bitcast.15), calls=%async_computation | async-start | bytes 65536 | tf_op jit(solution)/shard_map/all_to_all | solution.py:234
  19.5 7.4 %copy-start.8 = (bf16[256]{0:T(256)(128)(2,1)S(1)}, bf16[256]{0:T(256)(128)(2,1)}, u32[]{:S(2)}) copy-start(bf16[256]{0:T(256)(128)(2,1)} %param.23) | copy-start | bytes 1540
  19.5 10.3 %collective-permute-start = (bf16[2048,128]{1,0:T(8,128)(2,1)}, bf16[2048,128]{1,0:T(8,128)(2,1)S(1)}, u32[]{:S(2)}, u32[]{:S(2)}) collective-permute-start(bf16[2048,128]{1,0:T(8,128)(2,1)} %own_ref), channel_id=1, source_target_pairs={{0,4},{4,0},{1,5},{5,1},{2,6},{6,2},{3,7},{7,3},{8,12},{12,8},{9,1... | collective-permute-start | bytes 1572872 | tf_op jit(solution)/shard_map/ppermute | solution.py:192
  22.5 22.4 %collective-permute-start.1 = (bf16[2,960,256]{2,1,0:T(8,128)(2,1)S(1)}, bf16[2,960,256]{2,1,0:T(8,128)(2,1)S(1)}, u32[]{:S(2)}, u32[]{:S(2)}) collective-permute-start(bf16[2,960,256]{2,1,0:T(8,128)(2,1)S(1)} %get-tuple-element.18.own_ref), channel_id=1, source_target_pairs={{0,1},{1,2},{2,3},{3,0},{4,7},{5,4},{6,5},{7,6},{8,9},{9,10},{10,1... | collective-permute-start | bytes 2949128 | tf_op jit(solution)/shard_map/ppermute | solution.py:254
  35.3 27.9 %all-to-all-start.1 = ((f32[64,16,128]{2,1,0:T(8,128)}), f32[64,16,128]{2,1,0:T(8,128)S(1)}, u32[]{:S(2)}, u32[]{:S(2)}) async-start(f32[64,16,128]{2,1,0:T(8,128)} %bitcast.10), calls=%async_computation.1 | async-start | bytes 1048576 | tf_op jit(solution)/shard_map/all_to_all | solution.py:272
  44.9 18.3 %collective-permute-start.2 = (bf16[2,960,256]{2,1,0:T(8,128)(2,1)S(1)}, bf16[2,960,256]{2,1,0:T(8,128)(2,1)S(1)}, u32[]{:S(2)}, u32[]{:S(2)}) collective-permute-start(bf16[2,960,256]{2,1,0:T(8,128)(2,1)S(1)} %held.5.side_ref), channel_id=1, source_target_pairs={{0,1},{1,2},{2,3},{3,0},{4,7},{5,4},{6,5},{7,6},{8,9},{9,10},{10,1... | collective-permute-start | bytes 2949128 | tf_op jit(solution)/shard_map/ppermute | solution.py:270
  47.4 15.8 %collective-permute-start.3 = (bf16[2,960,256]{2,1,0:T(8,128)(2,1)S(1)}, bf16[2,960,256]{2,1,0:T(8,128)(2,1)}, u32[]{:S(2)}, u32[]{:S(2)}) collective-permute-start(bf16[2,960,256]{2,1,0:T(8,128)(2,1)S(1)} %held.5.side_ref), channel_id=1, source_target_pairs={{0,4},{4,0},{1,5},{5,1},{2,6},{6,2},{3,7},{7,3},{8,12},{12,8},{9,1... | collective-permute-start | bytes 2949128 | tf_op jit(solution)/shard_map/ppermute | solution.py:192

commit v9 on v8

--- a/solution.py
+++ b/solution.py
@@ -61,7 +61,7 @@
 
 
 def pack_kernel(
-    w1_ref, w2_ref, w3_ref, w4_ref, dense_ref, b1_ref, b2_ref, b3_ref, pack_ref, bottom_ref
+    w1_ref, w2_ref, w3_ref, w4_ref, dense_ref, b1_ref, b2_ref, b3_ref, table_ref, pack_ref, bottom_ref, keep_ref
 ):
     tail = w1_ref[HEAD_ROWS:, :]
     pack_ref[0, 0:HEAD_ROWS, :] = w1_ref[0:HEAD_ROWS, :]
@@ -84,6 +84,7 @@
     lower = relu(mm(dense_ref[...], b1_ref[...])).astype(BF)
     middle = relu(mm(lower, b2_ref[...])).astype(BF)
     bottom_ref[...] = relu(mm(middle, b3_ref[...]))
+    keep_ref[...] = table_ref[...]
 
 
 def lookup_kernel(meta_ref, idx_ref, own_ref, other_ref, out_ref, code_ref, lo_ref, count_ref):
@@ -235,18 +236,19 @@
     wanted = held(wanted, 60, pltpu.VMEM)
     w4t = jnp.transpose(w4)
     pack_rows = HEAD_ROWS + w2.shape[0] // 2 + w3.shape[0] // 4 + w4t.shape[0]
-    pack, bottom = pl.pallas_call(
+    pack, bottom, kept = pl.pallas_call(
         pack_kernel,
         out_shape=(
             jax.ShapeDtypeStruct((2, pack_rows, w2.shape[1]), BF),
             jax.ShapeDtypeStruct((samples, width), F32),
+            jax.ShapeDtypeStruct(tables.shape, BF),
         ),
-        in_specs=[VM] * 8,
-        out_specs=(VM, VM),
+        in_specs=[VM] * 9,
+        out_specs=(VM, VM, VM),
         compiler_params=params(8),
         cost_estimate=cost(3),
         name="pack",
-    )(w1, w2, w3, w4t, dense, b1, b2, b3)
+    )(w1, w2, w3, w4t, dense, b1, b2, b3, tables)
     sides = [(i, (i + 1) % reps) for i in range(reps)]
     sides += [(reps + i, reps + (i - 1) % reps) for i in range(reps)]
     tables, pack = lax.optimization_barrier((tables, pack))
@@ -265,7 +267,7 @@
         compiler_params=params(14),
         cost_estimate=cost(40),
         name="lookup",
-    )(meta, wanted, tables, other)
+    )(meta, wanted, kept, other)
     side = held(side, 60, pltpu.VMEM)
     across = lax.ppermute(side, (C, X), sides)
     mirror = shifted(side, C, 1)

time: 67.2 us -> 68.6 us (1.021)
  local copies, waits for them, and re-layouts: 0.12 us -> 1.96 us
  starting transfers between devices: 38.9 us -> 39.7 us
  waiting for transfers between devices: 16.4 us -> 15.7 us
    unnamed x18 -> x24, local copies, waits for them, and re-layouts: 0.04 us -> 1.88 us
    all_to_all x1, waiting for transfers between devices: 2.8 us -> 2.01 us  [body(): wanted = lax.all_to_all(rows, (Y, Z), 0, 0, tiled=True)]
    all_to_all x1, starting transfers between devices: 9.62 us -> 10.4 us  [body(): lax.all_to_all(partial_bags.reshape(peers, samples, width), (Y, Z), 0, 0,...]
  transfers between devices with their start and end apart: 6 -> 6, of which waited for: 2 -> 2; matrix products, arithmetic and copies ran while one was open for 0% -> 0% of each run, Pallas kernels for 9% -> 8%
where the time goes in v9:
time: 68.6 us; the launch traced here: 68 us
  starting transfers between devices  39.7 us (58%)
  waiting for transfers between devices  15.7 us (23%)
  Pallas kernels  10.4 us (15%)
  local copies, waits for them, and re-layouts  1.96 us (3%)
    all_to_all x1, starting transfers between devices, body(): wanted = lax.all_to_all(rows, (Y, Z), 0, 0, tiled=True)  17.3 us
    all_to_all x1, waiting for transfers between devices, body(): lax.all_to_all(partial_bags.reshape(peers, samples, width), (Y, Z), 0, 0,...  13.6 us
    all_to_all x1, starting transfers between devices, body(): lax.all_to_all(partial_bags.reshape(peers, samples, width), (Y, Z), 0, 0,...  10.4 us
    ppermute x2, starting transfers between devices, shifted(): return lax.ppermute(a, axis, [(i, (i + k) % n) for i in range(n)])  5.13 us
    pallas_call x1, Pallas kernels, body(): pl.pallas_call(lookup_kernel, out_shape=jax.ShapeDtypeStruct((peers * sam...  4.99 us
    ppermute x1, starting transfers between devices, body(): side = lax.ppermute(pack, (C, X), sides)  4.39 us
    pallas_call x1, Pallas kernels, body(): pl.pallas_call(top_kernel, out_shape=jax.ShapeDtypeStruct((1, samples), F...  3.34 us
    ppermute x1, starting transfers between devices, body(): across = lax.ppermute(side, (C, X), sides)  2.47 us
  transfers between devices with their start and end apart: 6, of which 2 were waited for; matrix products, arithmetic and copies ran while one was open for 0% of the time, Pallas kernels for 8%

profile of v9, /device:TPU:1, one launch (start us, length us, event | category | flops | bytes accessed | tf_op | source)
XLA Modules:
  0.0 68.0 jit_solution(13821673580469843446)
XLA Ops:
  0.0 0.0 copy-start.3
  0.0 0.0 copy-start.4
  0.0 0.0 copy-start.6
  0.0 1.6 %prepare.1 = s32[64,128]{1,0:T(8,128)} custom-call(s32[8,8,16]{2,1,0:T(8,128)} %bitcast.16, s32[8,16]{1,0:T(8,128)} %bitcast.17), custom_call_target="tpu_custom_call" | custom-call | flops 1000000000 | bytes 1048576 | tf_op jit(solution)/shard_map/prepare/pallas_call | solution.py:220
  1.7 0.0 copy-start.5
  1.7 0.1 pad_add_fusion.meta_ref
  1.8 17.3 %all-to-all-start = ((s32[64,1,128]{2,1,0:T(1,128)}), s32[64,1,128]{2,1,0:T(1,128)S(1)}, u32[]{:S(2)}, u32[]{:S(2)}) async-start(s32[64,1,128]{2,1,0:T(1,128)} %bitcast.15), calls=%async_computation | async-start | bytes 65536 | tf_op jit(solution)/shard_map/all_to_all | solution.py:235
  19.1 0.4 pack.1
  19.6 0.8 %copy-done.9 = bf16[2048,128]{1,0:T(8,128)(2,1)} copy-done((bf16[2048,128]{1,0:T(8,128)(2,1)}, bf16[2048,128]{1,0:T(8,128)(2,1)S(1)}, u32[]{:S(2)}) %copy-start.9) | copy-done | bytes 524312
  20.4 3.0 %collective-permute-start = (bf16[2048,128]{1,0:T(8,128)(2,1)S(1)}, bf16[2048,128]{1,0:T(8,128)(2,1)S(1)}, u32[]{:S(2)}, u32[]{:S(2)}) collective-permute-start(bf16[2048,128]{1,0:T(8,128)(2,1)S(1)} %copy-done.1), channel_id=1, source_target_pairs={{0,4},{4,0},{1,5},{5,1},{2,6},{6,2},{3,7},{7,3},{8,12},{12,8},{9,1... | collective-permute-start | bytes 1572872 | tf_op jit(solution)/shard_map/ppermute | solution.py:193
  23.4 4.4 %collective-permute-start.1 = (bf16[2,960,256]{2,1,0:T(8,128)(2,1)S(1)}, bf16[2,960,256]{2,1,0:T(8,128)(2,1)S(1)}, u32[]{:S(2)}, u32[]{:S(2)}) collective-permute-start(bf16[2,960,256]{2,1,0:T(8,128)(2,1)S(1)} %get-tuple-element.20.own_ref), channel_id=1, source_target_pairs={{0,1},{1,2},{2,3},{3,0},{4,7},{5,4},{6,5},{7,6},{8,9},{9,10},{10,1... | collective-permute-start | bytes 2949128 | tf_op jit(solution)/shard_map/ppermute | solution.py:256
  27.8 0.1 reshape.14.last_ref
  27.8 2.0 %all-to-all-done = s32[64,1,128]{2,1,0:T(1,128)S(1)} async-done(((s32[64,1,128]{2,1,0:T(1,128)}), s32[64,1,128]{2,1,0:T(1,128)S(1)}, u32[]{:S(2)}, u32[]{:S(2)}) %all-to-all-start) | async-done | bytes 32800 | tf_op jit(solution)/shard_map/all_to_all | solution.py:235
  29.9 0.0 collective-permute-done.other_ref
  29.9 1.0 %copy-done.10 = bf16[2048,128]{1,0:T(8,128)(2,1)S(1)} copy-done((bf16[2048,128]{1,0:T(8,128)(2,1)S(1)}, bf16[2048,128]{1,0:T(8,128)(2,1)}, u32[]{:S(2)}) %copy-start.10) | copy-done | bytes 524312
  30.9 5.0 %lookup.1 = f32[1024,128]{1,0:T(8,128)} custom-call(s32[4]{0:T(128)S(1)} %pad_add_fusion.meta_ref, s32[64,128]{1,0:T(8,128)S(1)} %held.3.idx_ref, bf16[2048,128]{1,0:T(8,128)(2,1)S(1)} %copy-done.10, bf16[2048,128]{1,0:T(8,128)(2,1)S(1)} %collective-permute-done.other_ref), custom_call_target="tpu_custom_call" | custom-call | flops 40000000000 | bytes 1048576 | tf_op jit(solution)/shard_map/lookup/pallas_call | solution.py:257
  35.9 10.4 %all-to-all-start.1 = ((f32[64,16,128]{2,1,0:T(8,128)}), f32[64,16,128]{2,1,0:T(8,128)S(1)}, u32[]{:S(2)}, u32[]{:S(2)}) async-start(f32[64,16,128]{2,1,0:T(8,128)} %bitcast.10), calls=%async_computation.1 | async-start | bytes 1048576 | tf_op jit(solution)/shard_map/all_to_all | solution.py:274
  46.3 0.0 collective-permute-done.1.in_ref
  46.3 2.5 %collective-permute-start.2 = (bf16[2,960,256]{2,1,0:T(8,128)(2,1)S(1)}, bf16[2,960,256]{2,1,0:T(8,128)(2,1)S(1)}, u32[]{:S(2)}, u32[]{:S(2)}) collective-permute-start(bf16[2,960,256]{2,1,0:T(8,128)(2,1)S(1)} %held.5.side_ref), channel_id=1, source_target_pairs={{0,1},{1,2},{2,3},{3,0},{4,7},{5,4},{6,5},{7,6},{8,9},{9,10},{10,1... | collective-permute-start | bytes 2949128 | tf_op jit(solution)/shard_map/ppermute | solution.py:272
  48.8 2.2 %collective-permute-start.3 = (bf16[2,960,256]{2,1,0:T(8,128)(2,1)S(1)}, bf16[2,960,256]{2,1,0:T(8,128)(2,1)}, u32[]{:S(2)}, u32[]{:S(2)}) collective-permute-start(bf16[2,960,256]{2,1,0:T(8,128)(2,1)S(1)} %held.5.side_ref), channel_id=1, source_target_pairs={{0,4},{4,0},{1,5},{5,1},{2,6},{6,2},{3,7},{7,3},{8,12},{12,8},{9,1... | collective-permute-start | bytes 2949128 | tf_op jit(solution)/shard_map/ppermute | solution.py:193
  51.0 13.6 %all-to-all-done.1.in_ref = f32[64,16,128]{2,1,0:T(8,128)S(1)} async-done(((f32[64,16,128]{2,1,0:T(8,128)}), f32[64,16,128]{2,1,0:T(8,128)S(1)}, u32[]{:S(2)}, u32[]{:S(2)}) %all-to-all-start.1) | async-done | bytes 524320 | tf_op jit(solution)/shard_map/all_to_all | solution.py:274
  64.6 0.0 collective-permute-done.2.across_ref
  64.6 0.0 collective-permute-done.3.mirror_ref
  64.6 3.3 %top.1 = f32[1,16]{1,0:T(1,128)} custom-call(s32[4]{0:T(128)S(1)} %pad_add_fusion.meta_ref, f32[64,16,128]{2,1,0:T(8,128)S(1)} %held.4.bags_ref, f32[16,128]{1,0:T(8,128)S(1)} %get-tuple-element.19.bottom_ref, bf16[4,1,64]{2,1,0:T(2,128)(2,1)S(1)} %reshape.14.last_ref, bf16[2,960,256]{2,1,0:T(8,128)(2,1)S(1)} %get-tuple-element.20.own_ref, ...), custom_call_target="tpu_custom_call" | custom-call | flops 5000000000 | bytes 1048576 | tf_op jit(solution)/shard_map/top/pallas_call | solution.py:278
  (21 shorter events, 0.0 us)
Async XLA Ops:
  0.0 19.0 %copy-start = (bf16[1024,256]{1,0:T(8,128)(2,1)S(1)}, bf16[1024,256]{1,0:T(8,128)(2,1)}, u32[]{:S(2)}) copy-start(bf16[1024,256]{1,0:T(8,128)(2,1)} %w2_ref.1) | copy-start | bytes 1572868
  0.0 19.0 %copy-start.1 = (bf16[2048,128]{1,0:T(8,128)(2,1)S(1)}, bf16[2048,128]{1,0:T(8,128)(2,1)}, u32[]{:S(2)}) copy-start(bf16[2048,128]{1,0:T(8,128)(2,1)} %table_ref) | copy-start | bytes 1572868
  0.0 19.0 %copy-start.2 = (bf16[1024,128]{1,0:T(8,128)(2,1)S(1)}, bf16[1024,128]{1,0:T(8,128)(2,1)}, u32[]{:S(2)}) copy-start(bf16[1024,128]{1,0:T(8,128)(2,1)} %w3_ref.1) | copy-start | bytes 786436
  0.0 19.1 %copy-start.3 = (bf16[512,256]{1,0:T(8,128)(2,1)S(1)}, bf16[512,256]{1,0:T(8,128)(2,1)}, u32[]{:S(2)}) copy-start(bf16[512,256]{1,0:T(8,128)(2,1)} %b2_ref.1) | copy-start | bytes 786436
  0.0 19.1 %copy-start.4 = (bf16[164,256]{1,0:T(8,128)(2,1)S(1)}, bf16[164,256]{1,0:T(8,128)(2,1)}, u32[]{:S(2)}) copy-start(bf16[164,256]{1,0:T(8,128)(2,1)} %w1_ref.1) | copy-start | bytes 251908
  0.0 19.1 %copy-start.6 = (bf16[256,128]{1,0:T(8,128)(2,1)S(1)}, bf16[256,128]{1,0:T(8,128)(2,1)}, u32[]{:S(2)}) copy-start(bf16[256,128]{1,0:T(8,128)(2,1)} %b3_ref.1) | copy-start | bytes 196612
  0.0 19.1 %copy-start.7 = (bf16[13,512]{1,0:T(8,128)(2,1)S(1)}, bf16[13,512]{1,0:T(8,128)(2,1)}, u32[]{:S(2)}) copy-start(bf16[13,512]{1,0:T(8,128)(2,1)} %b1_ref.1) | copy-start | bytes 39940
  1.7 17.4 %copy-start.5 = (bf16[512,64]{0,1:T(8,128)(2,1)S(1)}, bf16[512,64]{0,1:T(8,128)(2,1)}, u32[]{:S(2)}) copy-start(bf16[512,64]{0,1:T(8,128)(2,1)} %param.22) | copy-start | bytes 196612
  1.7 17.4 %copy-start.8 = (bf16[16,13]{1,0:T(8,128)(2,1)S(1)}, bf16[16,13]{1,0:T(8,128)(2,1)}, u32[]{:S(2)}) copy-start(bf16[16,13]{1,0:T(8,128)(2,1)} %dense_ref.1) | copy-start | bytes 1252
  1.8 28.1 %all-to-all-start = ((s32[64,1,128]{2,1,0:T(1,128)}), s32[64,1,128]{2,1,0:T(1,128)S(1)}, u32[]{:S(2)}, u32[]{:S(2)}) async-start(s32[64,1,128]{2,1,0:T(1,128)} %bitcast.15), calls=%async_computation | async-start | bytes 65536 | tf_op jit(solution)/shard_map/all_to_all | solution.py:235
  19.6 0.8 %copy-start.9 = (bf16[2048,128]{1,0:T(8,128)(2,1)}, bf16[2048,128]{1,0:T(8,128)(2,1)S(1)}, u32[]{:S(2)}) copy-start(bf16[2048,128]{1,0:T(8,128)(2,1)S(1)} %get-tuple-element.16.own_ref) | copy-start | bytes 1572868
  20.4 7.4 %copy-start.11 = (bf16[256]{0:T(256)(128)(2,1)S(1)}, bf16[256]{0:T(256)(128)(2,1)}, u32[]{:S(2)}) copy-start(bf16[256]{0:T(256)(128)(2,1)} %param.23) | copy-start | bytes 1540
  20.4 9.5 %collective-permute-start = (bf16[2048,128]{1,0:T(8,128)(2,1)S(1)}, bf16[2048,128]{1,0:T(8,128)(2,1)S(1)}, u32[]{:S(2)}, u32[]{:S(2)}) collective-permute-start(bf16[2048,128]{1,0:T(8,128)(2,1)S(1)} %copy-done.1), channel_id=1, source_target_pairs={{0,4},{4,0},{1,5},{5,1},{2,6},{6,2},{3,7},{7,3},{8,12},{12,8},{9,1... | collective-permute-start | bytes 1572872 | tf_op jit(solution)/shard_map/ppermute | solution.py:193
  23.4 23.0 %collective-permute-start.1 = (bf16[2,960,256]{2,1,0:T(8,128)(2,1)S(1)}, bf16[2,960,256]{2,1,0:T(8,128)(2,1)S(1)}, u32[]{:S(2)}, u32[]{:S(2)}) collective-permute-start(bf16[2,960,256]{2,1,0:T(8,128)(2,1)S(1)} %get-tuple-element.20.own_ref), channel_id=1, source_target_pairs={{0,1},{1,2},{2,3},{3,0},{4,7},{5,4},{6,5},{7,6},{8,9},{9,10},{10,1... | collective-permute-start | bytes 2949128 | tf_op jit(solution)/shard_map/ppermute | solution.py:256
  29.9 1.0 %copy-start.10 = (bf16[2048,128]{1,0:T(8,128)(2,1)S(1)}, bf16[2048,128]{1,0:T(8,128)(2,1)}, u32[]{:S(2)}) copy-start(bf16[2048,128]{1,0:T(8,128)(2,1)} %copy-done.9) | copy-start | bytes 1572868
  35.9 28.7 %all-to-all-start.1 = ((f32[64,16,128]{2,1,0:T(8,128)}), f32[64,16,128]{2,1,0:T(8,128)S(1)}, u32[]{:S(2)}, u32[]{:S(2)}) async-start(f32[64,16,128]{2,1,0:T(8,128)} %bitcast.10), calls=%async_computation.1 | async-start | bytes 1048576 | tf_op jit(solution)/shard_map/all_to_all | solution.py:274
  46.3 18.3 %collective-permute-start.2 = (bf16[2,960,256]{2,1,0:T(8,128)(2,1)S(1)}, bf16[2,960,256]{2,1,0:T(8,128)(2,1)S(1)}, u32[]{:S(2)}, u32[]{:S(2)}) collective-permute-start(bf16[2,960,256]{2,1,0:T(8,128)(2,1)S(1)} %held.5.side_ref), channel_id=1, source_target_pairs={{0,1},{1,2},{2,3},{3,0},{4,7},{5,4},{6,5},{7,6},{8,9},{9,10},{10,1... | collective-permute-start | bytes 2949128 | tf_op jit(solution)/shard_map/ppermute | solution.py:272
  48.8 15.8 %collective-permute-start.3 = (bf16[2,960,256]{2,1,0:T(8,128)(2,1)S(1)}, bf16[2,960,256]{2,1,0:T(8,128)(2,1)}, u32[]{:S(2)}, u32[]{:S(2)}) collective-permute-start(bf16[2,960,256]{2,1,0:T(8,128)(2,1)S(1)} %held.5.side_ref), channel_id=1, source_target_pairs={{0,4},{4,0},{1,5},{5,1},{2,6},{6,2},{3,7},{7,3},{8,12},{12,8},{9,1... | collective-permute-start | bytes 2949128 | tf_op jit(solution)/shard_map/ppermute | solution.py:193
